TPU v7x, 256 devices: a whole 4x4x8 slice. The times are simulated.
256 devices in a mesh: ctx: 128 (over y, x, z_lo, core), chan: 2 (over z_hi).
Axes of the slice: x: 4, y: 4, z: 8 (z_hi: 2, z_lo: 4; z = z_hi * 4 + z_lo), core: 2. Of those that a mesh axis runs over, the one named last changes fastest.
Arguments:
- streams: bfloat16 [32768, 3, 2048], P('ctx', None, 'chan'), may hold values from -6 to 6
- short_filter: float32 [3, 3, 2048], P(None, None, 'chan'), may hold values from -3 to 3
- residue: float32 [2048, 16], P('chan'), may hold values from -1.5 to 1.5
- decay_rate: float32 [2048, 16], P('chan'), may hold values from 1.5258789e-05 to 0.03, as said below
- skip_gain: float32 [2048], P('chan'), may hold values from 0.5 to 1.5
Outputs:
- hyena_out: bfloat16 [32768, 2048], P(('ctx', 'chan'))
Inputs may be any that keep to these rules, and one draw needn't show every extreme that they name: `decay_rate`: each rate is drawn for its channel and mode independently; nothing beyond these bounds is promised.
All inputs are finite; a program needn't handle non-finite values.
Results may differ from a plain program's by a relative error of at most 0.0095.
Values may be sent and summed in bfloat16 or wider, within the bound.
No kernel may reach another device: no remote copies, remote signals or barrier semaphores. Data moves between devices by JAX's collectives and lax.ppermute only.
A program may use at most 128 MiB of HBM per device.

v0:
```python
import functools

import jax
import jax.numpy as jnp
from jax import lax
from jax.experimental import pallas as pl
from jax.experimental.pallas import tpu as pltpu
from jax.sharding import PartitionSpec as P

LANES = 128
SUB = 8
F32 = jnp.float32
BF16 = jnp.bfloat16


def sub_index():
    return lax.broadcasted_iota(jnp.int32, (SUB, LANES), 0)


def rows_of(ref, cols):
    return [
        jnp.broadcast_to(ref[m : m + 1, cols], (SUB, LANES)) for m in range(ref.shape[0])
    ]


def features_kernel(
    chan_ref, x_ref, halo_ref, taps_ref, rate_ref,
    q_own, g_own, q_send, g_send, state_ref, half_ref, wide, gated,
):
    side = chan_ref[0]
    _, toks, width = x_ref.shape
    half = toks // 2
    tap_count = taps_ref.shape[0]
    rim = tap_count - 1
    step = 32
    for s in range(3):
        wide[s, SUB - rim : SUB, :] = halo_ref[s].astype(F32)
        for r in range(0, toks, step):
            wide[s, SUB + r : SUB + r + step, :] = x_ref[s, r : r + step, :].astype(F32)
    for c in range(0, width, LANES):
        cols = slice(c, c + LANES)
        taps = [
            [
                jnp.broadcast_to(taps_ref[j, s : s + 1, cols], (step, LANES))
                for j in range(tap_count)
            ]
            for s in range(3)
        ]
        for r in range(0, toks, step):
            feats = []
            for s in range(3):
                total = taps[s][0] * wide[s, SUB + r : SUB + r + step, cols]
                for j in range(1, tap_count):
                    total = total + taps[s][j] * wide[s, SUB + r - j : SUB + r - j + step, cols]
                feats.append(total.astype(BF16))
            gate = (feats[1].astype(F32) * feats[2].astype(F32)).astype(BF16)
            gated[r : r + step, :] = gate.astype(F32)
            at = r % half

            @pl.when(side == r // half)
            def _():
                q_own[at : at + step, cols] = feats[0]
                g_own[at : at + step, cols] = gate

            @pl.when(side != r // half)
            def _():
                q_send[at : at + step, cols] = feats[0]
                g_send[at : at + step, cols] = gate

        run = toks // SUB
        rates = rows_of(rate_ref, cols)
        keep = [jnp.exp(-rate) for rate in rates]

        def advance(j, states):
            now = gated[pl.ds(j, SUB, stride=run), :]
            return tuple(k * state + now for k, state in zip(keep, states))

        ends = lax.fori_loop(
            0, run, advance, tuple(jnp.zeros((SUB, LANES), F32) for _ in keep), unroll=4
        )
        index = sub_index()
        left = (SUB - 1 - index).astype(F32) * run
        in_half = index < SUB // 2
        left_half = jnp.maximum(SUB // 2 - 1 - index, 0).astype(F32) * run
        for m, (rate, end) in enumerate(zip(rates, ends)):
            state_ref[m : m + 1, cols] = jnp.sum(
                jnp.exp(-rate * left) * end, axis=0, keepdims=True
            )
            half_ref[m : m + 1, cols] = jnp.sum(
                jnp.where(in_half, jnp.exp(-rate * left_half) * end, 0.0), axis=0, keepdims=True
            )


def local_kernel(g_ref, res_ref, rate_ref, skip_ref, out_ref, gated):
    toks, width = g_ref.shape
    run = toks // SUB
    step = 32
    index = sub_index()
    for c in range(0, width, LANES):
        cols = slice(c, c + LANES)
        for r in range(0, toks, step):
            gated[r : r + step, :] = g_ref[r : r + step, cols].astype(F32)
        rates = rows_of(rate_ref, cols)
        keep = [jnp.exp(-rate) for rate in rates]

        def advance(j, states):
            now = gated[pl.ds(j, SUB, stride=run), :]
            return tuple(k * state + now for k, state in zip(keep, states))

        ends = lax.fori_loop(
            0, run, advance, tuple(jnp.zeros((SUB, LANES), F32) for _ in keep), unroll=4
        )
        begins = []
        for rate, total in zip(rates, ends):
            for shift in (1, 2, 4):
                total = total + jnp.where(
                    index >= shift,
                    jnp.exp(-rate * (shift * run)) * pltpu.roll(total, shift, 0),
                    0.0,
                )
            begins.append(jnp.where(index >= 1, pltpu.roll(total, 1, 0), 0.0))
        gains = [
            res * jnp.sqrt(2.0 * rate) for res, rate in zip(rows_of(res_ref, cols), rates)
        ]
        skip = jnp.broadcast_to(skip_ref[0:1, cols], (SUB, LANES))

        def emit(j, states):
            now = gated[pl.ds(j, SUB, stride=run), :]
            states = tuple(k * state + now for k, state in zip(keep, states))
            terms = [skip * now] + [gain * state for gain, state in zip(gains, states)]
            while len(terms) > 1:
                terms = [
                    terms[i] + terms[i + 1] if i + 1 < len(terms) else terms[i]
                    for i in range(0, len(terms), 2)
                ]
            out_ref[pl.ds(j + c * toks // LANES, SUB, stride=run), :] = terms[0]
            return states

        lax.fori_loop(0, run, emit, tuple(begins), unroll=4)


def finish_kernel(
    chan_ref, q_own, p_own, x_own, res_own, rate_own,
    q_far, p_far, x_far, res_far, rate_far, out_ref, carry,
):
    side = chan_ref[0]
    toks, width = q_own.shape
    run = toks // SUB
    index = sub_index()
    passed = (index * run + 1).astype(F32)
    step = 32
    for part, (q_ref, p_ref, x_ref, res_ref, rate_ref) in enumerate(
        ((q_own, p_own, x_own, res_own, rate_own), (q_far, p_far, x_far, res_far, rate_far))
    ):
        base = width * (side if part == 0 else 1 - side)
        for c in range(0, width, LANES):
            cols = slice(c, c + LANES)
            rates = rows_of(rate_ref, cols)
            keep = [jnp.exp(-rate) for rate in rates]
            begins = tuple(
                res * jnp.sqrt(2.0 * rate) * jnp.exp(-rate * passed) * x
                for res, rate, x in zip(rows_of(res_ref, cols), rates, rows_of(x_ref, cols))
            )

            def fade(j, states):
                terms = list(states)
                while len(terms) > 1:
                    terms = [terms[i] + terms[i + 1] for i in range(0, len(terms), 2)]
                carry[pl.ds(j, SUB, stride=run), :] = terms[0]
                return tuple(k * state for k, state in zip(keep, states))

            lax.fori_loop(0, run, fade, begins, unroll=4)
            where = pl.ds(pl.multiple_of(base + c, LANES), LANES)
            for r in range(0, toks, step):
                rows = slice(r, r + step)
                out_ref[rows, where] = (
                    q_ref[rows, cols].astype(F32) * (p_ref[c * toks // LANES + r : c * toks // LANES + r + step, :] + carry[rows, :])
                ).astype(BF16)


def stage(state_total, prefix, rate_span, index, stride, count, behind):
    ctx_count = lax.axis_size("ctx")
    place = index // stride % count
    sent = state_total.astype(BF16)
    arrived = []
    for k in range(1, count):
        route = []
        for i in range(ctx_count):
            j = i // stride % count
            route.append((i, i + ((j + k) % count - j) * stride))
        arrived.append(lax.ppermute(sent, "ctx", route))
    total = jnp.exp(-rate_span * ((count - 1 - place) * stride).astype(F32)) * state_total
    for k, got in enumerate(arrived, 1):
        got = got.astype(F32)
        origin = (place - k) % count
        total = total + jnp.exp(-rate_span * ((count - 1 - origin) * stride).astype(F32)) * got
        between = ((k - 1) * stride + behind).astype(F32)
        prefix = prefix + jnp.where(place >= k, jnp.exp(-rate_span * between), 0.0) * got
    return total, prefix


def shards(streams, short_filter, residue, decay_rate, skip_gain):
    ctx_count = lax.axis_size("ctx")
    index = lax.axis_index("ctx")
    side = lax.axis_index("chan")
    toks, _, width = streams.shape
    half = toks // 2
    modes = residue.shape[1]
    rim = short_filter.shape[0] - 1
    swap = [(0, 1), (1, 0)]

    x = jnp.transpose(streams, (1, 0, 2))
    rates = decay_rate.T
    weights = residue.T
    skip = skip_gain[None, :]
    halo = lax.ppermute(
        x[:, toks - rim :, :], "ctx", [(i, i + 1) for i in range(ctx_count - 1)]
    )
    params = lax.ppermute(jnp.concatenate([rates, weights, skip], axis=0), "chan", swap)
    rates_far, weights_far, skip_far = (
        params[:modes],
        params[modes : 2 * modes],
        params[2 * modes :],
    )
    chan_id = side.astype(jnp.int32).reshape(1)

    tile = 256 if width % 256 == 0 else LANES
    vmem = pltpu.CompilerParams(vmem_limit_bytes=48 * 1024 * 1024)
    rows = lambda n: pl.BlockSpec((n, tile), lambda i, *_: (0, i))
    q_own, g_own, q_send, g_send, state, state_half = pl.pallas_call(
        features_kernel,
        grid_spec=pltpu.PrefetchScalarGridSpec(
            num_scalar_prefetch=1,
            grid=(width // tile,),
            in_specs=[
                pl.BlockSpec((3, toks, tile), lambda i, *_: (0, 0, i)),
                pl.BlockSpec((3, rim, tile), lambda i, *_: (0, 0, i)),
                pl.BlockSpec((rim + 1, 3, tile), lambda i, *_: (0, 0, i)),
                rows(modes),
            ],
            out_specs=[rows(half)] * 4 + [rows(modes)] * 2,
            scratch_shapes=[
                pltpu.VMEM((3, toks + SUB, tile), F32),
                pltpu.VMEM((toks, LANES), F32),
            ],
        ),
        out_shape=[jax.ShapeDtypeStruct((half, width), BF16)] * 4
        + [jax.ShapeDtypeStruct((modes, width), F32)] * 2,
        compiler_params=vmem,
        name="features",
    )(chan_id, x, halo, short_filter, rates)

    g_far = lax.ppermute(g_send, "chan", swap)
    q_far = lax.ppermute(q_send, "chan", swap)

    def local(g, res, rate, skip_row, name):
        return pl.pallas_call(
            local_kernel,
            grid=(width // tile,),
            in_specs=[
                pl.BlockSpec((half, tile), lambda i: (0, i)),
                pl.BlockSpec((modes, tile), lambda i: (0, i)),
                pl.BlockSpec((modes, tile), lambda i: (0, i)),
                pl.BlockSpec((1, tile), lambda i: (0, i)),
            ],
            out_specs=pl.BlockSpec((half * tile // LANES, LANES), lambda i: (i, 0)),
            out_shape=jax.ShapeDtypeStruct((half * width // LANES, LANES), F32),
            scratch_shapes=[pltpu.VMEM((half, LANES), F32)],
            compiler_params=vmem,
            name=name,
        )(g, res, rate, skip_row)

    p_own = local(g_own, weights, rates, skip, "local_own")
    p_far = local(g_far, weights_far, rates_far, skip_far, "local_far")

    span = rates * float(toks)
    prefix = jnp.zeros_like(state)
    total = state
    stride = 1
    for count in scan_radices(ctx_count):
        total, prefix = stage(total, prefix, span, index, stride, count, index % stride)
        stride *= count

    later = jnp.exp(-rates * float(half)) * prefix + state_half
    mine = jnp.where(side == 0, prefix, later)
    theirs = jnp.where(side == 0, later, prefix)
    x_far = lax.ppermute(theirs.astype(BF16), "chan", swap).astype(F32)

    full = lambda a: pl.BlockSpec(a.shape, lambda *_: (0,) * a.ndim)
    operands = (
        q_own, p_own, mine, weights, rates, q_far, p_far, x_far, weights_far, rates_far,
    )
    return pl.pallas_call(
        finish_kernel,
        grid_spec=pltpu.PrefetchScalarGridSpec(
            num_scalar_prefetch=1,
            grid=(1,),
            in_specs=[full(a) for a in operands],
            out_specs=pl.BlockSpec((half, 2 * width), lambda *_: (0, 0)),
            scratch_shapes=[pltpu.VMEM((half, LANES), F32)],
        ),
        out_shape=jax.ShapeDtypeStruct((half, 2 * width), BF16),
        compiler_params=vmem,
        name="finish",
    )(chan_id, *operands)


def scan_radices(count):
    radices = [2] if count % 2 == 0 else []
    left = count // 2 if radices else count
    while left % 4 == 0:
        radices.append(4)
        left //= 4
    if left > 1:
        radices.append(left)
    return radices


def solution(mesh):
    return jax.shard_map(
        shards,
        mesh=mesh,
        in_specs=(
            P("ctx", None, "chan"),
            P(None, None, "chan"),
            P("chan", None),
            P("chan", None),
            P("chan"),
        ),
        out_specs=P(("ctx", "chan"), None),
        check_vma=False,
    )
```

profile of v0, /device:TPU:12, one launch (start us, length us, event | category | flops | bytes accessed | tf_op | source)
XLA Modules:
  0.0 74.3 jit_solution(4114912487726840313)
XLA Ops:
  0.0 0.0 copy-start.5
  0.0 0.8 %slice.16 = bf16[3,2,1024]{2,1,0:T(2,128)(2,1)S(1)} slice(bf16[3,256,1024]{2,1,0:T(8,128)(2,1)} %bitcast.17), slice={[0:3], [254:256], [0:1024]} | slice | bytes 24576 | tf_op jit(solution)/shard_map/slice | solution.py:217
  0.8 1.9 %collective-permute-start = (bf16[3,2,1024]{2,1,0:T(2,128)(2,1)S(1)}, bf16[3,2,1024]{2,1,0:T(2,128)(2,1)S(1)}, u32[]{:S(2)}, u32[]{:S(2)}) collective-permute-start(bf16[3,2,1024]{2,1,0:T(2,128)(2,1)S(1)} %slice.16), channel_id=1, source_target_pairs={{0,2},{2,4},{4,6},{6,8},{8,10},{10,12},{12,14},{14,16},{16,18},{18... | collective-permute-start | bytes 36872 | tf_op jit(solution)/shard_map/ppermute | solution.py:216
  2.8 5.8 %collective-permute-done.halo_ref = bf16[3,2,1024]{2,1,0:T(2,128)(2,1)S(1)} collective-permute-done((bf16[3,2,1024]{2,1,0:T(2,128)(2,1)S(1)}, bf16[3,2,1024]{2,1,0:T(2,128)(2,1)S(1)}, u32[]{:S(2)}, u32[]{:S(2)}) %collective-permute-start) | collective-permute-done | bytes 12320 | tf_op jit(solution)/shard_map/ppermute | solution.py:216
  8.5 0.0 copy-start
  8.5 0.8 %copy-done = f32[1024,16]{0,1:T(8,128)S(1)} copy-done((f32[1024,16]{0,1:T(8,128)S(1)}, f32[1024,16]{0,1:T(8,128)}, u32[]{:S(2)}) %copy-start) | copy-done | bytes 65560
  9.4 0.0 copy-start.2
  9.4 1.4 %copy-done.2 = bf16[256,3,1024]{2,0,1:T(8,128)(2,1)S(1)} copy-done((bf16[256,3,1024]{2,0,1:T(8,128)(2,1)S(1)}, bf16[256,3,1024]{2,0,1:T(8,128)(2,1)}, u32[]{:S(2)}) %copy-start.2) | copy-done | bytes 1572888
  10.8 0.0 copy-start.4
  10.8 0.8 %copy-done.4 = f32[3,3,1024]{2,1,0:T(4,128)S(1)} copy-done((f32[3,3,1024]{2,1,0:T(4,128)S(1)}, f32[3,3,1024]{2,1,0:T(4,128)}, u32[]{:S(2)}) %copy-start.4) | copy-done | bytes 36888
  11.6 0.0 copy-start.1
  11.6 0.0 copy-start.3
  11.6 4.8 %features.1 = (bf16[128,1024]{1,0:T(8,128)(2,1)S(1)}, bf16[128,1024]{1,0:T(8,128)(2,1)S(1)}, bf16[128,1024]{1,0:T(8,128)(2,1)S(1)}, bf16[128,1024]{1,0:T(8,128)(...) custom-call(s32[1]{0:T(128)} %bitcast.chan_ref, bf16[3,256,1024]{2,1,0:T(8,128)(2,1)S(1)} %bitcast.18, ...), custom_call_target="tpu_custom_call" | custom-call | tf_op jit(solution)/shard_map/features/pallas_call | solution.py:230
  16.4 0.1 collective-permute-start.1
  16.5 1.2 %collective-permute-done.1 = bf16[16,1024]{1,0:T(8,128)(2,1)S(1)} collective-permute-done((bf16[16,1024]{1,0:T(8,128)(2,1)S(1)}, bf16[16,1024]{1,0:T(8,128)(2,1)S(1)}, u32[]{:S(2)}, u32[]{:S(2)}) %collective-permute-start.1) | collective-permute-done | bytes 32800 | tf_op jit(solution)/shard_map/ppermute | solution.py:191
  17.7 0.0 copy-done.1
  17.7 2.0 %collective-permute-start.4 = (bf16[16,1024]{1,0:T(8,128)(2,1)S(1)}, bf16[16,1024]{1,0:T(8,128)(2,1)S(1)}, u32[]{:S(2)}, u32[]{:S(2)}) collective-permute-start(bf16[16,1024]{1,0:T(8,128)(2,1)S(1)} %fusion.18), channel_id=1, source_target_pairs={{0,12},{2,14},{4,0},{6,2},{8,4},{10,6},{12,8},{14,10},{16,28},{18,... | collective-permute-start | bytes 98312 | tf_op jit(solution)/shard_map/ppermute | solution.py:191
  19.8 0.0 collective-permute-start.3
  19.8 0.7 collective-permute-start.2
  20.4 1.3 %collective-permute-done.4 = bf16[16,1024]{1,0:T(8,128)(2,1)S(1)} collective-permute-done((bf16[16,1024]{1,0:T(8,128)(2,1)S(1)}, bf16[16,1024]{1,0:T(8,128)(2,1)S(1)}, u32[]{:S(2)}, u32[]{:S(2)}) %collective-permute-start.4) | collective-permute-done | bytes 32800 | tf_op jit(solution)/shard_map/ppermute | solution.py:191
  21.7 3.1 %collective-permute-done.3 = bf16[16,1024]{1,0:T(8,128)(2,1)S(1)} collective-permute-done((bf16[16,1024]{1,0:T(8,128)(2,1)S(1)}, bf16[16,1024]{1,0:T(8,128)(2,1)S(1)}, u32[]{:S(2)}, u32[]{:S(2)}) %collective-permute-start.3) | collective-permute-done | bytes 32800 | tf_op jit(solution)/shard_map/ppermute | solution.py:191
  24.8 0.7 collective-permute-done.2
  25.5 0.1 fusion.20
  25.5 0.6 collective-permute-start.7
  26.2 2.7 %collective-permute-start.6 = (bf16[16,1024]{1,0:T(8,128)(2,1)S(1)}, bf16[16,1024]{1,0:T(8,128)(2,1)S(1)}, u32[]{:S(2)}, u32[]{:S(2)}) collective-permute-start(bf16[16,1024]{1,0:T(8,128)(2,1)S(1)} %get-tuple-element.19), channel_id=1, source_target_pairs={{0,32},{2,34},{4,36},{6,38},{8,40},{10,42},{12,44},{14,46},{16,48}... | collective-permute-start | bytes 98312 | tf_op jit(solution)/shard_map/ppermute | solution.py:191
  28.9 1.0 %collective-permute-start.5 = (bf16[16,1024]{1,0:T(8,128)(2,1)S(1)}, bf16[16,1024]{1,0:T(8,128)(2,1)S(1)}, u32[]{:S(2)}, u32[]{:S(2)}) collective-permute-start(bf16[16,1024]{1,0:T(8,128)(2,1)S(1)} %get-tuple-element.19), channel_id=1, source_target_pairs={{0,16},{2,18},{4,20},{6,22},{8,24},{10,26},{12,28},{14,30},{16,32}... | collective-permute-start | bytes 98312 | tf_op jit(solution)/shard_map/ppermute | solution.py:191
  29.9 0.0 copy-done.5
  29.9 0.0 copy-done.3
  29.9 7.3 %collective-permute-start.13 = (f32[33,1024]{1,0:T(8,128)S(1)}, f32[33,1024]{1,0:T(8,128)S(1)}, u32[]{:S(2)}, u32[]{:S(2)}) collective-permute-start(f32[33,1024]{1,0:T(8,128)S(1)} %pad_maximum_fusion), channel_id=1, source_target_pairs={{0,1},{1,0},{2,3},{3,2},{4,5},{5,4},{6,7},{7,6},{8,9},{9,8},{10,11... | collective-permute-start | bytes 405512 | tf_op jit(solution)/shard_map/ppermute | solution.py:219
  37.2 0.3 collective-permute-start.11
  37.4 3.1 %local_own.1.p_own = f32[1024,128]{1,0:T(8,128)S(1)} custom-call(bf16[128,1024]{1,0:T(8,128)(2,1)S(1)} %get-tuple-element.12.g_ref, f32[16,1024]{1,0:T(8,128)S(1)} %bitcast.20, f32[16,1024]{1,0:T(8,128)S(1)} %bitcast.15, f32[1,1024]{1,0:T(1,128)S(1)} %bitcast.23), custom_call_target="tpu_custom_call" | custom-call | tf_op jit(solution)/shard_map/local_own/pallas_call | solution.py:257
  40.6 0.0 collective-permute-done.7
  40.6 5.8 %collective-permute-start.12 = (bf16[128,1024]{1,0:T(8,128)(2,1)S(1)}, bf16[128,1024]{1,0:T(8,128)(2,1)S(1)}, u32[]{:S(2)}, u32[]{:S(2)}) collective-permute-start(bf16[128,1024]{1,0:T(8,128)(2,1)S(1)} %get-tuple-element.16), channel_id=1, source_target_pairs={{0,1},{1,0},{2,3},{3,2},{4,5},{5,4},{6,7},{7,6},{8,9},{9,8},{10,11... | collective-permute-start | bytes 786440 | tf_op jit(solution)/shard_map/ppermute | solution.py:253
  46.3 0.0 collective-permute-done.6
  46.3 0.0 collective-permute-done.5
  46.3 0.1 fusion.16
  46.4 0.1 collective-permute-start.10
  46.5 3.0 %collective-permute-start.9 = (bf16[16,1024]{1,0:T(8,128)(2,1)S(1)}, bf16[16,1024]{1,0:T(8,128)(2,1)S(1)}, u32[]{:S(2)}, u32[]{:S(2)}) collective-permute-start(bf16[16,1024]{1,0:T(8,128)(2,1)S(1)} %fusion.16), channel_id=1, source_target_pairs={{0,128},{2,130},{4,132},{6,134},{8,136},{10,138},{12,140},{14,142}... | collective-permute-start | bytes 98312 | tf_op jit(solution)/shard_map/ppermute | solution.py:191
  49.5 0.0 collective-permute-done.13
  49.5 1.9 %collective-permute-start.8 = (bf16[16,1024]{1,0:T(8,128)(2,1)S(1)}, bf16[16,1024]{1,0:T(8,128)(2,1)S(1)}, u32[]{:S(2)}, u32[]{:S(2)}) collective-permute-start(bf16[16,1024]{1,0:T(8,128)(2,1)S(1)} %fusion.16), channel_id=1, source_target_pairs={{0,64},{2,66},{4,68},{6,70},{8,72},{10,74},{12,76},{14,78},{16,80}... | collective-permute-start | bytes 98312 | tf_op jit(solution)/shard_map/ppermute | solution.py:191
  51.4 0.0 collective-permute-done.10
  51.4 0.6 collective-permute-done.9
  52.0 1.4 %collective-permute-done.8 = bf16[16,1024]{1,0:T(8,128)(2,1)S(1)} collective-permute-done((bf16[16,1024]{1,0:T(8,128)(2,1)S(1)}, bf16[16,1024]{1,0:T(8,128)(2,1)S(1)}, u32[]{:S(2)}, u32[]{:S(2)}) %collective-permute-start.8) | collective-permute-done | bytes 32800 | tf_op jit(solution)/shard_map/ppermute | solution.py:191
  53.4 0.2 select_convert_fusion
  53.6 3.4 %collective-permute-start.14 = (bf16[16,1024]{1,0:T(8,128)(2,1)S(1)}, bf16[16,1024]{1,0:T(8,128)(2,1)S(1)}, u32[]{:S(2)}, u32[]{:S(2)}) collective-permute-start(bf16[16,1024]{1,0:T(8,128)(2,1)S(1)} %get-tuple-element.17), channel_id=1, source_target_pairs={{0,1},{1,0},{2,3},{3,2},{4,5},{5,4},{6,7},{7,6},{8,9},{9,8},{10,11... | collective-permute-start | bytes 98312 | tf_op jit(solution)/shard_map/ppermute | solution.py:287
  57.0 11.0 %collective-permute-done.14 = bf16[16,1024]{1,0:T(8,128)(2,1)S(1)} collective-permute-done((bf16[16,1024]{1,0:T(8,128)(2,1)S(1)}, bf16[16,1024]{1,0:T(8,128)(2,1)S(1)}, u32[]{:S(2)}, u32[]{:S(2)}) %collective-permute-start.14) | collective-permute-done | bytes 32800 | tf_op jit(solution)/shard_map/ppermute | solution.py:287
  68.0 0.0 collective-permute-done.12.g_ref
  68.0 3.1 %local_far.1.p_far = f32[1024,128]{1,0:T(8,128)S(1)} custom-call(bf16[128,1024]{1,0:T(8,128)(2,1)S(1)} %collective-permute-done.12.g_ref, f32[16,1024]{1,0:T(8,128)S(1)} %get-tuple-element.22.res_ref.res_far, f32[16,1024]{1,0:T(8,128)S(1)} %get-tuple-element.21.rate_ref.rate_far, f32[1,1024]{1,0:T(1,128)S(1)} %slice.19.skip_ref), custom_call_target="tpu_custom_call" | custom-call | tf_op jit(solution)/shard_map/local_far/pallas_call | solution.py:257
  71.2 0.0 collective-permute-done.11.q_far
  71.2 3.1 %finish.1 = bf16[128,2048]{1,0:T(8,128)(2,1)} custom-call(s32[1]{0:T(128)} %bitcast.chan_ref, bf16[128,1024]{1,0:T(8,128)(2,1)S(1)} %get-tuple-element.11.q_own, f32[1024,128]{1,0:T(8,128)S(1)} %local_own.1.p_own, f32[16,1024]{1,0:T(8,128)S(1)} %fusion.17.x_own, f32[16,1024]{1,0:T(8,128)S(1)} %bitcast.21, f32[16,1024]{1,0:T(8,128)S(1)} %bitcast.16, ...), custom_call_target="tpu_custom_call" | custom-call | tf_op jit(solution)/shard_map/finish/pallas_call | solution.py:293
  (7 shorter events, 0.1 us)
Async XLA Ops:
  0.0 29.9 %copy-start.5 = (f32[1024]{0:T(1024)S(1)}, f32[1024]{0:T(1024)}, u32[]{:S(2)}) copy-start(f32[1024]{0:T(1024)} %param.9) | copy-start | bytes 12292
  0.8 7.7 %collective-permute-start = (bf16[3,2,1024]{2,1,0:T(2,128)(2,1)S(1)}, bf16[3,2,1024]{2,1,0:T(2,128)(2,1)S(1)}, u32[]{:S(2)}, u32[]{:S(2)}) collective-permute-start(bf16[3,2,1024]{2,1,0:T(2,128)(2,1)S(1)} %slice.16), channel_id=1, source_target_pairs={{0,2},{2,4},{4,6},{6,8},{8,10},{10,12},{12,14},{14,16},{16,18},{18... | collective-permute-start | bytes 36872 | tf_op jit(solution)/shard_map/ppermute | solution.py:216
  8.5 0.8 %copy-start = (f32[1024,16]{0,1:T(8,128)S(1)}, f32[1024,16]{0,1:T(8,128)}, u32[]{:S(2)}) copy-start(f32[1024,16]{0,1:T(8,128)} %param.8) | copy-start | bytes 196612
  9.4 1.4 %copy-start.2 = (bf16[256,3,1024]{2,0,1:T(8,128)(2,1)S(1)}, bf16[256,3,1024]{2,0,1:T(8,128)(2,1)}, u32[]{:S(2)}) copy-start(bf16[256,3,1024]{2,0,1:T(8,128)(2,1)} %param.5) | copy-start | bytes 4718596
  10.8 0.8 %copy-start.4 = (f32[3,3,1024]{2,1,0:T(4,128)S(1)}, f32[3,3,1024]{2,1,0:T(4,128)}, u32[]{:S(2)}) copy-start(f32[3,3,1024]{2,1,0:T(4,128)} %taps_ref.1) | copy-start | bytes 110596
  11.6 6.1 %copy-start.1 = (f32[1024,16]{0,1:T(8,128)S(1)}, f32[1024,16]{0,1:T(8,128)}, u32[]{:S(2)}) copy-start(f32[1024,16]{0,1:T(8,128)} %param.8) | copy-start | bytes 196612
  11.6 18.3 %copy-start.3 = (f32[1024,16]{0,1:T(8,128)S(1)}, f32[1024,16]{0,1:T(8,128)}, u32[]{:S(2)}) copy-start(f32[1024,16]{0,1:T(8,128)} %param.7) | copy-start | bytes 196612
  16.4 1.3 %collective-permute-start.1 = (bf16[16,1024]{1,0:T(8,128)(2,1)S(1)}, bf16[16,1024]{1,0:T(8,128)(2,1)S(1)}, u32[]{:S(2)}, u32[]{:S(2)}) collective-permute-start(bf16[16,1024]{1,0:T(8,128)(2,1)S(1)} %convert_element_type.106), channel_id=1, source_target_pairs={{0,2},{2,0},{4,6},{6,4},{8,10},{10,8},{12,14},{14,12},{16,18},{18,... | collective-permute-start | bytes 98312 | tf_op jit(solution)/shard_map/ppermute | solution.py:191
  17.7 4.0 %collective-permute-start.4 = (bf16[16,1024]{1,0:T(8,128)(2,1)S(1)}, bf16[16,1024]{1,0:T(8,128)(2,1)S(1)}, u32[]{:S(2)}, u32[]{:S(2)}) collective-permute-start(bf16[16,1024]{1,0:T(8,128)(2,1)S(1)} %fusion.18), channel_id=1, source_target_pairs={{0,12},{2,14},{4,0},{6,2},{8,4},{10,6},{12,8},{14,10},{16,28},{18,... | collective-permute-start | bytes 98312 | tf_op jit(solution)/shard_map/ppermute | solution.py:191
  19.8 5.1 %collective-permute-start.3 = (bf16[16,1024]{1,0:T(8,128)(2,1)S(1)}, bf16[16,1024]{1,0:T(8,128)(2,1)S(1)}, u32[]{:S(2)}, u32[]{:S(2)}) collective-permute-start(bf16[16,1024]{1,0:T(8,128)(2,1)S(1)} %fusion.18), channel_id=1, source_target_pairs={{0,8},{2,10},{4,12},{6,14},{8,0},{10,2},{12,4},{14,6},{16,24},{18,... | collective-permute-start | bytes 98312 | tf_op jit(solution)/shard_map/ppermute | solution.py:191
  19.8 5.7 %collective-permute-start.2 = (bf16[16,1024]{1,0:T(8,128)(2,1)S(1)}, bf16[16,1024]{1,0:T(8,128)(2,1)S(1)}, u32[]{:S(2)}, u32[]{:S(2)}) collective-permute-start(bf16[16,1024]{1,0:T(8,128)(2,1)S(1)} %fusion.18), channel_id=1, source_target_pairs={{0,4},{2,6},{4,8},{6,10},{8,12},{10,14},{12,0},{14,2},{16,20},{18,... | collective-permute-start | bytes 98312 | tf_op jit(solution)/shard_map/ppermute | solution.py:191
  25.5 15.0 %collective-permute-start.7 = (bf16[16,1024]{1,0:T(8,128)(2,1)S(1)}, bf16[16,1024]{1,0:T(8,128)(2,1)S(1)}, u32[]{:S(2)}, u32[]{:S(2)}) collective-permute-start(bf16[16,1024]{1,0:T(8,128)(2,1)S(1)} %get-tuple-element.19), channel_id=1, source_target_pairs={{0,48},{2,50},{4,52},{6,54},{8,56},{10,58},{12,60},{14,62},{16,0},... | collective-permute-start | bytes 98312 | tf_op jit(solution)/shard_map/ppermute | solution.py:191
  26.2 20.2 %collective-permute-start.6 = (bf16[16,1024]{1,0:T(8,128)(2,1)S(1)}, bf16[16,1024]{1,0:T(8,128)(2,1)S(1)}, u32[]{:S(2)}, u32[]{:S(2)}) collective-permute-start(bf16[16,1024]{1,0:T(8,128)(2,1)S(1)} %get-tuple-element.19), channel_id=1, source_target_pairs={{0,32},{2,34},{4,36},{6,38},{8,40},{10,42},{12,44},{14,46},{16,48}... | collective-permute-start | bytes 98312 | tf_op jit(solution)/shard_map/ppermute | solution.py:191
  28.9 17.4 %collective-permute-start.5 = (bf16[16,1024]{1,0:T(8,128)(2,1)S(1)}, bf16[16,1024]{1,0:T(8,128)(2,1)S(1)}, u32[]{:S(2)}, u32[]{:S(2)}) collective-permute-start(bf16[16,1024]{1,0:T(8,128)(2,1)S(1)} %get-tuple-element.19), channel_id=1, source_target_pairs={{0,16},{2,18},{4,20},{6,22},{8,24},{10,26},{12,28},{14,30},{16,32}... | collective-permute-start | bytes 98312 | tf_op jit(solution)/shard_map/ppermute | solution.py:191
  29.9 19.6 %collective-permute-start.13 = (f32[33,1024]{1,0:T(8,128)S(1)}, f32[33,1024]{1,0:T(8,128)S(1)}, u32[]{:S(2)}, u32[]{:S(2)}) collective-permute-start(f32[33,1024]{1,0:T(8,128)S(1)} %pad_maximum_fusion), channel_id=1, source_target_pairs={{0,1},{1,0},{2,3},{3,2},{4,5},{5,4},{6,7},{7,6},{8,9},{9,8},{10,11... | collective-permute-start | bytes 405512 | tf_op jit(solution)/shard_map/ppermute | solution.py:219
  37.2 34.0 %collective-permute-start.11 = (bf16[128,1024]{1,0:T(8,128)(2,1)S(1)}, bf16[128,1024]{1,0:T(8,128)(2,1)S(1)}, u32[]{:S(2)}, u32[]{:S(2)}) collective-permute-start(bf16[128,1024]{1,0:T(8,128)(2,1)S(1)} %get-tuple-element.15), channel_id=1, source_target_pairs={{0,1},{1,0},{2,3},{3,2},{4,5},{5,4},{6,7},{7,6},{8,9},{9,8},{10,11... | collective-permute-start | bytes 786440 | tf_op jit(solution)/shard_map/ppermute | solution.py:254
  40.6 27.5 %collective-permute-start.12 = (bf16[128,1024]{1,0:T(8,128)(2,1)S(1)}, bf16[128,1024]{1,0:T(8,128)(2,1)S(1)}, u32[]{:S(2)}, u32[]{:S(2)}) collective-permute-start(bf16[128,1024]{1,0:T(8,128)(2,1)S(1)} %get-tuple-element.16), channel_id=1, source_target_pairs={{0,1},{1,0},{2,3},{3,2},{4,5},{5,4},{6,7},{7,6},{8,9},{9,8},{10,11... | collective-permute-start | bytes 786440 | tf_op jit(solution)/shard_map/ppermute | solution.py:253
  46.4 5.0 %collective-permute-start.10 = (bf16[16,1024]{1,0:T(8,128)(2,1)S(1)}, bf16[16,1024]{1,0:T(8,128)(2,1)S(1)}, u32[]{:S(2)}, u32[]{:S(2)}) collective-permute-start(bf16[16,1024]{1,0:T(8,128)(2,1)S(1)} %fusion.16), channel_id=1, source_target_pairs={{0,192},{2,194},{4,196},{6,198},{8,200},{10,202},{12,204},{14,206}... | collective-permute-start | bytes 98312 | tf_op jit(solution)/shard_map/ppermute | solution.py:191
  46.5 5.5 %collective-permute-start.9 = (bf16[16,1024]{1,0:T(8,128)(2,1)S(1)}, bf16[16,1024]{1,0:T(8,128)(2,1)S(1)}, u32[]{:S(2)}, u32[]{:S(2)}) collective-permute-start(bf16[16,1024]{1,0:T(8,128)(2,1)S(1)} %fusion.16), channel_id=1, source_target_pairs={{0,128},{2,130},{4,132},{6,134},{8,136},{10,138},{12,140},{14,142}... | collective-permute-start | bytes 98312 | tf_op jit(solution)/shard_map/ppermute | solution.py:191
  49.5 3.9 %collective-permute-start.8 = (bf16[16,1024]{1,0:T(8,128)(2,1)S(1)}, bf16[16,1024]{1,0:T(8,128)(2,1)S(1)}, u32[]{:S(2)}, u32[]{:S(2)}) collective-permute-start(bf16[16,1024]{1,0:T(8,128)(2,1)S(1)} %fusion.16), channel_id=1, source_target_pairs={{0,64},{2,66},{4,68},{6,70},{8,72},{10,74},{12,76},{14,78},{16,80}... | collective-permute-start | bytes 98312 | tf_op jit(solution)/shard_map/ppermute | solution.py:191
  53.6 14.4 %collective-permute-start.14 = (bf16[16,1024]{1,0:T(8,128)(2,1)S(1)}, bf16[16,1024]{1,0:T(8,128)(2,1)S(1)}, u32[]{:S(2)}, u32[]{:S(2)}) collective-permute-start(bf16[16,1024]{1,0:T(8,128)(2,1)S(1)} %get-tuple-element.17), channel_id=1, source_target_pairs={{0,1},{1,0},{2,3},{3,2},{4,5},{5,4},{6,7},{7,6},{8,9},{9,8},{10,11... | collective-permute-start | bytes 98312 | tf_op jit(solution)/shard_map/ppermute | solution.py:287
where the time goes:
time: 74.6 us; the launch traced here: 74.3 us
  starting transfers between devices  30.7 us (41%)
  waiting for transfers between devices  25 us (34%)
  Pallas kernels  14.2 us (19%)
  local copies, waits for them, and re-layouts  3.9 us (5%)
    ppermute x10, starting transfers between devices, stage(): arrived.append(lax.ppermute(sent, 'ctx', route))  12.1 us
    ppermute x1, waiting for transfers between devices, shards(): x_far = lax.ppermute(theirs.astype(BF16), 'chan', swap).astype(F32)  11 us
    ppermute x10, waiting for transfers between devices, stage(): arrived.append(lax.ppermute(sent, 'ctx', route))  8.2 us
    ppermute x1, starting transfers between devices, shards(): lax.ppermute(jnp.concatenate([rates, weights, skip], axis=0), 'chan', swap)  7.28 us
    pallas_call x2, Pallas kernels, local(): pl.pallas_call(local_kernel, grid=(width // tile,), in_specs=[pl.BlockSpe...  6.28 us
    ppermute x1, waiting for transfers between devices, shards(): lax.ppermute(x[:, toks - rim:, :], 'ctx', [(i, i + 1) for i in range(ctx_...  5.78 us
    ppermute x1, starting transfers between devices, shards(): g_far = lax.ppermute(g_send, 'chan', swap)  5.76 us
    pallas_call x1, Pallas kernels, shards(): pl.pallas_call(features_kernel, grid_spec=pltpu.PrefetchScalarGridSpec(nu...  4.8 us
  transfers between devices with their start and end apart: 15, of which 8 were waited for; matrix products, arithmetic and copies ran while one was open for 0% of the time, Pallas kernels for 8%

commit v1 on v0

v1 whole, which is shorter than its diff:
```python
import jax
import jax.numpy as jnp
from jax import lax
from jax.experimental import pallas as pl
from jax.experimental.pallas import tpu as pltpu
from jax.sharding import PartitionSpec as P

LANES = 128
SUB = 8
STEP = 32
F32 = jnp.float32
BF16 = jnp.bfloat16
VMEM_LIMIT = 16 * 1024 * 1024


def spread(ref, m, cols):
    return jnp.broadcast_to(ref[m : m + 1, cols], (SUB, LANES))


def tree_sum(terms):
    terms = list(terms)
    while len(terms) > 1:
        terms = [
            terms[i] + terms[i + 1] if i + 1 < len(terms) else terms[i]
            for i in range(0, len(terms), 2)
        ]
    return terms[0]


def short_conv(wide, taps, row, count, cols):
    total = taps[0] * wide[SUB + row : SUB + row + count, cols]
    for j in range(1, len(taps)):
        total = total + taps[j] * wide[SUB + row - j : SUB + row - j + count, cols]
    return total.astype(BF16)


def tap_rows(taps_ref, s, cols, count):
    return [
        jnp.broadcast_to(taps_ref[j, s : s + 1, cols], (count, LANES))
        for j in range(taps_ref.shape[0])
    ]


def state_kernel(
    x_hbm, halo_ref, taps_ref, rate_ref,
    gate_ref, ends_ref, state_ref, half_ref,
    raw, wide, gated, keep_ref, run_ref, sems,
):
    step_id = pl.program_id(0)
    steps = pl.num_programs(0)
    _, toks, width = wide.shape[0], wide.shape[1] - SUB, wide.shape[2]
    half = toks // 2
    rim = taps_ref.shape[0] - 1
    modes = rate_ref.shape[0]
    run = half // SUB

    def fetch(i):
        return pltpu.make_async_copy(
            x_hbm.at[pl.ds(1, 2), :, pl.ds(pl.multiple_of(i * width, LANES), width)],
            raw.at[i],
            sems.at[i],
        )

    @pl.when(step_id == 0)
    def _():
        for i in range(raw.shape[0]):
            fetch(i).start()

    keep_ref[...] = jnp.exp(-rate_ref[...])
    run_ref[...] = jnp.exp(-rate_ref[...] * run)
    fetch(step_id).wait()
    for s in range(2):
        wide[s, SUB - rim : SUB, :] = halo_ref[s + 1].astype(F32)
        for r in range(0, toks, STEP):
            wide[s, SUB + r : SUB + r + STEP, :] = raw[step_id, s, r : r + STEP, :].astype(F32)
    index = lax.broadcasted_iota(jnp.int32, (SUB, LANES), 0)
    for t, c in enumerate(range(0, width, LANES)):
        cols = slice(c, c + LANES)
        key_taps = tap_rows(taps_ref, 1, cols, STEP)
        value_taps = tap_rows(taps_ref, 2, cols, STEP)
        for r in range(0, toks, STEP):
            key = short_conv(wide.at[0], key_taps, r, STEP, cols)
            value = short_conv(wide.at[1], value_taps, r, STEP, cols)
            gate = (key.astype(F32) * value.astype(F32)).astype(BF16)
            gate_ref[r // half, r % half : r % half + STEP, cols] = gate
            gated[r : r + STEP, :] = gate.astype(F32)
        keep = [spread(keep_ref, m, cols) for m in range(modes)]
        run_keep = run_ref[:, cols]
        run_keep2 = run_keep * run_keep
        run_keep4 = run_keep2 * run_keep2
        half_rows = []
        for part in range(2):

            def advance(j, states, part=part):
                now = gated[pl.ds(j + part * half, SUB, stride=run), :]
                return tuple(k * state + now for k, state in zip(keep, states))

            ends = lax.fori_loop(
                1,
                run,
                advance,
                tuple(gated[pl.ds(part * half, SUB, stride=run), :] for _ in keep),
                unroll=5,
            )
            rows = []
            for m, end in enumerate(ends):
                ends_ref[part, t, m] = end
                for shift, factor in ((1, run_keep), (2, run_keep2), (4, run_keep4)):
                    end = end + jnp.broadcast_to(
                        factor[m : m + 1], (SUB, LANES)
                    ) * pltpu.roll(end, shift, 0)
                rows.append(end[SUB - 1 : SUB])
            half_rows.append(rows)
        run_keep8 = run_keep4 * run_keep4
        for m in range(modes):
            first, second = half_rows[0][m], half_rows[1][m]
            half_ref[m : m + 1, cols] = first
            state_ref[m : m + 1, cols] = run_keep8[m : m + 1] * first + second


def local_kernel(
    half_id, x_hbm, halo_ref, taps_ref, gate_ref, ends_ref, res_ref, rate_ref, skip_ref,
    out_ref, raw, wide, gated, shown, keep_ref, gain_ref, run_ref, sems,
):
    step_id = pl.program_id(0)
    part = half_id[0]
    half, width = gate_ref.shape
    rim = taps_ref.shape[0] - 1
    modes = rate_ref.shape[0]
    run = half // SUB

    def fetch(i):
        return pltpu.make_async_copy(
            x_hbm.at[0, :, pl.ds(pl.multiple_of(i * width, LANES), width)],
            raw.at[i],
            sems.at[i],
        )

    @pl.when(step_id == 0)
    def _():
        for i in range(raw.shape[0]):
            fetch(i).start()

    rates = rate_ref[...]
    keep_ref[...] = jnp.exp(-rates)
    run_ref[...] = jnp.exp(-rates * run)
    gain_ref[...] = res_ref[...] * jnp.sqrt(2.0 * rates)
    high = rates.astype(BF16)
    out_ref[2 * half : 2 * half + modes, :] = high
    out_ref[2 * half + modes : 2 * half + 2 * modes, :] = (rates - high.astype(F32)).astype(BF16)

    index = lax.broadcasted_iota(jnp.int32, (SUB, LANES), 0)
    for t, c in enumerate(range(0, width, LANES)):
        cols = slice(c, c + LANES)
        for r in range(0, half, STEP):
            gated[r : r + STEP, :] = gate_ref[r : r + STEP, cols].astype(F32)
        keep = [spread(keep_ref, m, cols) for m in range(modes)]
        gains = [spread(gain_ref, m, cols) for m in range(modes)]
        skip = spread(skip_ref, 0, cols)
        run_keep = run_ref[:, cols]
        run_keep2 = run_keep * run_keep
        run_keep4 = run_keep2 * run_keep2
        begins = []
        for m in range(modes):
            total = ends_ref[t, m]
            for shift, factor in ((1, run_keep), (2, run_keep2), (4, run_keep4)):
                total = total + jnp.where(
                    index >= shift,
                    jnp.broadcast_to(factor[m : m + 1], (SUB, LANES))
                    * pltpu.roll(total, shift, 0),
                    0.0,
                )
            begins.append(jnp.where(index >= 1, pltpu.roll(total, 1, 0), 0.0))

        def emit(j, states):
            now = gated[pl.ds(j, SUB, stride=run), :]
            states = tuple(k * state + now for k, state in zip(keep, states))
            shown[pl.ds(j, SUB, stride=run), :] = tree_sum(
                [skip * now] + [gain * state for gain, state in zip(gains, states)]
            )
            return states

        lax.fori_loop(0, run, emit, tuple(begins), unroll=4)
        for r in range(0, half, STEP):
            out_ref[half + r : half + r + STEP, cols] = shown[r : r + STEP, :].astype(BF16)

    fetch(step_id).wait()
    start = pl.multiple_of(part * half, half)
    for r in range(0, half, STEP):
        wide[SUB + r : SUB + r + STEP, :] = raw[
            step_id, pl.ds(pl.multiple_of(start + r, STEP), STEP), :
        ].astype(F32)
    before = raw[step_id, half - 16 : half, :].astype(F32)[16 - rim :]
    wide[SUB - rim : SUB, :] = jnp.where(part == 0, halo_ref[0].astype(F32), before)
    for c in range(0, width, LANES):
        cols = slice(c, c + LANES)
        taps = tap_rows(taps_ref, 0, cols, STEP)
        for r in range(0, half, STEP):
            out_ref[r : r + STEP, cols] = short_conv(wide, taps, r, STEP, cols)


def finish_kernel(
    chan_ref, own_ref, begin_own, far_ref, begin_far, out_ref, carry, keep_ref, run_ref
):
    side = chan_ref[0]
    modes, width = begin_own.shape
    half = out_ref.shape[0]
    run = half // SUB
    index = lax.broadcasted_iota(jnp.int32, (SUB, LANES), 0)
    for part, (pq_ref, begin_ref) in enumerate(((own_ref, begin_own), (far_ref, begin_far))):
        base = width * (side if part == 0 else 1 - side)
        rates = pq_ref[2 * half : 2 * half + modes, :].astype(F32) + pq_ref[
            2 * half + modes : 2 * half + 2 * modes, :
        ].astype(F32)
        keep_ref[...] = jnp.exp(-rates)
        run_ref[...] = jnp.exp(-rates * run)

        def tile(t, _, base=base, pq_ref=pq_ref, begin_ref=begin_ref):
            c = pl.multiple_of(t * LANES, LANES)
            cols = pl.ds(c, LANES)
            keep = [spread(keep_ref, m, cols) for m in range(modes)]
            run_keep = run_ref[:, cols]
            begin = begin_ref[:, cols].astype(F32) * keep_ref[:, cols]
            states = []
            powers = []
            for shift in (1, 2, 4):
                powers.append((index & shift, run_keep))
                run_keep = run_keep * run_keep
            for m in range(modes):
                state = jnp.broadcast_to(begin[m : m + 1], (SUB, LANES))
                for bit, factor in powers:
                    state = state * jnp.where(
                        bit != 0, jnp.broadcast_to(factor[m : m + 1], (SUB, LANES)), 1.0
                    )
                states.append(state)

            def fade(j, states):
                carry[pl.ds(j, SUB, stride=run), :] = tree_sum(states)
                return tuple(k * state for k, state in zip(keep, states))

            lax.fori_loop(0, run, fade, tuple(states), unroll=4)
            where = pl.ds(pl.multiple_of(base + c, LANES), LANES)
            for r in range(0, half, STEP):
                rows = slice(r, r + STEP)
                late = slice(half + r, half + r + STEP)
                out_ref[rows, where] = (
                    pq_ref[rows, cols].astype(F32)
                    * (pq_ref[late, cols].astype(F32) + carry[rows, :])
                ).astype(BF16)
            return 0

        lax.fori_loop(0, width // LANES, tile, 0)


def stage(run_state, prefix, span, index, stride, count, behind, last):
    ctx_count = lax.axis_size("ctx")
    place = index // stride % count
    sent = run_state.astype(BF16)
    arrived = []
    for k in range(1, count):
        route = []
        for i in range(ctx_count):
            j = i // stride % count
            if not last or j + k < count:
                route.append((i, i + ((j + k) % count - j) * stride))
        arrived.append(lax.ppermute(sent, "ctx", route))
    total = jnp.exp(-span * ((count - 1 - place) * stride).astype(F32)) * run_state
    for k, got in enumerate(arrived, 1):
        got = got.astype(F32)
        origin = (place - k) % count
        total = total + jnp.exp(-span * ((count - 1 - origin) * stride).astype(F32)) * got
        between = ((k - 1) * stride + behind).astype(F32)
        prefix = prefix + jnp.where(place >= k, jnp.exp(-span * between), 0.0) * got
    return total, prefix


def scan_counts(blocks):
    counts = [2] if blocks % 2 == 0 else []
    left = blocks // 2 if counts else blocks
    while left % 4 == 0:
        counts.append(4)
        left //= 4
    if left > 1:
        counts.append(left)
    return counts


def cheap(nbytes):
    return pl.CostEstimate(flops=1000, bytes_accessed=nbytes, transcendentals=0)


def shards(streams, short_filter, residue, decay_rate, skip_gain):
    ctx_count = lax.axis_size("ctx")
    index = lax.axis_index("ctx")
    side = lax.axis_index("chan")
    toks, _, width = streams.shape
    half = toks // 2
    modes = residue.shape[1]
    rim = short_filter.shape[0] - 1
    swap = [(0, 1), (1, 0)]
    tile = 256 if width % 256 == 0 else LANES
    steps = width // tile
    tiles = tile // LANES

    x = jnp.transpose(streams, (1, 0, 2))
    rates = decay_rate.T
    weights = residue.T
    skip = skip_gain[None, :]
    halo = lax.ppermute(
        x[:, toks - rim :, :], "ctx", [(i, i + 1) for i in range(ctx_count - 1)]
    )
    chan_id = side.astype(jnp.int32).reshape(1)

    x_kept, taps_kept, rates_kept = (
        pltpu.with_memory_space_constraint(a, pltpu.HBM) for a in (x, short_filter, rates)
    )
    params = pltpu.CompilerParams(vmem_limit_bytes=VMEM_LIMIT)
    in_hbm = pl.BlockSpec(memory_space=pltpu.HBM)
    strip = lambda *lead: pl.BlockSpec(lead + (tile,), lambda i, *_: (0,) * len(lead) + (i,))
    gate, ends, state, state_half = pl.pallas_call(
        state_kernel,
        grid=(steps,),
        in_specs=[in_hbm, strip(3, rim), strip(rim + 1, 3), strip(modes)],
        out_specs=[
            strip(2, half),
            pl.BlockSpec((2, tiles, modes, SUB, LANES), lambda i: (0, i, 0, 0, 0)),
            strip(modes),
            strip(modes),
        ],
        out_shape=[
            jax.ShapeDtypeStruct((2, half, width), BF16),
            jax.ShapeDtypeStruct((2, width // LANES, modes, SUB, LANES), F32),
            jax.ShapeDtypeStruct((modes, width), F32),
            jax.ShapeDtypeStruct((modes, width), F32),
        ],
        scratch_shapes=[
            pltpu.VMEM((steps, 2, toks, tile), BF16),
            pltpu.VMEM((2, toks + SUB, tile), F32),
            pltpu.VMEM((toks, LANES), F32),
            pltpu.VMEM((modes, tile), F32),
            pltpu.VMEM((modes, tile), F32),
            pltpu.SemaphoreType.DMA((steps,)),
        ],
        compiler_params=params,
        cost_estimate=cheap(1000),
        name="states",
    )(x_kept, halo, taps_kept, rates_kept)

    def local(which, name):
        return pl.pallas_call(
            local_kernel,
            grid_spec=pltpu.PrefetchScalarGridSpec(
                num_scalar_prefetch=1,
                grid=(steps,),
                in_specs=[
                    in_hbm,
                    strip(3, rim),
                    strip(rim + 1, 3),
                    pl.BlockSpec((None, half, tile), lambda i, w: (w[0], 0, i)),
                    pl.BlockSpec(
                        (None, tiles, modes, SUB, LANES), lambda i, w: (w[0], i, 0, 0, 0)
                    ),
                    strip(modes),
                    strip(modes),
                    strip(1),
                ],
                out_specs=strip(2 * half + 2 * modes),
                scratch_shapes=[
                    pltpu.VMEM((steps, toks, tile), BF16),
                    pltpu.VMEM((half + SUB, tile), F32),
                    pltpu.VMEM((half, LANES), F32),
                    pltpu.VMEM((half, LANES), F32),
                    pltpu.VMEM((modes, tile), F32),
                    pltpu.VMEM((modes, tile), F32),
                    pltpu.VMEM((modes, tile), F32),
                    pltpu.SemaphoreType.DMA((steps,)),
                ],
            ),
            out_shape=jax.ShapeDtypeStruct((2 * half + 2 * modes, width), BF16),
            compiler_params=params,
            cost_estimate=cheap(1000),
            name=name,
        )(which, x_kept, halo, short_filter, gate, ends, weights, rates, skip)

    sent = local(1 - chan_id, "local_sent")
    own = local(chan_id, "local_own")

    span = rates * float(toks)
    prefix = jnp.zeros_like(state)
    run_state = state
    stride = 1
    counts = scan_counts(ctx_count)
    for level, count in enumerate(counts):
        if level == 1:
            run_state, sent = lax.optimization_barrier((run_state, sent))
        last = level == len(counts) - 1
        run_state, prefix = stage(
            run_state, prefix, span, index, stride, count, index % stride, last
        )
        stride *= count

    far = lax.ppermute(sent, "chan", swap)
    gains = weights * jnp.sqrt(2.0 * rates)
    first = gains * prefix
    second = gains * (jnp.exp(-rates * float(half)) * prefix + state_half)
    mine = jnp.where(side == 0, first, second)
    theirs = jnp.where(side == 0, second, first).astype(BF16)
    begin_far = lax.ppermute(theirs, "chan", swap)

    full = lambda a: pl.BlockSpec(a.shape, lambda *_: (0,) * a.ndim)
    operands = (own, mine, far, begin_far)
    return pl.pallas_call(
        finish_kernel,
        grid_spec=pltpu.PrefetchScalarGridSpec(
            num_scalar_prefetch=1,
            grid=(1,),
            in_specs=[full(a) for a in operands],
            out_specs=pl.BlockSpec((half, 2 * width), lambda *_: (0, 0)),
            scratch_shapes=[
                pltpu.VMEM((half, LANES), F32),
                pltpu.VMEM((modes, width), F32),
                pltpu.VMEM((modes, width), F32),
            ],
        ),
        out_shape=jax.ShapeDtypeStruct((half, 2 * width), BF16),
        compiler_params=params,
        cost_estimate=cheap(1000),
        name="finish",
    )(chan_id, *operands)


def solution(mesh):
    return jax.shard_map(
        shards,
        mesh=mesh,
        in_specs=(
            P("ctx", None, "chan"),
            P(None, None, "chan"),
            P("chan", None),
            P("chan", None),
            P("chan"),
        ),
        out_specs=P(("ctx", "chan"), None),
        check_vma=False,
    )
```

time: 74.6 us -> 65.4 us (0.88)
  the two profiles are of different devices: /device:TPU:12 before, /device:TPU:40 now
where the time goes in v1:
time: 65.4 us; the launch traced here: 65.1 us
  starting transfers between devices  29.8 us (46%)
  waiting for transfers between devices  20 us (31%)
  Pallas kernels  13.7 us (21%)
  local copies, waits for them, and re-layouts  0.87 us (1%)
    ppermute x10, starting transfers between devices, stage(): arrived.append(lax.ppermute(sent, 'ctx', route))  17.8 us
    ppermute x1, waiting for transfers between devices, shards(): begin_far = lax.ppermute(theirs, 'chan', swap)  13 us
    ppermute x1, starting transfers between devices, shards(): far = lax.ppermute(sent, 'chan', swap)  7.19 us
    pallas_call x2, Pallas kernels, local(): pl.pallas_call(local_kernel, grid_spec=pltpu.PrefetchScalarGridSpec(num_s...  5.75 us
    pallas_call x1, Pallas kernels, shards(): pl.pallas_call(state_kernel, grid=(steps,), in_specs=[in_hbm, strip(3, ri...  5.07 us
    ppermute x10, waiting for transfers between devices, stage(): arrived.append(lax.ppermute(sent, 'ctx', route))  3.93 us
    ppermute x1, waiting for transfers between devices, shards(): lax.ppermute(x[:, toks - rim:, :], 'ctx', [(i, i + 1) for i in range(ctx_...  3.09 us
    ppermute x1, starting transfers between devices, shards(): begin_far = lax.ppermute(theirs, 'chan', swap)  2.85 us
  transfers between devices with their start and end apart: 13, of which 4 were waited for; matrix products, arithmetic and copies ran while one was open for 0% of the time, Pallas kernels for 9%

profile of v1, /device:TPU:40, one launch (start us, length us, event | category | flops | bytes accessed | tf_op | source)
XLA Modules:
  0.0 65.1 jit_solution(10228538398641246070)
XLA Ops:
  0.0 0.0 copy-start
  0.0 0.0 copy-start.2
  0.0 0.0 copy-start.1
  0.0 0.0 copy-start.3
  0.0 0.9 %slice.4 = bf16[3,2,1024]{2,1,0:T(2,128)(2,1)S(1)} slice(bf16[3,256,1024]{2,1,0:T(8,128)(2,1)} %bitcast.32), slice={[0:3], [254:256], [0:1024]} | slice | bytes 24576 | tf_op jit(solution)/shard_map/slice | solution.py:310
  0.9 1.9 %collective-permute-start = (bf16[3,2,1024]{2,1,0:T(2,128)(2,1)S(1)}, bf16[3,2,1024]{2,1,0:T(2,128)(2,1)S(1)}, u32[]{:S(2)}, u32[]{:S(2)}) collective-permute-start(bf16[3,2,1024]{2,1,0:T(2,128)(2,1)S(1)} %slice.4), channel_id=1, source_target_pairs={{0,2},{2,4},{4,6},{6,8},{8,10},{10,12},{12,14},{14,16},{16,18},{18... | collective-permute-start | bytes 36872 | tf_op jit(solution)/shard_map/ppermute | solution.py:309
  2.8 3.1 %collective-permute-done.halo_ref = bf16[3,2,1024]{2,1,0:T(2,128)(2,1)S(1)} collective-permute-done((bf16[3,2,1024]{2,1,0:T(2,128)(2,1)S(1)}, bf16[3,2,1024]{2,1,0:T(2,128)(2,1)S(1)}, u32[]{:S(2)}, u32[]{:S(2)}) %collective-permute-start) | collective-permute-done | bytes 12320 | tf_op jit(solution)/shard_map/ppermute | solution.py:309
  5.9 5.1 %states.1 = (bf16[2,128,1024]{2,1,0:T(8,128)(2,1)S(1)}, f32[2,8,16,8,128]{4,3,2,1,0:T(8,128)S(1)}, f32[16,1024]{1,0:T(8,128)S(1)}, f32[16,1024]{1,0:T(8,128)S(1)}) custom-call(bf16[3,256,1024]{2,1,0:T(8,128)(2,1)} %bitcast.33, bf16[3,2,1024]{2,1,0:T(2,128)(2,1)S(1)} %collective-permute-done.halo_ref, f32[3,3,1024]{2,1,0:T(4,128)} %taps_ref.5, ...), custom_call_target="tpu_custom_call" | custom-call | flops 1000 | bytes 1000 | tf_op jit(solution)/shard_map/states/pallas_call | solution.py:320
  11.0 0.1 collective-permute-start.1
  11.1 0.0 copy-done
  11.1 0.0 copy-done.2
  11.1 0.0 copy-done.1
  11.1 0.0 copy-done.3
  11.2 2.9 %local_sent.1 = bf16[288,1024]{1,0:T(8,128)(2,1)S(1)} custom-call(s32[1]{0:T(128)S(6)} %sub.69.half_id, bf16[3,256,1024]{2,1,0:T(8,128)(2,1)} %bitcast.34, bf16[3,2,1024]{2,1,0:T(2,128)(2,1)S(1)} %collective-permute-done.halo_ref, f32[3,3,1024]{2,1,0:T(4,128)S(1)} %copy-done.2, bf16[2,128,1024]{2,1,0:T(8,128)(2,1)S(1)} %get-tuple-element.11.gate_ref, ...), custom_call_target="tpu_custom_call" | custom-call | flops 1000 | bytes 1000 | tf_op jit(solution)/shard_map/local_sent/pallas_call | solution.py:350
  14.0 0.0 collective-permute-done.1
  14.1 2.0 %collective-permute-start.2 = (bf16[16,1024]{1,0:T(8,128)(2,1)S(1)}, bf16[16,1024]{1,0:T(8,128)(2,1)S(1)}, u32[]{:S(2)}, u32[]{:S(2)}) collective-permute-start(bf16[16,1024]{1,0:T(8,128)(2,1)S(1)} %convert_element_type.108), channel_id=1, source_target_pairs={{0,4},{2,6},{4,8},{6,10},{8,12},{10,14},{12,0},{14,2},{16,20},{18,... | collective-permute-start | bytes 98312 | tf_op jit(solution)/shard_map/ppermute | solution.py:266
  16.1 5.4 %collective-permute-start.3 = (bf16[16,1024]{1,0:T(8,128)(2,1)S(1)}, bf16[16,1024]{1,0:T(8,128)(2,1)S(1)}, u32[]{:S(2)}, u32[]{:S(2)}) collective-permute-start(bf16[16,1024]{1,0:T(8,128)(2,1)S(1)} %convert_element_type.108), channel_id=1, source_target_pairs={{0,8},{2,10},{4,12},{6,14},{8,0},{10,2},{12,4},{14,6},{16,24},{18,... | collective-permute-start | bytes 98312 | tf_op jit(solution)/shard_map/ppermute | solution.py:266
  21.5 0.0 collective-permute-start.4
  21.5 0.0 collective-permute-done.2
  21.5 2.8 %collective-permute-done.3 = bf16[16,1024]{1,0:T(8,128)(2,1)S(1)} collective-permute-done((bf16[16,1024]{1,0:T(8,128)(2,1)S(1)}, bf16[16,1024]{1,0:T(8,128)(2,1)S(1)}, u32[]{:S(2)}, u32[]{:S(2)}) %collective-permute-start.3) | collective-permute-done | bytes 32800 | tf_op jit(solution)/shard_map/ppermute | solution.py:266
  24.2 1.1 %collective-permute-done.4 = bf16[16,1024]{1,0:T(8,128)(2,1)S(1)} collective-permute-done((bf16[16,1024]{1,0:T(8,128)(2,1)S(1)}, bf16[16,1024]{1,0:T(8,128)(2,1)S(1)}, u32[]{:S(2)}, u32[]{:S(2)}) %collective-permute-start.4) | collective-permute-done | bytes 32800 | tf_op jit(solution)/shard_map/ppermute | solution.py:266
  25.4 0.1 fusion.19
  25.4 0.1 collective-permute-start.5
  25.5 2.1 %collective-permute-start.6 = (bf16[16,1024]{1,0:T(8,128)(2,1)S(1)}, bf16[16,1024]{1,0:T(8,128)(2,1)S(1)}, u32[]{:S(2)}, u32[]{:S(2)}) collective-permute-start(bf16[16,1024]{1,0:T(8,128)(2,1)S(1)} %get-tuple-element.20), channel_id=1, source_target_pairs={{0,32},{2,34},{4,36},{6,38},{8,40},{10,42},{12,44},{14,46},{16,48}... | collective-permute-start | bytes 98312 | tf_op jit(solution)/shard_map/ppermute | solution.py:266
  27.6 1.4 %collective-permute-start.7 = (bf16[16,1024]{1,0:T(8,128)(2,1)S(1)}, bf16[16,1024]{1,0:T(8,128)(2,1)S(1)}, u32[]{:S(2)}, u32[]{:S(2)}) collective-permute-start(bf16[16,1024]{1,0:T(8,128)(2,1)S(1)} %get-tuple-element.20), channel_id=1, source_target_pairs={{0,48},{2,50},{4,52},{6,54},{8,56},{10,58},{12,60},{14,62},{16,0},... | collective-permute-start | bytes 98312 | tf_op jit(solution)/shard_map/ppermute | solution.py:266
  29.1 7.2 %collective-permute-start.11 = (bf16[288,1024]{1,0:T(8,128)(2,1)S(1)}, bf16[288,1024]{1,0:T(8,128)(2,1)S(1)}, u32[]{:S(2)}, u32[]{:S(2)}) collective-permute-start(bf16[288,1024]{1,0:T(8,128)(2,1)S(1)} %local_sent.1), channel_id=1, source_target_pairs={{0,1},{1,0},{2,3},{3,2},{4,5},{5,4},{6,7},{7,6},{8,9},{9,8},{10,11... | collective-permute-start | bytes 1769480 | tf_op jit(solution)/shard_map/ppermute | solution.py:402
  36.2 0.0 collective-permute-done.5
  36.3 0.0 collective-permute-done.6
  36.3 0.0 collective-permute-done.7
  36.3 0.1 fusion.16
  36.3 0.7 %collective-permute-start.10 = (bf16[16,1024]{1,0:T(8,128)(2,1)S(1)}, bf16[16,1024]{1,0:T(8,128)(2,1)S(1)}, u32[]{:S(2)}, u32[]{:S(2)}) collective-permute-start(bf16[16,1024]{1,0:T(8,128)(2,1)S(1)} %fusion.16), channel_id=1, source_target_pairs={{0,192},{2,194},{4,196},{6,198},{8,200},{10,202},{12,204},{14,206}... | collective-permute-start | bytes 98312 | tf_op jit(solution)/shard_map/ppermute | solution.py:266
  37.0 3.5 %collective-permute-start.8 = (bf16[16,1024]{1,0:T(8,128)(2,1)S(1)}, bf16[16,1024]{1,0:T(8,128)(2,1)S(1)}, u32[]{:S(2)}, u32[]{:S(2)}) collective-permute-start(bf16[16,1024]{1,0:T(8,128)(2,1)S(1)} %fusion.16), channel_id=1, source_target_pairs={{0,64},{2,66},{4,68},{6,70},{8,72},{10,74},{12,76},{14,78},{16,80}... | collective-permute-start | bytes 98312 | tf_op jit(solution)/shard_map/ppermute | solution.py:266
  40.5 2.6 %collective-permute-start.9 = (bf16[16,1024]{1,0:T(8,128)(2,1)S(1)}, bf16[16,1024]{1,0:T(8,128)(2,1)S(1)}, u32[]{:S(2)}, u32[]{:S(2)}) collective-permute-start(bf16[16,1024]{1,0:T(8,128)(2,1)S(1)} %fusion.16), channel_id=1, source_target_pairs={{0,128},{2,130},{4,132},{6,134},{8,136},{10,138},{12,140},{14,142}... | collective-permute-start | bytes 98312 | tf_op jit(solution)/shard_map/ppermute | solution.py:266
  43.2 2.9 %local_own.1.own_ref = bf16[288,1024]{1,0:T(8,128)(2,1)S(1)} custom-call(s32[1]{0:T(128)} %bitcast.half_id.chan_ref, bf16[3,256,1024]{2,1,0:T(8,128)(2,1)} %bitcast.35, bf16[3,2,1024]{2,1,0:T(2,128)(2,1)S(1)} %collective-permute-done.halo_ref, f32[3,3,1024]{2,1,0:T(4,128)S(1)} %copy-done.2, bf16[2,128,1024]{2,1,0:T(8,128)(2,1)S(1)} %get-tuple-element.11.gate_ref, ...), custom_call_target="tpu_custom_call" | custom-call | flops 1000 | bytes 1000 | tf_op jit(solution)/shard_map/local_own/pallas_call | solution.py:350
  46.1 0.0 collective-permute-done.10
  46.1 0.0 collective-permute-done.8
  46.1 0.0 collective-permute-done.9
  46.1 0.2 select_convert_fusion
  46.4 2.9 %collective-permute-start.12 = (bf16[16,1024]{1,0:T(8,128)(2,1)S(1)}, bf16[16,1024]{1,0:T(8,128)(2,1)S(1)}, u32[]{:S(2)}, u32[]{:S(2)}) collective-permute-start(bf16[16,1024]{1,0:T(8,128)(2,1)S(1)} %get-tuple-element.17), channel_id=1, source_target_pairs={{0,1},{1,0},{2,3},{3,2},{4,5},{5,4},{6,7},{7,6},{8,9},{9,8},{10,11... | collective-permute-start | bytes 98312 | tf_op jit(solution)/shard_map/ppermute | solution.py:408
  49.3 13.0 %collective-permute-done.12.begin_far = bf16[16,1024]{1,0:T(8,128)(2,1)S(1)} collective-permute-done((bf16[16,1024]{1,0:T(8,128)(2,1)S(1)}, bf16[16,1024]{1,0:T(8,128)(2,1)S(1)}, u32[]{:S(2)}, u32[]{:S(2)}) %collective-permute-start.12) | collective-permute-done | bytes 32800 | tf_op jit(solution)/shard_map/ppermute | solution.py:408
  62.3 0.0 collective-permute-done.11.far_ref
  62.3 2.9 %finish.1 = bf16[128,2048]{1,0:T(8,128)(2,1)} custom-call(s32[1]{0:T(128)} %bitcast.half_id.chan_ref, bf16[288,1024]{1,0:T(8,128)(2,1)S(1)} %local_own.1.own_ref, f32[16,1024]{1,0:T(8,128)S(1)} %broadcast_select_fusion.begin_own, bf16[288,1024]{1,0:T(8,128)(2,1)S(1)} %collective-permute-done.11.far_ref, bf16[16,1024]{1,0:T(8,128)(2,1)S(1)} %collective-permute-done.12.begin_far), custom_call_target="tpu_custom_call" | custom-call | flops 1000 | bytes 1000 | tf_op jit(solution)/shard_map/finish/pallas_call | solution.py:412
  (4 shorter events, 0.1 us)
Async XLA Ops:
  0.0 11.1 %copy-start = (f32[1024,16]{0,1:T(8,128)S(1)}, f32[1024,16]{0,1:T(8,128)}, u32[]{:S(2)}) copy-start(f32[1024,16]{0,1:T(8,128)} %param.8) | copy-start | bytes 196612
  0.0 11.1 %copy-start.2 = (f32[3,3,1024]{2,1,0:T(4,128)S(1)}, f32[3,3,1024]{2,1,0:T(4,128)}, u32[]{:S(2)}) copy-start(f32[3,3,1024]{2,1,0:T(4,128)} %taps_ref.5) | copy-start | bytes 110596
  0.0 11.1 %copy-start.1 = (f32[1024,16]{0,1:T(8,128)S(1)}, f32[1024,16]{0,1:T(8,128)}, u32[]{:S(2)}) copy-start(f32[1024,16]{0,1:T(8,128)} %param.7) | copy-start | bytes 196612
  0.0 11.1 %copy-start.3 = (f32[1024]{0:T(1024)S(1)}, f32[1024]{0:T(1024)}, u32[]{:S(2)}) copy-start(f32[1024]{0:T(1024)} %param.9) | copy-start | bytes 12292
  0.9 5.0 %collective-permute-start = (bf16[3,2,1024]{2,1,0:T(2,128)(2,1)S(1)}, bf16[3,2,1024]{2,1,0:T(2,128)(2,1)S(1)}, u32[]{:S(2)}, u32[]{:S(2)}) collective-permute-start(bf16[3,2,1024]{2,1,0:T(2,128)(2,1)S(1)} %slice.4), channel_id=1, source_target_pairs={{0,2},{2,4},{4,6},{6,8},{8,10},{10,12},{12,14},{14,16},{16,18},{18... | collective-permute-start | bytes 36872 | tf_op jit(solution)/shard_map/ppermute | solution.py:309
  11.0 3.1 %collective-permute-start.1 = (bf16[16,1024]{1,0:T(8,128)(2,1)S(1)}, bf16[16,1024]{1,0:T(8,128)(2,1)S(1)}, u32[]{:S(2)}, u32[]{:S(2)}) collective-permute-start(bf16[16,1024]{1,0:T(8,128)(2,1)S(1)} %convert_element_type.103), channel_id=1, source_target_pairs={{0,2},{2,0},{4,6},{6,4},{8,10},{10,8},{12,14},{14,12},{16,18},{18,... | collective-permute-start | bytes 98312 | tf_op jit(solution)/shard_map/ppermute | solution.py:266
  14.1 7.4 %collective-permute-start.2 = (bf16[16,1024]{1,0:T(8,128)(2,1)S(1)}, bf16[16,1024]{1,0:T(8,128)(2,1)S(1)}, u32[]{:S(2)}, u32[]{:S(2)}) collective-permute-start(bf16[16,1024]{1,0:T(8,128)(2,1)S(1)} %convert_element_type.108), channel_id=1, source_target_pairs={{0,4},{2,6},{4,8},{6,10},{8,12},{10,14},{12,0},{14,2},{16,20},{18,... | collective-permute-start | bytes 98312 | tf_op jit(solution)/shard_map/ppermute | solution.py:266
  16.1 8.1 %collective-permute-start.3 = (bf16[16,1024]{1,0:T(8,128)(2,1)S(1)}, bf16[16,1024]{1,0:T(8,128)(2,1)S(1)}, u32[]{:S(2)}, u32[]{:S(2)}) collective-permute-start(bf16[16,1024]{1,0:T(8,128)(2,1)S(1)} %convert_element_type.108), channel_id=1, source_target_pairs={{0,8},{2,10},{4,12},{6,14},{8,0},{10,2},{12,4},{14,6},{16,24},{18,... | collective-permute-start | bytes 98312 | tf_op jit(solution)/shard_map/ppermute | solution.py:266
  21.5 3.9 %collective-permute-start.4 = (bf16[16,1024]{1,0:T(8,128)(2,1)S(1)}, bf16[16,1024]{1,0:T(8,128)(2,1)S(1)}, u32[]{:S(2)}, u32[]{:S(2)}) collective-permute-start(bf16[16,1024]{1,0:T(8,128)(2,1)S(1)} %convert_element_type.108), channel_id=1, source_target_pairs={{0,12},{2,14},{4,0},{6,2},{8,4},{10,6},{12,8},{14,10},{16,28},{18,... | collective-permute-start | bytes 98312 | tf_op jit(solution)/shard_map/ppermute | solution.py:266
  25.4 10.8 %collective-permute-start.5 = (bf16[16,1024]{1,0:T(8,128)(2,1)S(1)}, bf16[16,1024]{1,0:T(8,128)(2,1)S(1)}, u32[]{:S(2)}, u32[]{:S(2)}) collective-permute-start(bf16[16,1024]{1,0:T(8,128)(2,1)S(1)} %get-tuple-element.20), channel_id=1, source_target_pairs={{0,16},{2,18},{4,20},{6,22},{8,24},{10,26},{12,28},{14,30},{16,32}... | collective-permute-start | bytes 98312 | tf_op jit(solution)/shard_map/ppermute | solution.py:266
  25.5 10.7 %collective-permute-start.6 = (bf16[16,1024]{1,0:T(8,128)(2,1)S(1)}, bf16[16,1024]{1,0:T(8,128)(2,1)S(1)}, u32[]{:S(2)}, u32[]{:S(2)}) collective-permute-start(bf16[16,1024]{1,0:T(8,128)(2,1)S(1)} %get-tuple-element.20), channel_id=1, source_target_pairs={{0,32},{2,34},{4,36},{6,38},{8,40},{10,42},{12,44},{14,46},{16,48}... | collective-permute-start | bytes 98312 | tf_op jit(solution)/shard_map/ppermute | solution.py:266
  27.6 8.6 %collective-permute-start.7 = (bf16[16,1024]{1,0:T(8,128)(2,1)S(1)}, bf16[16,1024]{1,0:T(8,128)(2,1)S(1)}, u32[]{:S(2)}, u32[]{:S(2)}) collective-permute-start(bf16[16,1024]{1,0:T(8,128)(2,1)S(1)} %get-tuple-element.20), channel_id=1, source_target_pairs={{0,48},{2,50},{4,52},{6,54},{8,56},{10,58},{12,60},{14,62},{16,0},... | collective-permute-start | bytes 98312 | tf_op jit(solution)/shard_map/ppermute | solution.py:266
  29.1 33.2 %collective-permute-start.11 = (bf16[288,1024]{1,0:T(8,128)(2,1)S(1)}, bf16[288,1024]{1,0:T(8,128)(2,1)S(1)}, u32[]{:S(2)}, u32[]{:S(2)}) collective-permute-start(bf16[288,1024]{1,0:T(8,128)(2,1)S(1)} %local_sent.1), channel_id=1, source_target_pairs={{0,1},{1,0},{2,3},{3,2},{4,5},{5,4},{6,7},{7,6},{8,9},{9,8},{10,11... | collective-permute-start | bytes 1769480 | tf_op jit(solution)/shard_map/ppermute | solution.py:402
  36.3 9.8 %collective-permute-start.10 = (bf16[16,1024]{1,0:T(8,128)(2,1)S(1)}, bf16[16,1024]{1,0:T(8,128)(2,1)S(1)}, u32[]{:S(2)}, u32[]{:S(2)}) collective-permute-start(bf16[16,1024]{1,0:T(8,128)(2,1)S(1)} %fusion.16), channel_id=1, source_target_pairs={{0,192},{2,194},{4,196},{6,198},{8,200},{10,202},{12,204},{14,206}... | collective-permute-start | bytes 98312 | tf_op jit(solution)/shard_map/ppermute | solution.py:266
  37.0 9.1 %collective-permute-start.8 = (bf16[16,1024]{1,0:T(8,128)(2,1)S(1)}, bf16[16,1024]{1,0:T(8,128)(2,1)S(1)}, u32[]{:S(2)}, u32[]{:S(2)}) collective-permute-start(bf16[16,1024]{1,0:T(8,128)(2,1)S(1)} %fusion.16), channel_id=1, source_target_pairs={{0,64},{2,66},{4,68},{6,70},{8,72},{10,74},{12,76},{14,78},{16,80}... | collective-permute-start | bytes 98312 | tf_op jit(solution)/shard_map/ppermute | solution.py:266
  40.5 5.6 %collective-permute-start.9 = (bf16[16,1024]{1,0:T(8,128)(2,1)S(1)}, bf16[16,1024]{1,0:T(8,128)(2,1)S(1)}, u32[]{:S(2)}, u32[]{:S(2)}) collective-permute-start(bf16[16,1024]{1,0:T(8,128)(2,1)S(1)} %fusion.16), channel_id=1, source_target_pairs={{0,128},{2,130},{4,132},{6,134},{8,136},{10,138},{12,140},{14,142}... | collective-permute-start | bytes 98312 | tf_op jit(solution)/shard_map/ppermute | solution.py:266
  46.4 15.9 %collective-permute-start.12 = (bf16[16,1024]{1,0:T(8,128)(2,1)S(1)}, bf16[16,1024]{1,0:T(8,128)(2,1)S(1)}, u32[]{:S(2)}, u32[]{:S(2)}) collective-permute-start(bf16[16,1024]{1,0:T(8,128)(2,1)S(1)} %get-tuple-element.17), channel_id=1, source_target_pairs={{0,1},{1,0},{2,3},{3,2},{4,5},{5,4},{6,7},{7,6},{8,9},{9,8},{10,11... | collective-permute-start | bytes 98312 | tf_op jit(solution)/shard_map/ppermute | solution.py:408

commit v2 on v1

v2 whole, which is shorter than its diff:
```python
import jax
import jax.numpy as jnp
from jax import lax
from jax.experimental import pallas as pl
from jax.experimental.pallas import tpu as pltpu
from jax.sharding import PartitionSpec as P

LANES = 128
SUB = 8
STEP = 32
PAIR = 16
F32 = jnp.float32
BF16 = jnp.bfloat16
VMEM_LIMIT = 16 * 1024 * 1024


def spread(ref, m, cols):
    return jnp.broadcast_to(ref[m : m + 1, cols], (SUB, LANES))


def tree_sum(terms):
    terms = list(terms)
    while len(terms) > 1:
        terms = [
            terms[i] + terms[i + 1] if i + 1 < len(terms) else terms[i]
            for i in range(0, len(terms), 2)
        ]
    return terms[0]


def short_conv(load, taps, j):
    total = taps[0] * load(j)
    for k in range(1, len(taps)):
        total = total + taps[k] * load(j - k)
    return total


def tap_rows(taps_ref, s, cols):
    return [
        jnp.broadcast_to(taps_ref[j, s : s + 1, cols], (SUB, LANES))
        for j in range(taps_ref.shape[0])
    ]


def modes_at(ref, i, modes):
    return jnp.concatenate(
        [ref[pl.ds(i + SUB * m, SUB, stride=SUB), :] for m in range(0, modes, SUB)], axis=0
    )


def put_modes_at(ref, i, value):
    for m in range(0, value.shape[0], SUB):
        ref[pl.ds(i + SUB * m, SUB, stride=SUB), :] = value[m : m + SUB]


def state_kernel(
    x_hbm, taps_ref, rate_ref,
    gate_ref, ends_ref, state_ref, sum_ref,
    raw, raw_query, wide, keep_ref, run_ref, sems,
):
    step_id = pl.program_id(0)
    _, _, toks, width = raw.shape
    half = toks // 2
    rim = taps_ref.shape[0] - 1
    modes = rate_ref.shape[0]
    run = half // SUB

    def fetches(i):
        cols = pl.ds(pl.multiple_of(i * width, LANES), width)
        return (
            pltpu.make_async_copy(x_hbm.at[pl.ds(1, 2), :, cols], raw.at[i], sems.at[0, i]),
            pltpu.make_async_copy(
                x_hbm.at[0, pl.ds(0, PAIR), cols], raw_query.at[i, 0], sems.at[1, i]
            ),
            pltpu.make_async_copy(
                x_hbm.at[0, pl.ds(toks - PAIR, PAIR), cols], raw_query.at[i, 1], sems.at[2, i]
            ),
        )

    @pl.when(step_id == 0)
    def _():
        for i in range(raw.shape[0]):
            for copy in fetches(i):
                copy.start()

    keep_ref[...] = jnp.exp(-rate_ref[...])
    run_ref[...] = jnp.exp(-rate_ref[...] * run)
    for copy in fetches(step_id):
        copy.wait()
    index = lax.broadcasted_iota(jnp.int32, (SUB, LANES), 0)
    for t, c in enumerate(range(0, width, LANES)):
        cols = slice(c, c + LANES)
        for s in range(2):
            wide[s, :SUB, :] = jnp.zeros((SUB, LANES), F32)
            for r in range(0, toks, STEP):
                wide[s, SUB + r : SUB + r + STEP, :] = raw[
                    step_id, s, r : r + STEP, cols
                ].astype(F32)
        key_taps = tap_rows(taps_ref, 1, cols)
        value_taps = tap_rows(taps_ref, 2, cols)
        keep = [spread(keep_ref, m, cols) for m in range(modes)]
        total = None
        for part in range(2):
            base = part * half
            states = None
            for j in range(run):
                load = lambda s, at: wide[s, pl.ds(SUB + base + at, SUB, stride=run), :]
                key = short_conv(lambda at: load(0, at), key_taps, j)
                value = short_conv(lambda at: load(1, at), value_taps, j)
                gate = key * value
                if part == 0 and j < rim:
                    gate = jnp.where(index == 0, 0.0, gate)
                gate_ref[pl.ds(t * toks + base + j, SUB, stride=run), :] = gate
                if states is None:
                    states = [gate] * modes
                else:
                    states = [k * state + gate for k, state in zip(keep, states)]
            for m, end in enumerate(states):
                ends_ref[t, part, m * SUB : (m + 1) * SUB, :] = end
            run_keep = run_ref[:, cols]
            for i in range(SUB):
                end = modes_at(ends_ref.at[t, part], i, modes)
                total = end if total is None else run_keep * total + end
        state_ref[:, cols] = total
        sum_ref[:modes, cols] = total.astype(BF16)
        query = raw_query[step_id, :, :, cols].astype(F32)
        sum_ref[modes:, cols] = jnp.concatenate(
            [
                wide[0, SUB : SUB + rim, :],
                wide[1, SUB : SUB + rim, :],
                query[1, PAIR - rim :],
                wide[0, SUB + toks - rim : SUB + toks, :],
                wide[1, SUB + toks - rim : SUB + toks, :],
                query[0, :rim],
                jnp.zeros((PAIR - 6 * rim, LANES), F32),
            ],
            axis=0,
        ).astype(BF16)


def first_gates(past, first, taps):
    rows = []
    for s in range(2):
        before, here = past[s], first[s]
        line = [before[0:1], before[1:2], here[0:1], here[1:2]]
        rows.append(
            [
                taps[s][0] * line[at] + taps[s][1] * line[at - 1] + taps[s][2] * line[at - 2]
                for at in (2, 3)
            ]
        )
    return [key * value for key, value in zip(*rows)]


def join_kernel(ids, stride, count, toks, last, *refs):
    taps_ref, rate_ref, state_ref, prefix_ref, past_ref, own_ref = refs[:6]
    near = (own_ref,) + refs[6 : 5 + count]
    outs = refs[5 + count :]
    prefix_out, past_out = outs[:2]
    modes, width = rate_ref.shape
    index = ids[0]
    place = lax.rem(lax.div(index, stride), count)
    behind = lax.rem(index, stride)
    origins = [lax.rem(place - k + count, count) for k in range(count)]
    as_float = lambda n: n.astype(F32)

    def tile(t, _):
        cols = pl.ds(pl.multiple_of(t * LANES, LANES), LANES)
        rates = rate_ref[:, cols]
        span = rates * float(toks)
        taps = [[taps_ref[j, s : s + 1, cols] for j in range(3)] for s in (1, 2)]
        extra = [ref[modes:, cols].astype(F32) for ref in near]
        firsts = [(e[0:2], e[2:4]) for e in extra]
        states = [state_ref[:, cols]] + [ref[:modes, cols].astype(F32) for ref in near[1:]]
        first_keep = jnp.exp(-rates * float(toks - 1))
        second_keep = jnp.exp(-rates * float(toks - 2))
        rest = jnp.exp(-span * float(stride - 1))
        joins = []
        for k in range(count):
            linked = origins[k] >= 1
            past = extra[(k + 1) % count][4:10]
            past = jnp.where(linked, past, 0.0)
            one, two = first_gates((past[2:4], past[4:6]), firsts[k], taps)
            join = first_keep * one + second_keep * two
            if not last:
                join = jnp.where(linked, join, 0.0)
            joins.append(join)
            states[k] = states[k] + rest * join
        prefix = prefix_ref[:, cols] + jnp.where(
            behind >= 1,
            jnp.exp(-span * as_float(jnp.maximum(behind - 1, 0))) * joins[0],
            0.0,
        )
        for k in range(1, count):
            gap = as_float((k - 1) * stride + behind)
            prefix = prefix + jnp.where(place >= k, jnp.exp(-span * gap) * states[k], 0.0)
        prefix_out[:, cols] = prefix
        past = jnp.where((place >= 1) & (behind == 0), extra[1][4:10], past_ref[0:6, cols])
        past_out[:, cols] = jnp.concatenate([past, jnp.zeros((SUB - 6, LANES), F32)], axis=0)
        if not last:
            state_out, sum_out = outs[2:]
            total = None
            for k in range(count):
                gap = as_float((count - 1 - origins[k]) * stride)
                term = jnp.exp(-span * gap) * states[k]
                total = term if total is None else total + term
            state_out[:, cols] = total
            first = extra[0]
            end = extra[0]
            for k in range(1, count):
                first = jnp.where(origins[k] == 0, extra[k], first)
                end = jnp.where(origins[k] == count - 1, extra[k], end)
            sum_out[:modes, cols] = total.astype(BF16)
            sum_out[modes:, cols] = jnp.concatenate([first[0:4], end[4:]], axis=0).astype(BF16)
        return 0

    lax.fori_loop(0, width // LANES, tile, 0)


def local_kernel(
    part_id, x_hbm, taps_ref, gate_ref, ends_ref, res_ref, rate_ref, skip_ref,
    query_ref, local_ref, raw, wide, begins, keep_ref, gain_ref, run_ref, sems,
):
    step_id = pl.program_id(0)
    part = part_id[0]
    _, toks, width = raw.shape
    half = toks // 2
    rim = taps_ref.shape[0] - 1
    modes = rate_ref.shape[0]
    run = half // SUB

    def fetch(i):
        return pltpu.make_async_copy(
            x_hbm.at[0, :, pl.ds(pl.multiple_of(i * width, LANES), width)],
            raw.at[i],
            sems.at[i],
        )

    @pl.when(step_id == 0)
    def _():
        for i in range(raw.shape[0]):
            fetch(i).start()

    rates = rate_ref[...]
    keep_ref[...] = jnp.exp(-rates)
    run_ref[...] = jnp.exp(-rates * run)
    gain_ref[...] = res_ref[...] * jnp.sqrt(2.0 * rates)
    for t, c in enumerate(range(0, width, LANES)):
        cols = slice(c, c + LANES)
        run_keep = run_ref[:, cols]
        state = jnp.zeros((modes, LANES), F32)
        for i in range(SUB):
            state = run_keep * state + modes_at(ends_ref.at[t, 0], i, modes)
        state = jnp.where(part == 0, 0.0, state)
        for i in range(SUB):
            put_modes_at(begins, i, state)
            if i + 1 < SUB:
                state = run_keep * state + modes_at(ends_ref.at[t, part], i, modes)
        keep = [spread(keep_ref, m, cols) for m in range(modes)]
        gains = [spread(gain_ref, m, cols) for m in range(modes)]
        skip = spread(skip_ref, 0, cols)
        states = [begins[m * SUB : (m + 1) * SUB, :] for m in range(modes)]
        for j in range(run):
            now = gate_ref[pl.ds(t * toks + part * half + j, SUB, stride=run), :]
            states = [k * state + now for k, state in zip(keep, states)]
            local_ref[pl.ds(t * half + j, SUB, stride=run), :] = tree_sum(
                [skip * now] + [gain * state for gain, state in zip(gains, states)]
            )

    fetch(step_id).wait()
    start = pl.multiple_of(part * half, half)
    for t, c in enumerate(range(0, width, LANES)):
        cols = slice(c, c + LANES)
        for r in range(0, half, STEP):
            wide[SUB + r : SUB + r + STEP, :] = raw[
                step_id, pl.ds(pl.multiple_of(start + r, STEP), STEP), cols
            ].astype(F32)
        before = raw[step_id, half - 16 : half, cols].astype(F32)[16 - rim :]
        wide[SUB - rim : SUB, :] = before
        taps = tap_rows(taps_ref, 0, cols)
        for j in range(run):
            query_ref[pl.ds(t * half + j, SUB, stride=run), :] = short_conv(
                lambda at: wide[pl.ds(SUB + at, SUB, stride=run), :], taps, j
            )


def finish_kernel(
    ids, query_ref, local_ref, prefix_ref, past_ref, sum_ref, taps_ref, res_ref, rate_ref, skip_ref,
    out_ref, begins, carry,
):
    part = ids[0]
    modes, width = prefix_ref.shape
    half = out_ref.shape[0]
    run = half // SUB
    row = lax.broadcasted_iota(jnp.int32, (STEP, LANES), 0)
    for t, c in enumerate(range(0, width, LANES)):
        cols = slice(c, c + LANES)
        rates = rate_ref[:, cols]
        gains = res_ref[:, cols] * jnp.sqrt(2.0 * rates)
        keep_all = jnp.exp(-rates)
        run_keep = jnp.exp(-rates * run)
        past = past_ref[:, cols]
        here = sum_ref[modes:, cols].astype(F32)
        taps = [[taps_ref[j, s : s + 1, cols] for j in range(3)] for s in range(3)]
        one, two = first_gates((past[2:4], past[4:6]), (here[0:2], here[2:4]), taps[1:])
        line = [past[0:1], past[1:2], here[10:11], here[11:12]]
        queries = [
            taps[0][0] * line[at] + taps[0][1] * line[at - 1] + taps[0][2] * line[at - 2]
            for at in (2, 3)
        ]
        grow = jnp.exp(rates)
        state = gains * (prefix_ref[:, cols] + grow * (one + grow * two))
        state = state * jnp.where(part == 0, keep_all, jnp.exp(-rates * (half + 1)))
        for i in range(SUB):
            put_modes_at(begins, i, state)
            state = run_keep * state
        keep = [jnp.broadcast_to(keep_all[m : m + 1], (SUB, LANES)) for m in range(modes)]
        states = [begins[m * SUB : (m + 1) * SUB, :] for m in range(modes)]
        for j in range(run):
            carry[pl.ds(j, SUB, stride=run), :] = tree_sum(states)
            states = [k * state for k, state in zip(keep, states)]
        skip = skip_ref[:, cols]
        over = jnp.sum(gains * grow, axis=0, keepdims=True)
        for r in range(0, half, STEP):
            rows = slice(t * half + r, t * half + r + STEP)
            value = query_ref[rows, :] * (local_ref[rows, :] + carry[r : r + STEP, :])
            if r == 0:
                begin = carry[0:SUB, :]
                head = queries[0] * (begin[0:1] - over * two + skip * one)
                second = queries[1] * (begin[1:2] + skip * two)
                value = jnp.where((row == 0) & (part == 0), head, value)
                value = jnp.where((row == 1) & (part == 0), second, value)
            out_ref[r : r + STEP, cols] = value.astype(BF16)


def place_kernel(ids, far_ref, held_ref, out_ref, sem):
    del held_ref
    width = far_ref.shape[1]
    copy = pltpu.make_async_copy(
        far_ref,
        out_ref.at[:, pl.ds(pl.multiple_of(ids[0] * width, LANES), width)],
        sem,
    )
    copy.start()
    copy.wait()


def scan_counts(blocks):
    counts = [2] if blocks % 2 == 0 else []
    left = blocks // 2 if counts else blocks
    while left % 4 == 0:
        counts.append(4)
        left //= 4
    if left > 1:
        counts.append(left)
    return counts


def shards(streams, short_filter, residue, decay_rate, skip_gain):
    ctx_count = lax.axis_size("ctx")
    index = lax.axis_index("ctx")
    side = lax.axis_index("chan").astype(jnp.int32).reshape(1)
    toks, _, width = streams.shape
    half = toks // 2
    modes = residue.shape[1]
    rim = short_filter.shape[0] - 1
    tile = 256 if width % 256 == 0 else LANES
    steps = width // tile
    tiles = tile // LANES
    all_tiles = width // LANES

    x = jnp.transpose(streams, (1, 0, 2))
    rates = decay_rate.T
    weights = residue.T
    skip = skip_gain[None, :]
    x_kept, taps_kept, rates_kept = (
        pltpu.with_memory_space_constraint(a, pltpu.HBM) for a in (x, short_filter, rates)
    )
    params = pltpu.CompilerParams(vmem_limit_bytes=VMEM_LIMIT)
    in_hbm = pl.BlockSpec(memory_space=pltpu.HBM)
    strip = lambda *lead: pl.BlockSpec(lead + (tile,), lambda i, *_: (0,) * len(lead) + (i,))
    tall = lambda rows: pl.BlockSpec((tiles * rows, LANES), lambda i, *_: (i, 0))
    ends_spec = pl.BlockSpec((tiles, 2, modes * SUB, LANES), lambda i, *_: (i, 0, 0, 0))
    gate, ends, state, summary = pl.pallas_call(
        state_kernel,
        grid=(steps,),
        in_specs=[in_hbm, strip(rim + 1, 3), strip(modes)],
        out_specs=[tall(toks), ends_spec, strip(modes), strip(modes + PAIR)],
        out_shape=[
            jax.ShapeDtypeStruct((all_tiles * toks, LANES), F32),
            jax.ShapeDtypeStruct((all_tiles, 2, modes * SUB, LANES), F32),
            jax.ShapeDtypeStruct((modes, width), F32),
            jax.ShapeDtypeStruct((modes + PAIR, width), BF16),
        ],
        scratch_shapes=[
            pltpu.VMEM((steps, 2, toks, tile), BF16),
            pltpu.VMEM((steps, 2, PAIR, tile), BF16),
            pltpu.VMEM((2, toks + SUB, LANES), F32),
            pltpu.VMEM((modes, tile), F32),
            pltpu.VMEM((modes, tile), F32),
            pltpu.SemaphoreType.DMA((3, steps)),
        ],
        compiler_params=params,
        name="states",
    )(x_kept, taps_kept, rates_kept)

    def local(which, name):
        return pl.pallas_call(
            local_kernel,
            grid_spec=pltpu.PrefetchScalarGridSpec(
                num_scalar_prefetch=1,
                grid=(steps,),
                in_specs=[
                    in_hbm,
                    strip(rim + 1, 3),
                    tall(toks),
                    ends_spec,
                    strip(modes),
                    strip(modes),
                    strip(1),
                ],
                out_specs=[tall(half), tall(half)],
                scratch_shapes=[
                    pltpu.VMEM((steps, toks, tile), BF16),
                    pltpu.VMEM((half + SUB, LANES), F32),
                    pltpu.VMEM((modes * SUB, LANES), F32),
                    pltpu.VMEM((modes, tile), F32),
                    pltpu.VMEM((modes, tile), F32),
                    pltpu.VMEM((modes, tile), F32),
                    pltpu.SemaphoreType.DMA((steps,)),
                ],
            ),
            out_shape=[jax.ShapeDtypeStruct((all_tiles * half, LANES), F32)] * 2,
            compiler_params=params,
            name=name,
        )(which, x_kept, short_filter, gate, ends, weights, rates, skip)

    locals_sent = local(1 - side, "local_sent")
    locals_own = local(side, "local_own")

    ids = index.astype(jnp.int32).reshape(1)
    in_vmem = pl.BlockSpec(memory_space=pltpu.VMEM)
    prefix = jnp.zeros((modes, width), F32)
    past = jnp.zeros((SUB, width), F32)
    own = summary
    stride = 1
    counts = scan_counts(ctx_count)
    for level, count in enumerate(counts):
        last = level == len(counts) - 1
        if level == 2:
            summary, locals_sent = lax.optimization_barrier((summary, locals_sent))
        if level == 3:
            summary, locals_own = lax.optimization_barrier((summary, locals_own))
        arrived = []
        for k in range(1, count):
            route = []
            for i in range(ctx_count):
                j = i // stride % count
                route.append((i, i + ((j + k) % count - j) * stride))
            arrived.append(lax.ppermute(summary, "ctx", route))
        shapes = [
            jax.ShapeDtypeStruct((modes, width), F32),
            jax.ShapeDtypeStruct((SUB, width), F32),
        ]
        if not last:
            shapes += [
                jax.ShapeDtypeStruct((modes, width), F32),
                jax.ShapeDtypeStruct((modes + PAIR, width), BF16),
            ]

        def body(ids, *refs, stride=stride, count=count, last=last):
            join_kernel(ids, stride, count, toks, last, *refs)

        results = pl.pallas_call(
            body,
            in_specs=[pl.BlockSpec(memory_space=pltpu.SMEM)] + [in_vmem] * (5 + count),
            out_specs=[in_vmem] * len(shapes),
            out_shape=shapes,
            compiler_params=params,
            name=f"join_{level}",
        )(ids, short_filter, rates, state, prefix, past, summary, *arrived)
        prefix, past = results[:2]
        if not last:
            state, summary = results[2:]
        stride *= count

    def finish(which, column, columns, locals_, prefix, name):
        return pl.pallas_call(
            finish_kernel,
            grid_spec=pltpu.PrefetchScalarGridSpec(
                num_scalar_prefetch=1,
                grid=(steps,),
                in_specs=[
                    tall(half),
                    tall(half),
                    strip(modes),
                    strip(SUB),
                    strip(modes + PAIR),
                    strip(rim + 1, 3),
                    strip(modes),
                    strip(modes),
                    strip(1),
                ],
                out_specs=pl.BlockSpec((half, tile), lambda i, ids: (0, ids[1] * steps + i)),
                scratch_shapes=[
                    pltpu.VMEM((modes * SUB, LANES), F32),
                    pltpu.VMEM((half, LANES), F32),
                ],
            ),
            out_shape=jax.ShapeDtypeStruct((half, columns), BF16),
            compiler_params=params,
            name=name,
        )(
            jnp.concatenate([which, column]),
            *locals_,
            prefix,
            past,
            own,
            short_filter,
            weights,
            rates,
            skip,
        )

    sent = finish(1 - side, jnp.zeros_like(side), width, locals_sent, prefix, "finish_sent")
    far = lax.ppermute(sent, "chan", [(0, 1), (1, 0)])
    prefix, sent = lax.optimization_barrier((prefix, sent))
    held = finish(side, side, 2 * width, locals_own, prefix, "finish_own")
    return pl.pallas_call(
        place_kernel,
        grid_spec=pltpu.PrefetchScalarGridSpec(
            num_scalar_prefetch=1,
            grid=(1,),
            in_specs=[pl.BlockSpec(memory_space=pl.ANY)] * 2,
            out_specs=pl.BlockSpec(memory_space=pl.ANY),
            scratch_shapes=[pltpu.SemaphoreType.DMA(())],
        ),
        out_shape=jax.ShapeDtypeStruct((half, 2 * width), BF16),
        input_output_aliases={2: 0},
        compiler_params=params,
        name="place",
    )(1 - side, far, held)


def solution(mesh):
    return jax.shard_map(
        shards,
        mesh=mesh,
        in_specs=(
            P("ctx", None, "chan"),
            P(None, None, "chan"),
            P("chan", None),
            P("chan", None),
            P("chan"),
        ),
        out_specs=P(("ctx", "chan"), None),
        check_vma=False,
    )
```

time: 65.4 us -> 53.4 us (0.82)
  the two profiles are of different devices: /device:TPU:40 before, /device:TPU:32 now
where the time goes in v2:
time: 53.4 us; the launch traced here: 53.1 us
  starting transfers between devices  22.8 us (43%)
  Pallas kernels  16 us (30%)
  waiting for transfers between devices  14 us (26%)
    ppermute x10, starting transfers between devices, shards(): arrived.append(lax.ppermute(summary, 'ctx', route))  16.8 us
    ppermute x1, waiting for transfers between devices, shards(): far = lax.ppermute(sent, 'chan', [(0, 1), (1, 0)])  7.42 us
    ppermute x10, waiting for transfers between devices, shards(): arrived.append(lax.ppermute(summary, 'ctx', route))  6.55 us
    ppermute x1, starting transfers between devices, shards(): far = lax.ppermute(sent, 'chan', [(0, 1), (1, 0)])  6.03 us
    pallas_call x2, Pallas kernels, local(): pl.pallas_call(local_kernel, grid_spec=pltpu.PrefetchScalarGridSpec(num_s...  5.19 us
    pallas_call x1, Pallas kernels, shards(): pl.pallas_call(state_kernel, grid=(steps,), in_specs=[in_hbm, strip(rim +...  4.29 us
    pallas_call x2, Pallas kernels, finish(): pl.pallas_call(finish_kernel, grid_spec=pltpu.PrefetchScalarGridSpec(num_...  4.21 us
    pallas_call x4, Pallas kernels, shards(): pl.pallas_call(body, in_specs=[pl.BlockSpec(memory_space=pltpu.SMEM)] + [...  1.57 us
  transfers between devices with their start and end apart: 11, of which 8 were waited for; matrix products, arithmetic and copies ran while one was open for 0% of the time, Pallas kernels for 15%

profile of v2, /device:TPU:32, one launch (start us, length us, event | category | flops | bytes accessed | tf_op | source)
XLA Modules:
  0.0 53.1 jit_solution(711225094805098411)
XLA Ops:
  0.0 0.0 copy-start
  0.0 0.0 copy-start.1
  0.0 0.0 copy-start.2
  0.0 0.0 copy-start.3
  0.0 4.3 %states.1 = (f32[2048,128]{1,0:T(8,128)S(1)}, f32[8,2,128,128]{3,2,1,0:T(8,128)S(1)}, f32[16,1024]{1,0:T(8,128)S(1)}, bf16[32,1024]{1,0:T(8,128)(2,1)S(1)}) custom-call(bf16[3,256,1024]{2,1,0:T(8,128)(2,1)} %bitcast.23, f32[3,3,1024]{2,1,0:T(4,128)} %taps_ref.9, f32[16,1024]{1,0:T(8,128)} %bitcast.6), custom_call_target="tpu_custom_call" | custom-call | tf_op jit(solution)/shard_map/states/pallas_call | solution.py:384
  4.3 0.1 collective-permute-start
  4.4 1.2 %collective-permute-done.refs_6_ = bf16[32,1024]{1,0:T(8,128)(2,1)S(1)} collective-permute-done((bf16[32,1024]{1,0:T(8,128)(2,1)S(1)}, bf16[32,1024]{1,0:T(8,128)(2,1)S(1)}, u32[]{:S(2)}, u32[]{:S(2)}) %collective-permute-start) | collective-permute-done | bytes 65568 | tf_op jit(solution)/shard_map/ppermute | solution.py:460
  5.7 0.0 copy-done
  5.7 0.0 copy-done.1
  5.7 0.3 join_0.1
  6.0 2.0 %collective-permute-start.1 = (bf16[32,1024]{1,0:T(8,128)(2,1)S(1)}, bf16[32,1024]{1,0:T(8,128)(2,1)S(1)}, u32[]{:S(2)}, u32[]{:S(2)}) collective-permute-start(bf16[32,1024]{1,0:T(8,128)(2,1)S(1)} %get-tuple-element.39.refs_5_), channel_id=1, source_target_pairs={{0,4},{2,6},{4,8},{6,10},{8,12},{10,14},{12,0},{14,2},{16,20},{18,... | collective-permute-start | bytes 196616 | tf_op jit(solution)/shard_map/ppermute | solution.py:460
  8.0 2.3 %collective-permute-start.2 = (bf16[32,1024]{1,0:T(8,128)(2,1)S(1)}, bf16[32,1024]{1,0:T(8,128)(2,1)S(1)}, u32[]{:S(2)}, u32[]{:S(2)}) collective-permute-start(bf16[32,1024]{1,0:T(8,128)(2,1)S(1)} %get-tuple-element.39.refs_5_), channel_id=1, source_target_pairs={{0,8},{2,10},{4,12},{6,14},{8,0},{10,2},{12,4},{14,6},{16,24},{18,... | collective-permute-start | bytes 196616 | tf_op jit(solution)/shard_map/ppermute | solution.py:460
  10.2 1.1 %collective-permute-start.3 = (bf16[32,1024]{1,0:T(8,128)(2,1)S(1)}, bf16[32,1024]{1,0:T(8,128)(2,1)S(1)}, u32[]{:S(2)}, u32[]{:S(2)}) collective-permute-start(bf16[32,1024]{1,0:T(8,128)(2,1)S(1)} %get-tuple-element.39.refs_5_), channel_id=1, source_target_pairs={{0,12},{2,14},{4,0},{6,2},{8,4},{10,6},{12,8},{14,10},{16,28},{18,... | collective-permute-start | bytes 196616 | tf_op jit(solution)/shard_map/ppermute | solution.py:460
  11.3 0.0 copy-done.2
  11.3 0.0 copy-done.3
  11.4 2.6 %local_sent.1 = (f32[1024,128]{1,0:T(8,128)S(1)}, f32[1024,128]{1,0:T(8,128)S(1)}) custom-call(s32[1]{0:T(128)S(6)} %sub.2.part_id.ids, bf16[3,256,1024]{2,1,0:T(8,128)(2,1)} %bitcast.24, f32[3,3,1024]{2,1,0:T(4,128)S(1)} %copy-done.1, f32[2048,128]{1,0:T(8,128)S(1)} %get-tuple-element.41.gate_ref, f32[8,2,128,128]{3,2,1,0:T(8,128)S(1)} %get-tuple-element.42.ends_ref, ...), custom_call_target="tpu_custom_call" | custom-call | tf_op jit(solution)/shard_map/local_sent/pallas_call | solution.py:408
  14.0 0.0 collective-permute-done.1.refs_6_
  14.0 0.5 %collective-permute-done.2.refs_7_ = bf16[32,1024]{1,0:T(8,128)(2,1)S(1)} collective-permute-done((bf16[32,1024]{1,0:T(8,128)(2,1)S(1)}, bf16[32,1024]{1,0:T(8,128)(2,1)S(1)}, u32[]{:S(2)}, u32[]{:S(2)}) %collective-permute-start.2) | collective-permute-done | bytes 65568 | tf_op jit(solution)/shard_map/ppermute | solution.py:460
  14.5 1.7 %collective-permute-done.3.refs_8_ = bf16[32,1024]{1,0:T(8,128)(2,1)S(1)} collective-permute-done((bf16[32,1024]{1,0:T(8,128)(2,1)S(1)}, bf16[32,1024]{1,0:T(8,128)(2,1)S(1)}, u32[]{:S(2)}, u32[]{:S(2)}) %collective-permute-start.3) | collective-permute-done | bytes 65568 | tf_op jit(solution)/shard_map/ppermute | solution.py:460
  16.2 0.5 join_1.1
  16.7 1.3 %collective-permute-start.4 = (bf16[32,1024]{1,0:T(8,128)(2,1)S(1)}, bf16[32,1024]{1,0:T(8,128)(2,1)S(1)}, u32[]{:S(2)}, u32[]{:S(2)}) collective-permute-start(bf16[32,1024]{1,0:T(8,128)(2,1)S(1)} %get-tuple-element.50.refs_5_), channel_id=1, source_target_pairs={{0,16},{2,18},{4,20},{6,22},{8,24},{10,26},{12,28},{14,30},{16,32}... | collective-permute-start | bytes 196616 | tf_op jit(solution)/shard_map/ppermute | solution.py:460
  18.0 2.7 %collective-permute-start.5 = (bf16[32,1024]{1,0:T(8,128)(2,1)S(1)}, bf16[32,1024]{1,0:T(8,128)(2,1)S(1)}, u32[]{:S(2)}, u32[]{:S(2)}) collective-permute-start(bf16[32,1024]{1,0:T(8,128)(2,1)S(1)} %get-tuple-element.50.refs_5_), channel_id=1, source_target_pairs={{0,32},{2,34},{4,36},{6,38},{8,40},{10,42},{12,44},{14,46},{16,48}... | collective-permute-start | bytes 196616 | tf_op jit(solution)/shard_map/ppermute | solution.py:460
  20.7 1.4 %collective-permute-start.6 = (bf16[32,1024]{1,0:T(8,128)(2,1)S(1)}, bf16[32,1024]{1,0:T(8,128)(2,1)S(1)}, u32[]{:S(2)}, u32[]{:S(2)}) collective-permute-start(bf16[32,1024]{1,0:T(8,128)(2,1)S(1)} %get-tuple-element.50.refs_5_), channel_id=1, source_target_pairs={{0,48},{2,50},{4,52},{6,54},{8,56},{10,58},{12,60},{14,62},{16,0},... | collective-permute-start | bytes 196616 | tf_op jit(solution)/shard_map/ppermute | solution.py:460
  22.2 2.6 %local_own.1 = (f32[1024,128]{1,0:T(8,128)S(1)}, f32[1024,128]{1,0:T(8,128)S(1)}) custom-call(s32[1]{0:T(128)} %bitcast.part_id, bf16[3,256,1024]{2,1,0:T(8,128)(2,1)} %bitcast.25, f32[3,3,1024]{2,1,0:T(4,128)S(1)} %copy-done.1, f32[2048,128]{1,0:T(8,128)S(1)} %get-tuple-element.41.gate_ref, f32[8,2,128,128]{3,2,1,0:T(8,128)S(1)} %get-tuple-element.42.ends_ref, ...), custom_call_target="tpu_custom_call" | custom-call | tf_op jit(solution)/shard_map/local_own/pallas_call | solution.py:408
  24.7 0.0 collective-permute-done.4.refs_6_
  24.8 0.0 collective-permute-done.5.refs_7_
  24.8 0.2 collective-permute-done.6.refs_8_
  25.0 0.5 join_2.1
  25.5 1.7 %collective-permute-start.7 = (bf16[32,1024]{1,0:T(8,128)(2,1)S(1)}, bf16[32,1024]{1,0:T(8,128)(2,1)S(1)}, u32[]{:S(2)}, u32[]{:S(2)}) collective-permute-start(bf16[32,1024]{1,0:T(8,128)(2,1)S(1)} %get-tuple-element.57.refs_5_), channel_id=1, source_target_pairs={{0,64},{2,66},{4,68},{6,70},{8,72},{10,74},{12,76},{14,78},{16,80}... | collective-permute-start | bytes 196616 | tf_op jit(solution)/shard_map/ppermute | solution.py:460
  27.1 2.9 %collective-permute-start.8 = (bf16[32,1024]{1,0:T(8,128)(2,1)S(1)}, bf16[32,1024]{1,0:T(8,128)(2,1)S(1)}, u32[]{:S(2)}, u32[]{:S(2)}) collective-permute-start(bf16[32,1024]{1,0:T(8,128)(2,1)S(1)} %get-tuple-element.57.refs_5_), channel_id=1, source_target_pairs={{0,128},{2,130},{4,132},{6,134},{8,136},{10,138},{12,140},{14,142}... | collective-permute-start | bytes 196616 | tf_op jit(solution)/shard_map/ppermute | solution.py:460
  30.0 1.3 %collective-permute-start.9 = (bf16[32,1024]{1,0:T(8,128)(2,1)S(1)}, bf16[32,1024]{1,0:T(8,128)(2,1)S(1)}, u32[]{:S(2)}, u32[]{:S(2)}) collective-permute-start(bf16[32,1024]{1,0:T(8,128)(2,1)S(1)} %get-tuple-element.57.refs_5_), channel_id=1, source_target_pairs={{0,192},{2,194},{4,196},{6,198},{8,200},{10,202},{12,204},{14,206}... | collective-permute-start | bytes 196616 | tf_op jit(solution)/shard_map/ppermute | solution.py:460
  31.4 0.1 pad_add_fusion.ids
  31.4 0.3 collective-permute-done.7.refs_6_
  31.7 1.3 %collective-permute-done.8.refs_7_ = bf16[32,1024]{1,0:T(8,128)(2,1)S(1)} collective-permute-done((bf16[32,1024]{1,0:T(8,128)(2,1)S(1)}, bf16[32,1024]{1,0:T(8,128)(2,1)S(1)}, u32[]{:S(2)}, u32[]{:S(2)}) %collective-permute-start.8) | collective-permute-done | bytes 65568 | tf_op jit(solution)/shard_map/ppermute | solution.py:460
  33.0 1.3 %collective-permute-done.9.refs_8_ = bf16[32,1024]{1,0:T(8,128)(2,1)S(1)} collective-permute-done((bf16[32,1024]{1,0:T(8,128)(2,1)S(1)}, bf16[32,1024]{1,0:T(8,128)(2,1)S(1)}, u32[]{:S(2)}, u32[]{:S(2)}) %collective-permute-start.9) | collective-permute-done | bytes 65568 | tf_op jit(solution)/shard_map/ppermute | solution.py:460
  34.3 0.4 join_3.1
  34.7 1.6 %finish_sent.1 = bf16[128,1024]{1,0:T(8,128)(2,1)S(1)} custom-call(s32[2]{0:T(128)S(1)} %pad_add_fusion.ids, f32[1024,128]{1,0:T(8,128)S(1)} %get-tuple-element.45.query_ref, f32[1024,128]{1,0:T(8,128)S(1)} %get-tuple-element.46.local_ref, f32[16,1024]{1,0:T(8,128)S(1)} %get-tuple-element.62.prefix_ref, f32[8,1024]{1,0:T(8,128)S(1)} %get-tuple-element.59.past_ref, ...), custom_call_target="tpu_custom_call" | custom-call | tf_op jit(solution)/shard_map/finish_sent/pallas_call | solution.py:488
  36.3 6.0 %collective-permute-start.10 = (bf16[128,1024]{1,0:T(8,128)(2,1)S(1)}, bf16[128,1024]{1,0:T(8,128)(2,1)S(1)}, u32[]{:S(2)}, u32[]{:S(2)}) collective-permute-start(bf16[128,1024]{1,0:T(8,128)(2,1)S(1)} %finish_sent.1), channel_id=1, source_target_pairs={{0,1},{1,0},{2,3},{3,2},{4,5},{5,4},{6,7},{7,6},{8,9},{9,8},{10,11... | collective-permute-start | bytes 786440 | tf_op jit(solution)/shard_map/ppermute | solution.py:526
  42.3 0.1 pad_add_fusion.1.ids
  42.4 2.6 %finish_own.1.held_ref = bf16[128,2048]{1,0:T(8,128)(2,1)} custom-call(s32[2]{0:T(128)S(1)} %pad_add_fusion.1.ids, f32[1024,128]{1,0:T(8,128)S(1)} %get-tuple-element.60.query_ref, f32[1024,128]{1,0:T(8,128)S(1)} %get-tuple-element.61.local_ref, f32[16,1024]{1,0:T(8,128)S(1)} %get-tuple-element.62.prefix_ref, f32[8,1024]{1,0:T(8,128)S(1)} %get-tuple-element.59.past_ref, ...), custom_call_target="tpu_custom_call" | custom-call | tf_op jit(solution)/shard_map/finish_own/pallas_call | solution.py:488
  45.0 7.4 %collective-permute-done.10.far_ref = bf16[128,1024]{1,0:T(8,128)(2,1)S(1)} collective-permute-done((bf16[128,1024]{1,0:T(8,128)(2,1)S(1)}, bf16[128,1024]{1,0:T(8,128)(2,1)S(1)}, u32[]{:S(2)}, u32[]{:S(2)}) %collective-permute-start.10) | collective-permute-done | bytes 262176 | tf_op jit(solution)/shard_map/ppermute | solution.py:526
  52.4 0.7 %place.1 = bf16[128,2048]{1,0:T(8,128)(2,1)} custom-call(s32[1]{0:T(128)S(6)} %sub.2.part_id.ids, bf16[128,1024]{1,0:T(8,128)(2,1)S(1)} %collective-permute-done.10.far_ref, bf16[128,2048]{1,0:T(8,128)(2,1)} %finish_own.1.held_ref), custom_call_target="tpu_custom_call", output_to_operand_aliasing={{}: (2, {})} | custom-call | tf_op jit(solution)/shard_map/place/pallas_call | solution.py:529
  (2 shorter events, 0.0 us)
Async XLA Ops:
  0.0 5.7 %copy-start = (f32[1024,16]{0,1:T(8,128)S(1)}, f32[1024,16]{0,1:T(8,128)}, u32[]{:S(2)}) copy-start(f32[1024,16]{0,1:T(8,128)} %param.8) | copy-start | bytes 196612
  0.0 5.7 %copy-start.1 = (f32[3,3,1024]{2,1,0:T(4,128)S(1)}, f32[3,3,1024]{2,1,0:T(4,128)}, u32[]{:S(2)}) copy-start(f32[3,3,1024]{2,1,0:T(4,128)} %taps_ref.9) | copy-start | bytes 110596
  0.0 11.3 %copy-start.2 = (f32[1024,16]{0,1:T(8,128)S(1)}, f32[1024,16]{0,1:T(8,128)}, u32[]{:S(2)}) copy-start(f32[1024,16]{0,1:T(8,128)} %param.7) | copy-start | bytes 196612
  0.0 11.3 %copy-start.3 = (f32[1024]{0:T(1024)S(1)}, f32[1024]{0:T(1024)}, u32[]{:S(2)}) copy-start(f32[1024]{0:T(1024)} %param.9) | copy-start | bytes 12292
  4.3 1.3 %collective-permute-start = (bf16[32,1024]{1,0:T(8,128)(2,1)S(1)}, bf16[32,1024]{1,0:T(8,128)(2,1)S(1)}, u32[]{:S(2)}, u32[]{:S(2)}) collective-permute-start(bf16[32,1024]{1,0:T(8,128)(2,1)S(1)} %get-tuple-element.35.refs_5_.sum_ref), channel_id=1, source_target_pairs={{0,2},{2,0},{4,6},{6,4},{8,10},{10,8},{12,14},{14,12},{16,18},{18,... | collective-permute-start | bytes 196616 | tf_op jit(solution)/shard_map/ppermute | solution.py:460
  6.0 8.0 %collective-permute-start.1 = (bf16[32,1024]{1,0:T(8,128)(2,1)S(1)}, bf16[32,1024]{1,0:T(8,128)(2,1)S(1)}, u32[]{:S(2)}, u32[]{:S(2)}) collective-permute-start(bf16[32,1024]{1,0:T(8,128)(2,1)S(1)} %get-tuple-element.39.refs_5_), channel_id=1, source_target_pairs={{0,4},{2,6},{4,8},{6,10},{8,12},{10,14},{12,0},{14,2},{16,20},{18,... | collective-permute-start | bytes 196616 | tf_op jit(solution)/shard_map/ppermute | solution.py:460
  8.0 6.5 %collective-permute-start.2 = (bf16[32,1024]{1,0:T(8,128)(2,1)S(1)}, bf16[32,1024]{1,0:T(8,128)(2,1)S(1)}, u32[]{:S(2)}, u32[]{:S(2)}) collective-permute-start(bf16[32,1024]{1,0:T(8,128)(2,1)S(1)} %get-tuple-element.39.refs_5_), channel_id=1, source_target_pairs={{0,8},{2,10},{4,12},{6,14},{8,0},{10,2},{12,4},{14,6},{16,24},{18,... | collective-permute-start | bytes 196616 | tf_op jit(solution)/shard_map/ppermute | solution.py:460
  10.2 6.0 %collective-permute-start.3 = (bf16[32,1024]{1,0:T(8,128)(2,1)S(1)}, bf16[32,1024]{1,0:T(8,128)(2,1)S(1)}, u32[]{:S(2)}, u32[]{:S(2)}) collective-permute-start(bf16[32,1024]{1,0:T(8,128)(2,1)S(1)} %get-tuple-element.39.refs_5_), channel_id=1, source_target_pairs={{0,12},{2,14},{4,0},{6,2},{8,4},{10,6},{12,8},{14,10},{16,28},{18,... | collective-permute-start | bytes 196616 | tf_op jit(solution)/shard_map/ppermute | solution.py:460
  16.7 8.0 %collective-permute-start.4 = (bf16[32,1024]{1,0:T(8,128)(2,1)S(1)}, bf16[32,1024]{1,0:T(8,128)(2,1)S(1)}, u32[]{:S(2)}, u32[]{:S(2)}) collective-permute-start(bf16[32,1024]{1,0:T(8,128)(2,1)S(1)} %get-tuple-element.50.refs_5_), channel_id=1, source_target_pairs={{0,16},{2,18},{4,20},{6,22},{8,24},{10,26},{12,28},{14,30},{16,32}... | collective-permute-start | bytes 196616 | tf_op jit(solution)/shard_map/ppermute | solution.py:460
  18.0 6.8 %collective-permute-start.5 = (bf16[32,1024]{1,0:T(8,128)(2,1)S(1)}, bf16[32,1024]{1,0:T(8,128)(2,1)S(1)}, u32[]{:S(2)}, u32[]{:S(2)}) collective-permute-start(bf16[32,1024]{1,0:T(8,128)(2,1)S(1)} %get-tuple-element.50.refs_5_), channel_id=1, source_target_pairs={{0,32},{2,34},{4,36},{6,38},{8,40},{10,42},{12,44},{14,46},{16,48}... | collective-permute-start | bytes 196616 | tf_op jit(solution)/shard_map/ppermute | solution.py:460
  20.7 4.3 %collective-permute-start.6 = (bf16[32,1024]{1,0:T(8,128)(2,1)S(1)}, bf16[32,1024]{1,0:T(8,128)(2,1)S(1)}, u32[]{:S(2)}, u32[]{:S(2)}) collective-permute-start(bf16[32,1024]{1,0:T(8,128)(2,1)S(1)} %get-tuple-element.50.refs_5_), channel_id=1, source_target_pairs={{0,48},{2,50},{4,52},{6,54},{8,56},{10,58},{12,60},{14,62},{16,0},... | collective-permute-start | bytes 196616 | tf_op jit(solution)/shard_map/ppermute | solution.py:460
  25.5 6.2 %collective-permute-start.7 = (bf16[32,1024]{1,0:T(8,128)(2,1)S(1)}, bf16[32,1024]{1,0:T(8,128)(2,1)S(1)}, u32[]{:S(2)}, u32[]{:S(2)}) collective-permute-start(bf16[32,1024]{1,0:T(8,128)(2,1)S(1)} %get-tuple-element.57.refs_5_), channel_id=1, source_target_pairs={{0,64},{2,66},{4,68},{6,70},{8,72},{10,74},{12,76},{14,78},{16,80}... | collective-permute-start | bytes 196616 | tf_op jit(solution)/shard_map/ppermute | solution.py:460
  27.1 5.8 %collective-permute-start.8 = (bf16[32,1024]{1,0:T(8,128)(2,1)S(1)}, bf16[32,1024]{1,0:T(8,128)(2,1)S(1)}, u32[]{:S(2)}, u32[]{:S(2)}) collective-permute-start(bf16[32,1024]{1,0:T(8,128)(2,1)S(1)} %get-tuple-element.57.refs_5_), channel_id=1, source_target_pairs={{0,128},{2,130},{4,132},{6,134},{8,136},{10,138},{12,140},{14,142}... | collective-permute-start | bytes 196616 | tf_op jit(solution)/shard_map/ppermute | solution.py:460
  30.0 4.3 %collective-permute-start.9 = (bf16[32,1024]{1,0:T(8,128)(2,1)S(1)}, bf16[32,1024]{1,0:T(8,128)(2,1)S(1)}, u32[]{:S(2)}, u32[]{:S(2)}) collective-permute-start(bf16[32,1024]{1,0:T(8,128)(2,1)S(1)} %get-tuple-element.57.refs_5_), channel_id=1, source_target_pairs={{0,192},{2,194},{4,196},{6,198},{8,200},{10,202},{12,204},{14,206}... | collective-permute-start | bytes 196616 | tf_op jit(solution)/shard_map/ppermute | solution.py:460
  36.3 16.1 %collective-permute-start.10 = (bf16[128,1024]{1,0:T(8,128)(2,1)S(1)}, bf16[128,1024]{1,0:T(8,128)(2,1)S(1)}, u32[]{:S(2)}, u32[]{:S(2)}) collective-permute-start(bf16[128,1024]{1,0:T(8,128)(2,1)S(1)} %finish_sent.1), channel_id=1, source_target_pairs={{0,1},{1,0},{2,3},{3,2},{4,5},{5,4},{6,7},{7,6},{8,9},{9,8},{10,11... | collective-permute-start | bytes 786440 | tf_op jit(solution)/shard_map/ppermute | solution.py:526

commit v3 on v2

--- a/solution.py
+++ b/solution.py
@@ -155,6 +155,7 @@
 def join_kernel(ids, stride, count, toks, last, *refs):
     taps_ref, rate_ref, state_ref, prefix_ref, past_ref, own_ref = refs[:6]
     near = (own_ref,) + refs[6 : 5 + count]
+    shared = count == 4 and stride % 2 == 0
     outs = refs[5 + count :]
     prefix_out, past_out = outs[:2]
     modes, width = rate_ref.shape
@@ -169,9 +170,13 @@
         rates = rate_ref[:, cols]
         span = rates * float(toks)
         taps = [[taps_ref[j, s : s + 1, cols] for j in range(3)] for s in (1, 2)]
-        extra = [ref[modes:, cols].astype(F32) for ref in near]
+        full = [ref[:, cols].astype(F32) for ref in near]
+        if shared:
+            odd = lax.rem(index, 2) == 1
+            full[1], full[3] = jnp.where(odd, full[3], full[1]), jnp.where(odd, full[1], full[3])
+        extra = [value[modes:] for value in full]
         firsts = [(e[0:2], e[2:4]) for e in extra]
-        states = [state_ref[:, cols]] + [ref[:modes, cols].astype(F32) for ref in near[1:]]
+        states = [state_ref[:, cols]] + [value[:modes] for value in full[1:]]
         first_keep = jnp.exp(-rates * float(toks - 1))
         second_keep = jnp.exp(-rates * float(toks - 2))
         rest = jnp.exp(-span * float(stride - 1))
@@ -345,6 +350,25 @@
     copy.wait()
 
 
+def exchange(summary, blocks, index, stride, count):
+    def route(hop):
+        pairs = []
+        for i in range(blocks):
+            j = i // stride % count
+            pairs.append((i, i + ((j + hop(i)) % count - j) * stride))
+        return pairs
+
+    def send(value, hop):
+        return lax.ppermute(value, "ctx", route(hop))
+
+    if count != 4 or stride % 2:
+        return [send(summary, lambda i, k=k: k) for k in range(1, count)]
+    beside = send(summary, lambda i: 3 if i % 2 else 1)
+    across = send(summary, lambda i: 2)
+    other = lax.ppermute(beside, "ctx", [(i, i ^ 1) for i in range(blocks)])
+    return [beside, across, other]
+
+
 def scan_counts(blocks):
     counts = [2] if blocks % 2 == 0 else []
     left = blocks // 2 if counts else blocks
@@ -404,7 +428,7 @@
         name="states",
     )(x_kept, taps_kept, rates_kept)
 
-    def local(which, name):
+    def local(which, gate, name):
         return pl.pallas_call(
             local_kernel,
             grid_spec=pltpu.PrefetchScalarGridSpec(
@@ -435,8 +459,7 @@
             name=name,
         )(which, x_kept, short_filter, gate, ends, weights, rates, skip)
 
-    locals_sent = local(1 - side, "local_sent")
-    locals_own = local(side, "local_own")
+    locals_sent = local(1 - side, gate, "local_sent")
 
     ids = index.astype(jnp.int32).reshape(1)
     in_vmem = pl.BlockSpec(memory_space=pltpu.VMEM)
@@ -449,15 +472,7 @@
         last = level == len(counts) - 1
         if level == 2:
             summary, locals_sent = lax.optimization_barrier((summary, locals_sent))
-        if level == 3:
-            summary, locals_own = lax.optimization_barrier((summary, locals_own))
-        arrived = []
-        for k in range(1, count):
-            route = []
-            for i in range(ctx_count):
-                j = i // stride % count
-                route.append((i, i + ((j + k) % count - j) * stride))
-            arrived.append(lax.ppermute(summary, "ctx", route))
+        arrived = exchange(summary, ctx_count, index, stride, count)
         shapes = [
             jax.ShapeDtypeStruct((modes, width), F32),
             jax.ShapeDtypeStruct((SUB, width), F32),
@@ -524,7 +539,8 @@
 
     sent = finish(1 - side, jnp.zeros_like(side), width, locals_sent, prefix, "finish_sent")
     far = lax.ppermute(sent, "chan", [(0, 1), (1, 0)])
-    prefix, sent = lax.optimization_barrier((prefix, sent))
+    prefix, gate, sent = lax.optimization_barrier((prefix, gate, sent))
+    locals_own = local(side, gate, "local_own")
     held = finish(side, side, 2 * width, locals_own, prefix, "finish_own")
     return pl.pallas_call(
         place_kernel,

time: 53.4 us -> 51.9 us (0.972)
  the two profiles are of different devices: /device:TPU:32 before, /device:TPU:96 now
where the time goes in v3:
time: 51.9 us; the launch traced here: 51.6 us
  waiting for transfers between devices  19.4 us (37%)
  Pallas kernels  16.1 us (31%)
  starting transfers between devices  15.8 us (30%)
    ppermute x7, waiting for transfers between devices, send(): return lax.ppermute(value, 'ctx', route(hop))  11.8 us
    ppermute x7, starting transfers between devices, send(): return lax.ppermute(value, 'ctx', route(hop))  10.7 us
    ppermute x1, waiting for transfers between devices, shards(): far = lax.ppermute(sent, 'chan', [(0, 1), (1, 0)])  7.57 us
    pallas_call x2, Pallas kernels, local(): pl.pallas_call(local_kernel, grid_spec=pltpu.PrefetchScalarGridSpec(num_s...  5.22 us
    ppermute x1, starting transfers between devices, shards(): far = lax.ppermute(sent, 'chan', [(0, 1), (1, 0)])  5.13 us
    pallas_call x1, Pallas kernels, shards(): pl.pallas_call(state_kernel, grid=(steps,), in_specs=[in_hbm, strip(rim +...  4.29 us
    pallas_call x2, Pallas kernels, finish(): pl.pallas_call(finish_kernel, grid_spec=pltpu.PrefetchScalarGridSpec(num_...  4.2 us
    pallas_call x4, Pallas kernels, shards(): pl.pallas_call(body, in_specs=[pl.BlockSpec(memory_space=pltpu.SMEM)] + [...  1.66 us
  transfers between devices with their start and end apart: 11, of which 7 were waited for; matrix products, arithmetic and copies ran while one was open for 0% of the time, Pallas kernels for 15%

profile of v3, /device:TPU:96, one launch (start us, length us, event | category | flops | bytes accessed | tf_op | source)
XLA Modules:
  0.0 51.6 jit_solution(9556547042854424173)
XLA Ops:
  0.0 0.0 copy-start
  0.0 0.0 copy-start.1
  0.0 0.0 copy-start.2
  0.0 0.0 copy-start.3
  0.0 4.3 %states.1 = (f32[2048,128]{1,0:T(8,128)S(1)}, f32[8,2,128,128]{3,2,1,0:T(8,128)S(1)}, f32[16,1024]{1,0:T(8,128)S(1)}, bf16[32,1024]{1,0:T(8,128)(2,1)S(1)}) custom-call(bf16[3,256,1024]{2,1,0:T(8,128)(2,1)} %bitcast.23, f32[3,3,1024]{2,1,0:T(4,128)} %taps_ref.9, f32[16,1024]{1,0:T(8,128)} %bitcast.6), custom_call_target="tpu_custom_call" | custom-call | tf_op jit(solution)/shard_map/states/pallas_call | solution.py:408
  4.3 0.1 collective-permute-start
  4.4 1.2 %collective-permute-done.refs_6_ = bf16[32,1024]{1,0:T(8,128)(2,1)S(1)} collective-permute-done((bf16[32,1024]{1,0:T(8,128)(2,1)S(1)}, bf16[32,1024]{1,0:T(8,128)(2,1)S(1)}, u32[]{:S(2)}, u32[]{:S(2)}) %collective-permute-start) | collective-permute-done | bytes 65568 | tf_op jit(solution)/shard_map/ppermute | solution.py:362
  5.7 0.0 copy-done
  5.7 0.0 copy-done.1
  5.7 0.3 join_0.1
  6.0 1.0 %collective-permute-start.1 = (bf16[32,1024]{1,0:T(8,128)(2,1)S(1)}, bf16[32,1024]{1,0:T(8,128)(2,1)S(1)}, u32[]{:S(2)}, u32[]{:S(2)}) collective-permute-start(bf16[32,1024]{1,0:T(8,128)(2,1)S(1)} %get-tuple-element.37.refs_5_), channel_id=1, source_target_pairs={{0,4},{2,14},{4,8},{6,2},{8,12},{10,6},{12,0},{14,10},{16,20},{18,... | collective-permute-start | bytes 196616 | tf_op jit(solution)/shard_map/ppermute | solution.py:362
  7.0 0.7 %collective-permute-start.2 = (bf16[32,1024]{1,0:T(8,128)(2,1)S(1)}, bf16[32,1024]{1,0:T(8,128)(2,1)S(1)}, u32[]{:S(2)}, u32[]{:S(2)}) collective-permute-start(bf16[32,1024]{1,0:T(8,128)(2,1)S(1)} %get-tuple-element.37.refs_5_), channel_id=1, source_target_pairs={{0,8},{2,10},{4,12},{6,14},{8,0},{10,2},{12,4},{14,6},{16,24},{18,... | collective-permute-start | bytes 196616 | tf_op jit(solution)/shard_map/ppermute | solution.py:362
  7.6 4.1 %collective-permute-done.1.refs_6_ = bf16[32,1024]{1,0:T(8,128)(2,1)S(1)} collective-permute-done((bf16[32,1024]{1,0:T(8,128)(2,1)S(1)}, bf16[32,1024]{1,0:T(8,128)(2,1)S(1)}, u32[]{:S(2)}, u32[]{:S(2)}) %collective-permute-start.1) | collective-permute-done | bytes 65568 | tf_op jit(solution)/shard_map/ppermute | solution.py:362
  11.7 0.0 collective-permute-start.3
  11.7 0.0 copy-done.2
  11.7 0.0 copy-done.3
  11.8 2.6 %local_sent.1 = (f32[1024,128]{1,0:T(8,128)S(1)}, f32[1024,128]{1,0:T(8,128)S(1)}) custom-call(s32[1]{0:T(128)S(6)} %sub.2.part_id.ids, bf16[3,256,1024]{2,1,0:T(8,128)(2,1)} %bitcast.24, f32[3,3,1024]{2,1,0:T(4,128)S(1)} %copy-done.1, f32[2048,128]{1,0:T(8,128)S(1)} %get-tuple-element.55.gate_ref, f32[8,2,128,128]{3,2,1,0:T(8,128)S(1)} %get-tuple-element.40.ends_ref, ...), custom_call_target="tpu_custom_call" | custom-call | tf_op jit(solution)/shard_map/local_sent/pallas_call | solution.py:432
  14.4 0.0 collective-permute-done.2.refs_7_
  14.4 0.0 collective-permute-done.3.refs_8_
  14.4 0.5 join_1.1
  14.9 1.6 %collective-permute-start.4 = (bf16[32,1024]{1,0:T(8,128)(2,1)S(1)}, bf16[32,1024]{1,0:T(8,128)(2,1)S(1)}, u32[]{:S(2)}, u32[]{:S(2)}) collective-permute-start(bf16[32,1024]{1,0:T(8,128)(2,1)S(1)} %get-tuple-element.48.refs_5_), channel_id=1, source_target_pairs={{0,16},{2,50},{4,20},{6,54},{8,24},{10,58},{12,28},{14,62},{16,32}... | collective-permute-start | bytes 196616 | tf_op jit(solution)/shard_map/ppermute | solution.py:362
  16.6 2.7 %collective-permute-start.5 = (bf16[32,1024]{1,0:T(8,128)(2,1)S(1)}, bf16[32,1024]{1,0:T(8,128)(2,1)S(1)}, u32[]{:S(2)}, u32[]{:S(2)}) collective-permute-start(bf16[32,1024]{1,0:T(8,128)(2,1)S(1)} %get-tuple-element.48.refs_5_), channel_id=1, source_target_pairs={{0,32},{2,34},{4,36},{6,38},{8,40},{10,42},{12,44},{14,46},{16,48}... | collective-permute-start | bytes 196616 | tf_op jit(solution)/shard_map/ppermute | solution.py:362
  19.3 1.2 %collective-permute-done.4.refs_6_ = bf16[32,1024]{1,0:T(8,128)(2,1)S(1)} collective-permute-done((bf16[32,1024]{1,0:T(8,128)(2,1)S(1)}, bf16[32,1024]{1,0:T(8,128)(2,1)S(1)}, u32[]{:S(2)}, u32[]{:S(2)}) %collective-permute-start.4) | collective-permute-done | bytes 65568 | tf_op jit(solution)/shard_map/ppermute | solution.py:362
  20.5 0.0 collective-permute-start.6
  20.5 2.1 %collective-permute-done.5.refs_7_ = bf16[32,1024]{1,0:T(8,128)(2,1)S(1)} collective-permute-done((bf16[32,1024]{1,0:T(8,128)(2,1)S(1)}, bf16[32,1024]{1,0:T(8,128)(2,1)S(1)}, u32[]{:S(2)}, u32[]{:S(2)}) %collective-permute-start.5) | collective-permute-done | bytes 65568 | tf_op jit(solution)/shard_map/ppermute | solution.py:362
  22.6 0.0 collective-permute-done.6.refs_8_
  22.6 0.5 join_2.1
  23.1 1.7 %collective-permute-start.7 = (bf16[32,1024]{1,0:T(8,128)(2,1)S(1)}, bf16[32,1024]{1,0:T(8,128)(2,1)S(1)}, u32[]{:S(2)}, u32[]{:S(2)}) collective-permute-start(bf16[32,1024]{1,0:T(8,128)(2,1)S(1)} %get-tuple-element.52.refs_5_), channel_id=1, source_target_pairs={{0,64},{2,194},{4,68},{6,198},{8,72},{10,202},{12,76},{14,206},{16... | collective-permute-start | bytes 196616 | tf_op jit(solution)/shard_map/ppermute | solution.py:362
  24.7 2.9 %collective-permute-start.8 = (bf16[32,1024]{1,0:T(8,128)(2,1)S(1)}, bf16[32,1024]{1,0:T(8,128)(2,1)S(1)}, u32[]{:S(2)}, u32[]{:S(2)}) collective-permute-start(bf16[32,1024]{1,0:T(8,128)(2,1)S(1)} %get-tuple-element.52.refs_5_), channel_id=1, source_target_pairs={{0,128},{2,130},{4,132},{6,134},{8,136},{10,138},{12,140},{14,142}... | collective-permute-start | bytes 196616 | tf_op jit(solution)/shard_map/ppermute | solution.py:362
  27.6 1.0 %collective-permute-done.7.refs_6_ = bf16[32,1024]{1,0:T(8,128)(2,1)S(1)} collective-permute-done((bf16[32,1024]{1,0:T(8,128)(2,1)S(1)}, bf16[32,1024]{1,0:T(8,128)(2,1)S(1)}, u32[]{:S(2)}, u32[]{:S(2)}) %collective-permute-start.7) | collective-permute-done | bytes 65568 | tf_op jit(solution)/shard_map/ppermute | solution.py:362
  28.6 0.0 collective-permute-start.9
  28.6 0.1 pad_add_fusion.ids
  28.7 2.2 %collective-permute-done.8.refs_7_ = bf16[32,1024]{1,0:T(8,128)(2,1)S(1)} collective-permute-done((bf16[32,1024]{1,0:T(8,128)(2,1)S(1)}, bf16[32,1024]{1,0:T(8,128)(2,1)S(1)}, u32[]{:S(2)}, u32[]{:S(2)}) %collective-permute-start.8) | collective-permute-done | bytes 65568 | tf_op jit(solution)/shard_map/ppermute | solution.py:362
  30.9 0.0 collective-permute-done.9.refs_8_
  30.9 0.4 join_3.1
  31.3 1.6 %finish_sent.1 = bf16[128,1024]{1,0:T(8,128)(2,1)S(1)} custom-call(s32[2]{0:T(128)S(1)} %pad_add_fusion.ids, f32[1024,128]{1,0:T(8,128)S(1)} %get-tuple-element.43.query_ref, f32[1024,128]{1,0:T(8,128)S(1)} %get-tuple-element.44.local_ref, f32[16,1024]{1,0:T(8,128)S(1)} %get-tuple-element.58.prefix_ref, f32[8,1024]{1,0:T(8,128)S(1)} %get-tuple-element.54.past_ref, ...), custom_call_target="tpu_custom_call" | custom-call | tf_op jit(solution)/shard_map/finish_sent/pallas_call | solution.py:503
  33.0 5.1 %collective-permute-start.10 = (bf16[128,1024]{1,0:T(8,128)(2,1)S(1)}, bf16[128,1024]{1,0:T(8,128)(2,1)S(1)}, u32[]{:S(2)}, u32[]{:S(2)}) collective-permute-start(bf16[128,1024]{1,0:T(8,128)(2,1)S(1)} %finish_sent.1), channel_id=1, source_target_pairs={{0,1},{1,0},{2,3},{3,2},{4,5},{5,4},{6,7},{7,6},{8,9},{9,8},{10,11... | collective-permute-start | bytes 786440 | tf_op jit(solution)/shard_map/ppermute | solution.py:541
  38.1 0.1 pad_add_fusion.1.ids
  38.2 2.6 %local_own.1 = (f32[1024,128]{1,0:T(8,128)S(1)}, f32[1024,128]{1,0:T(8,128)S(1)}) custom-call(s32[1]{0:T(128)} %bitcast.part_id, bf16[3,256,1024]{2,1,0:T(8,128)(2,1)} %bitcast.25, f32[3,3,1024]{2,1,0:T(4,128)S(1)} %copy-done.1, f32[2048,128]{1,0:T(8,128)S(1)} %get-tuple-element.55.gate_ref, f32[8,2,128,128]{3,2,1,0:T(8,128)S(1)} %get-tuple-element.40.ends_ref, ...), custom_call_target="tpu_custom_call" | custom-call | tf_op jit(solution)/shard_map/local_own/pallas_call | solution.py:432
  40.8 2.6 %finish_own.1.held_ref = bf16[128,2048]{1,0:T(8,128)(2,1)} custom-call(s32[2]{0:T(128)S(1)} %pad_add_fusion.1.ids, f32[1024,128]{1,0:T(8,128)S(1)} %get-tuple-element.56.query_ref, f32[1024,128]{1,0:T(8,128)S(1)} %get-tuple-element.57.local_ref, f32[16,1024]{1,0:T(8,128)S(1)} %get-tuple-element.58.prefix_ref, f32[8,1024]{1,0:T(8,128)S(1)} %get-tuple-element.54.past_ref, ...), custom_call_target="tpu_custom_call" | custom-call | tf_op jit(solution)/shard_map/finish_own/pallas_call | solution.py:503
  43.3 7.6 %collective-permute-done.10.far_ref = bf16[128,1024]{1,0:T(8,128)(2,1)S(1)} collective-permute-done((bf16[128,1024]{1,0:T(8,128)(2,1)S(1)}, bf16[128,1024]{1,0:T(8,128)(2,1)S(1)}, u32[]{:S(2)}, u32[]{:S(2)}) %collective-permute-start.10) | collective-permute-done | bytes 262176 | tf_op jit(solution)/shard_map/ppermute | solution.py:541
  50.9 0.7 %place.1 = bf16[128,2048]{1,0:T(8,128)(2,1)} custom-call(s32[1]{0:T(128)S(6)} %sub.2.part_id.ids, bf16[128,1024]{1,0:T(8,128)(2,1)S(1)} %collective-permute-done.10.far_ref, bf16[128,2048]{1,0:T(8,128)(2,1)} %finish_own.1.held_ref), custom_call_target="tpu_custom_call", output_to_operand_aliasing={{}: (2, {})} | custom-call | tf_op jit(solution)/shard_map/place/pallas_call | solution.py:545
  (2 shorter events, 0.0 us)
Async XLA Ops:
  0.0 5.7 %copy-start = (f32[1024,16]{0,1:T(8,128)S(1)}, f32[1024,16]{0,1:T(8,128)}, u32[]{:S(2)}) copy-start(f32[1024,16]{0,1:T(8,128)} %param.8) | copy-start | bytes 196612
  0.0 5.7 %copy-start.1 = (f32[3,3,1024]{2,1,0:T(4,128)S(1)}, f32[3,3,1024]{2,1,0:T(4,128)}, u32[]{:S(2)}) copy-start(f32[3,3,1024]{2,1,0:T(4,128)} %taps_ref.9) | copy-start | bytes 110596
  0.0 11.7 %copy-start.2 = (f32[1024,16]{0,1:T(8,128)S(1)}, f32[1024,16]{0,1:T(8,128)}, u32[]{:S(2)}) copy-start(f32[1024,16]{0,1:T(8,128)} %param.7) | copy-start | bytes 196612
  0.0 11.7 %copy-start.3 = (f32[1024]{0:T(1024)S(1)}, f32[1024]{0:T(1024)}, u32[]{:S(2)}) copy-start(f32[1024]{0:T(1024)} %param.9) | copy-start | bytes 12292
  4.3 1.3 %collective-permute-start = (bf16[32,1024]{1,0:T(8,128)(2,1)S(1)}, bf16[32,1024]{1,0:T(8,128)(2,1)S(1)}, u32[]{:S(2)}, u32[]{:S(2)}) collective-permute-start(bf16[32,1024]{1,0:T(8,128)(2,1)S(1)} %get-tuple-element.33.refs_5_.sum_ref), channel_id=1, source_target_pairs={{0,2},{2,0},{4,6},{6,4},{8,10},{10,8},{12,14},{14,12},{16,18},{18,... | collective-permute-start | bytes 196616 | tf_op jit(solution)/shard_map/ppermute | solution.py:362
  6.0 5.8 %collective-permute-start.1 = (bf16[32,1024]{1,0:T(8,128)(2,1)S(1)}, bf16[32,1024]{1,0:T(8,128)(2,1)S(1)}, u32[]{:S(2)}, u32[]{:S(2)}) collective-permute-start(bf16[32,1024]{1,0:T(8,128)(2,1)S(1)} %get-tuple-element.37.refs_5_), channel_id=1, source_target_pairs={{0,4},{2,14},{4,8},{6,2},{8,12},{10,6},{12,0},{14,10},{16,20},{18,... | collective-permute-start | bytes 196616 | tf_op jit(solution)/shard_map/ppermute | solution.py:362
  7.0 7.4 %collective-permute-start.2 = (bf16[32,1024]{1,0:T(8,128)(2,1)S(1)}, bf16[32,1024]{1,0:T(8,128)(2,1)S(1)}, u32[]{:S(2)}, u32[]{:S(2)}) collective-permute-start(bf16[32,1024]{1,0:T(8,128)(2,1)S(1)} %get-tuple-element.37.refs_5_), channel_id=1, source_target_pairs={{0,8},{2,10},{4,12},{6,14},{8,0},{10,2},{12,4},{14,6},{16,24},{18,... | collective-permute-start | bytes 196616 | tf_op jit(solution)/shard_map/ppermute | solution.py:362
  11.7 2.7 %collective-permute-start.3 = (bf16[32,1024]{1,0:T(8,128)(2,1)S(1)}, bf16[32,1024]{1,0:T(8,128)(2,1)S(1)}, u32[]{:S(2)}, u32[]{:S(2)}) collective-permute-start(bf16[32,1024]{1,0:T(8,128)(2,1)S(1)} %collective-permute-done.1.refs_6_), channel_id=1, source_target_pairs={{0,2},{2,0},{4,6},{6,4},{8,10},{10,8},{12,14},{14,12},{16,18},{18,... | collective-permute-start | bytes 196616 | tf_op jit(solution)/shard_map/ppermute | solution.py:368
  14.9 5.6 %collective-permute-start.4 = (bf16[32,1024]{1,0:T(8,128)(2,1)S(1)}, bf16[32,1024]{1,0:T(8,128)(2,1)S(1)}, u32[]{:S(2)}, u32[]{:S(2)}) collective-permute-start(bf16[32,1024]{1,0:T(8,128)(2,1)S(1)} %get-tuple-element.48.refs_5_), channel_id=1, source_target_pairs={{0,16},{2,50},{4,20},{6,54},{8,24},{10,58},{12,28},{14,62},{16,32}... | collective-permute-start | bytes 196616 | tf_op jit(solution)/shard_map/ppermute | solution.py:362
  16.6 6.0 %collective-permute-start.5 = (bf16[32,1024]{1,0:T(8,128)(2,1)S(1)}, bf16[32,1024]{1,0:T(8,128)(2,1)S(1)}, u32[]{:S(2)}, u32[]{:S(2)}) collective-permute-start(bf16[32,1024]{1,0:T(8,128)(2,1)S(1)} %get-tuple-element.48.refs_5_), channel_id=1, source_target_pairs={{0,32},{2,34},{4,36},{6,38},{8,40},{10,42},{12,44},{14,46},{16,48}... | collective-permute-start | bytes 196616 | tf_op jit(solution)/shard_map/ppermute | solution.py:362
  20.5 2.1 %collective-permute-start.6 = (bf16[32,1024]{1,0:T(8,128)(2,1)S(1)}, bf16[32,1024]{1,0:T(8,128)(2,1)S(1)}, u32[]{:S(2)}, u32[]{:S(2)}) collective-permute-start(bf16[32,1024]{1,0:T(8,128)(2,1)S(1)} %collective-permute-done.4.refs_6_), channel_id=1, source_target_pairs={{0,2},{2,0},{4,6},{6,4},{8,10},{10,8},{12,14},{14,12},{16,18},{18,... | collective-permute-start | bytes 196616 | tf_op jit(solution)/shard_map/ppermute | solution.py:368
  23.1 5.6 %collective-permute-start.7 = (bf16[32,1024]{1,0:T(8,128)(2,1)S(1)}, bf16[32,1024]{1,0:T(8,128)(2,1)S(1)}, u32[]{:S(2)}, u32[]{:S(2)}) collective-permute-start(bf16[32,1024]{1,0:T(8,128)(2,1)S(1)} %get-tuple-element.52.refs_5_), channel_id=1, source_target_pairs={{0,64},{2,194},{4,68},{6,198},{8,72},{10,202},{12,76},{14,206},{16... | collective-permute-start | bytes 196616 | tf_op jit(solution)/shard_map/ppermute | solution.py:362
  24.7 6.2 %collective-permute-start.8 = (bf16[32,1024]{1,0:T(8,128)(2,1)S(1)}, bf16[32,1024]{1,0:T(8,128)(2,1)S(1)}, u32[]{:S(2)}, u32[]{:S(2)}) collective-permute-start(bf16[32,1024]{1,0:T(8,128)(2,1)S(1)} %get-tuple-element.52.refs_5_), channel_id=1, source_target_pairs={{0,128},{2,130},{4,132},{6,134},{8,136},{10,138},{12,140},{14,142}... | collective-permute-start | bytes 196616 | tf_op jit(solution)/shard_map/ppermute | solution.py:362
  28.6 2.3 %collective-permute-start.9 = (bf16[32,1024]{1,0:T(8,128)(2,1)S(1)}, bf16[32,1024]{1,0:T(8,128)(2,1)S(1)}, u32[]{:S(2)}, u32[]{:S(2)}) collective-permute-start(bf16[32,1024]{1,0:T(8,128)(2,1)S(1)} %collective-permute-done.7.refs_6_), channel_id=1, source_target_pairs={{0,2},{2,0},{4,6},{6,4},{8,10},{10,8},{12,14},{14,12},{16,18},{18,... | collective-permute-start | bytes 196616 | tf_op jit(solution)/shard_map/ppermute | solution.py:368
  33.0 17.9 %collective-permute-start.10 = (bf16[128,1024]{1,0:T(8,128)(2,1)S(1)}, bf16[128,1024]{1,0:T(8,128)(2,1)S(1)}, u32[]{:S(2)}, u32[]{:S(2)}) collective-permute-start(bf16[128,1024]{1,0:T(8,128)(2,1)S(1)} %finish_sent.1), channel_id=1, source_target_pairs={{0,1},{1,0},{2,3},{3,2},{4,5},{5,4},{6,7},{7,6},{8,9},{9,8},{10,11... | collective-permute-start | bytes 786440 | tf_op jit(solution)/shard_map/ppermute | solution.py:541

commit v4 on v3

--- a/solution.py
+++ b/solution.py
@@ -1,3 +1,5 @@
+import functools
+
 import jax
 import jax.numpy as jnp
 from jax import lax
@@ -28,10 +30,10 @@
     return terms[0]
 
 
-def short_conv(load, taps, j):
-    total = taps[0] * load(j)
+def short_conv(line, taps):
+    total = taps[0] * line[-1]
     for k in range(1, len(taps)):
-        total = total + taps[k] * load(j - k)
+        total = total + taps[k] * line[-1 - k]
     return total
 
 
@@ -54,15 +56,15 @@
 
 
 def state_kernel(
-    x_hbm, taps_ref, rate_ref,
+    x_hbm, taps_hbm, rate_hbm,
     gate_ref, ends_ref, state_ref, sum_ref,
-    raw, raw_query, wide, keep_ref, run_ref, sems,
+    raw, raw_query, wide, keep_ref, run_ref, taps_all, rate_all, sems, small_sems,
 ):
     step_id = pl.program_id(0)
     _, _, toks, width = raw.shape
     half = toks // 2
-    rim = taps_ref.shape[0] - 1
-    modes = rate_ref.shape[0]
+    rim = taps_all.shape[0] - 1
+    modes = rate_all.shape[0]
     run = half // SUB
 
     def fetches(i):
@@ -77,14 +79,26 @@
             ),
         )
 
+    small = (
+        pltpu.make_async_copy(taps_hbm, taps_all, small_sems.at[0]),
+        pltpu.make_async_copy(rate_hbm, rate_all, small_sems.at[1]),
+    )
+
     @pl.when(step_id == 0)
     def _():
+        for copy in small:
+            copy.start()
         for i in range(raw.shape[0]):
             for copy in fetches(i):
                 copy.start()
-
-    keep_ref[...] = jnp.exp(-rate_ref[...])
-    run_ref[...] = jnp.exp(-rate_ref[...] * run)
+        for copy in small:
+            copy.wait()
+
+    strip = pl.ds(pl.multiple_of(step_id * width, LANES), width)
+    taps_ref = taps_all.at[:, :, strip]
+    rates = rate_all[:, strip]
+    keep_ref[...] = jnp.exp(-rates)
+    run_ref[...] = jnp.exp(-rates * run)
     for copy in fetches(step_id):
         copy.wait()
     index = lax.broadcasted_iota(jnp.int32, (SUB, LANES), 0)
@@ -103,11 +117,11 @@
         for part in range(2):
             base = part * half
             states = None
+            load = lambda s, at: wide[s, pl.ds(SUB + base + at, SUB, stride=run), :]
+            lines = [[load(s, at) for at in range(-rim, 0)] for s in range(2)]
             for j in range(run):
-                load = lambda s, at: wide[s, pl.ds(SUB + base + at, SUB, stride=run), :]
-                key = short_conv(lambda at: load(0, at), key_taps, j)
-                value = short_conv(lambda at: load(1, at), value_taps, j)
-                gate = key * value
+                lines = [line[-rim:] + [load(s, j)] for s, line in enumerate(lines)]
+                gate = short_conv(lines[0], key_taps) * short_conv(lines[1], value_taps)
                 if part == 0 and j < rim:
                     gate = jnp.where(index == 0, 0.0, gate)
                 gate_ref[pl.ds(t * toks + base + j, SUB, stride=run), :] = gate
@@ -223,9 +237,9 @@
 
 
 def local_kernel(
-    part_id, x_hbm, taps_ref, gate_ref, ends_ref, res_ref, rate_ref, skip_ref,
-    query_ref, local_ref, raw, wide, begins, keep_ref, gain_ref, run_ref, sems,
+    first_strip, part_id, x_hbm, taps_ref, gate_ref, ends_ref, res_ref, rate_ref, skip_ref, *refs
 ):
+    query_ref, local_ref, raw, wide, begins, keep_ref, gain_ref, run_ref, sems = refs[-9:]
     step_id = pl.program_id(0)
     part = part_id[0]
     _, toks, width = raw.shape
@@ -236,7 +250,7 @@
 
     def fetch(i):
         return pltpu.make_async_copy(
-            x_hbm.at[0, :, pl.ds(pl.multiple_of(i * width, LANES), width)],
+            x_hbm.at[0, :, pl.ds(pl.multiple_of((first_strip + i) * width, LANES), width)],
             raw.at[i],
             sems.at[i],
         )
@@ -283,10 +297,11 @@
         before = raw[step_id, half - 16 : half, cols].astype(F32)[16 - rim :]
         wide[SUB - rim : SUB, :] = before
         taps = tap_rows(taps_ref, 0, cols)
+        load = lambda at: wide[pl.ds(SUB + at, SUB, stride=run), :]
+        line = [load(at) for at in range(-rim, 0)]
         for j in range(run):
-            query_ref[pl.ds(t * half + j, SUB, stride=run), :] = short_conv(
-                lambda at: wide[pl.ds(SUB + at, SUB, stride=run), :], taps, j
-            )
+            line = line[-rim:] + [load(j)]
+            query_ref[pl.ds(t * half + j, SUB, stride=run), :] = short_conv(line, taps)
 
 
 def finish_kernel(
@@ -298,8 +313,9 @@
     half = out_ref.shape[0]
     run = half // SUB
     row = lax.broadcasted_iota(jnp.int32, (STEP, LANES), 0)
-    for t, c in enumerate(range(0, width, LANES)):
-        cols = slice(c, c + LANES)
+
+    def tile(t, _):
+        cols = pl.ds(pl.multiple_of(t * LANES, LANES), LANES)
         rates = rate_ref[:, cols]
         gains = res_ref[:, cols] * jnp.sqrt(2.0 * rates)
         keep_all = jnp.exp(-rates)
@@ -327,7 +343,7 @@
         skip = skip_ref[:, cols]
         over = jnp.sum(gains * grow, axis=0, keepdims=True)
         for r in range(0, half, STEP):
-            rows = slice(t * half + r, t * half + r + STEP)
+            rows = pl.ds(pl.multiple_of(t * half + r, STEP), STEP)
             value = query_ref[rows, :] * (local_ref[rows, :] + carry[r : r + STEP, :])
             if r == 0:
                 begin = carry[0:SUB, :]
@@ -336,6 +352,9 @@
                 value = jnp.where((row == 0) & (part == 0), head, value)
                 value = jnp.where((row == 1) & (part == 0), second, value)
             out_ref[r : r + STEP, cols] = value.astype(BF16)
+        return 0
+
+    lax.fori_loop(0, width // LANES, tile, 0)
 
 
 def place_kernel(ids, far_ref, held_ref, out_ref, sem):
@@ -408,7 +427,7 @@
     gate, ends, state, summary = pl.pallas_call(
         state_kernel,
         grid=(steps,),
-        in_specs=[in_hbm, strip(rim + 1, 3), strip(modes)],
+        in_specs=[in_hbm] * 3,
         out_specs=[tall(toks), ends_spec, strip(modes), strip(modes + PAIR)],
         out_shape=[
             jax.ShapeDtypeStruct((all_tiles * toks, LANES), F32),
@@ -422,44 +441,55 @@
             pltpu.VMEM((2, toks + SUB, LANES), F32),
             pltpu.VMEM((modes, tile), F32),
             pltpu.VMEM((modes, tile), F32),
+            pltpu.VMEM((rim + 1, 3, width), F32),
+            pltpu.VMEM((modes, width), F32),
             pltpu.SemaphoreType.DMA((3, steps)),
+            pltpu.SemaphoreType.DMA((2,)),
         ],
         compiler_params=params,
         name="states",
     )(x_kept, taps_kept, rates_kept)
 
-    def local(which, gate, name):
+    def shifted(first, *lead):
+        return pl.BlockSpec(lead + (tile,), lambda i, *_: (0,) * len(lead) + (first + i,))
+
+    def local(which, gate, first, count, held, name):
         return pl.pallas_call(
-            local_kernel,
+            functools.partial(local_kernel, first),
             grid_spec=pltpu.PrefetchScalarGridSpec(
                 num_scalar_prefetch=1,
-                grid=(steps,),
+                grid=(count,),
                 in_specs=[
                     in_hbm,
-                    strip(rim + 1, 3),
-                    tall(toks),
-                    ends_spec,
-                    strip(modes),
-                    strip(modes),
-                    strip(1),
-                ],
-                out_specs=[tall(half), tall(half)],
+                    shifted(first, rim + 1, 3),
+                    pl.BlockSpec((tiles * toks, LANES), lambda i, *_: (first + i, 0)),
+                    pl.BlockSpec(
+                        (tiles, 2, modes * SUB, LANES), lambda i, *_: (first + i, 0, 0, 0)
+                    ),
+                    shifted(first, modes),
+                    shifted(first, modes),
+                    shifted(first, 1),
+                ]
+                + [pl.BlockSpec(memory_space=pl.ANY)] * len(held),
+                out_specs=[pl.BlockSpec((tiles * half, LANES), lambda i, *_: (first + i, 0))] * 2,
                 scratch_shapes=[
-                    pltpu.VMEM((steps, toks, tile), BF16),
+                    pltpu.VMEM((count, toks, tile), BF16),
                     pltpu.VMEM((half + SUB, LANES), F32),
                     pltpu.VMEM((modes * SUB, LANES), F32),
                     pltpu.VMEM((modes, tile), F32),
                     pltpu.VMEM((modes, tile), F32),
                     pltpu.VMEM((modes, tile), F32),
-                    pltpu.SemaphoreType.DMA((steps,)),
+                    pltpu.SemaphoreType.DMA((count,)),
                 ],
             ),
             out_shape=[jax.ShapeDtypeStruct((all_tiles * half, LANES), F32)] * 2,
+            input_output_aliases={8: 0, 9: 1} if held else {},
             compiler_params=params,
             name=name,
-        )(which, x_kept, short_filter, gate, ends, weights, rates, skip)
-
-    locals_sent = local(1 - side, gate, "local_sent")
+        )(which, x_kept, short_filter, gate, ends, weights, rates, skip, *held)
+
+    few = steps // 2
+    locals_sent = local(1 - side, gate, 0, few, (), "local_sent_0")
 
     ids = index.astype(jnp.int32).reshape(1)
     in_vmem = pl.BlockSpec(memory_space=pltpu.VMEM)
@@ -471,6 +501,9 @@
     for level, count in enumerate(counts):
         last = level == len(counts) - 1
         if level == 2:
+            summary, locals_sent = lax.optimization_barrier((summary, locals_sent))
+            locals_sent = local(1 - side, gate, few, steps - few, locals_sent, "local_sent_1")
+        if level == 3:
             summary, locals_sent = lax.optimization_barrier((summary, locals_sent))
         arrived = exchange(summary, ctx_count, index, stride, count)
         shapes = [
@@ -537,10 +570,18 @@
             skip,
         )
 
-    sent = finish(1 - side, jnp.zeros_like(side), width, locals_sent, prefix, "finish_sent")
+    sent = pl.pallas_call(
+        finish_kernel,
+        in_specs=[pl.BlockSpec(memory_space=pltpu.SMEM)] + [in_vmem] * 9,
+        out_specs=in_vmem,
+        out_shape=jax.ShapeDtypeStruct((half, width), BF16),
+        scratch_shapes=[pltpu.VMEM((modes * SUB, LANES), F32), pltpu.VMEM((half, LANES), F32)],
+        compiler_params=params,
+        name="finish_sent",
+    )(1 - side, *locals_sent, prefix, past, own, short_filter, weights, rates, skip)
     far = lax.ppermute(sent, "chan", [(0, 1), (1, 0)])
     prefix, gate, sent = lax.optimization_barrier((prefix, gate, sent))
-    locals_own = local(side, gate, "local_own")
+    locals_own = local(side, gate, 0, steps, (), "local_own")
     held = finish(side, side, 2 * width, locals_own, prefix, "finish_own")
     return pl.pallas_call(
         place_kernel,

time: 51.9 us -> 50.8 us (0.979)
  the two profiles are of different devices: /device:TPU:96 before, /device:TPU:0 now
where the time goes in v4:
time: 50.8 us; the launch traced here: 50.6 us
  starting transfers between devices  18.2 us (36%)
  waiting for transfers between devices  16.8 us (33%)
  Pallas kernels  15.4 us (30%)
    ppermute x7, starting transfers between devices, send(): return lax.ppermute(value, 'ctx', route(hop))  12.3 us
    ppermute x7, waiting for transfers between devices, send(): return lax.ppermute(value, 'ctx', route(hop))  9.85 us
    ppermute x1, waiting for transfers between devices, shards(): far = lax.ppermute(sent, 'chan', [(0, 1), (1, 0)])  6.93 us
    ppermute x1, starting transfers between devices, shards(): far = lax.ppermute(sent, 'chan', [(0, 1), (1, 0)])  5.87 us
    pallas_call x3, Pallas kernels, local(): pl.pallas_call(functools.partial(local_kernel, first), grid_spec=pltpu.Pr...  5.73 us
    pallas_call x1, Pallas kernels, shards(): pl.pallas_call(state_kernel, grid=(steps,), in_specs=[in_hbm] * 3, out_sp...  3.72 us
    pallas_call x1, Pallas kernels, finish(): pl.pallas_call(finish_kernel, grid_spec=pltpu.PrefetchScalarGridSpec(num_...  2.68 us
    pallas_call x4, Pallas kernels, shards(): pl.pallas_call(body, in_specs=[pl.BlockSpec(memory_space=pltpu.SMEM)] + [...  1.64 us
  transfers between devices with their start and end apart: 11, of which 8 were waited for; matrix products, arithmetic and copies ran while one was open for 0% of the time, Pallas kernels for 17%

profile of v4, /device:TPU:0, one launch (start us, length us, event | category | flops | bytes accessed | tf_op | source)
XLA Modules:
  0.0 50.6 jit_solution(15927624804980120603)
XLA Ops:
  0.0 0.0 copy-start.1
  0.0 0.0 copy-start
  0.0 0.0 copy-start.2
  0.0 0.0 copy-start.3
  0.0 3.7 %states.1 = (f32[2048,128]{1,0:T(8,128)S(1)}, f32[8,2,128,128]{3,2,1,0:T(8,128)S(1)}, f32[16,1024]{1,0:T(8,128)S(1)}, bf16[32,1024]{1,0:T(8,128)(2,1)S(1)}) custom-call(bf16[3,256,1024]{2,1,0:T(8,128)(2,1)} %bitcast.26, f32[3,3,1024]{2,1,0:T(4,128)} %taps_ref.9, f32[16,1024]{1,0:T(8,128)} %bitcast.6), custom_call_target="tpu_custom_call" | custom-call | tf_op jit(solution)/shard_map/states/pallas_call | solution.py:427
  3.7 0.1 collective-permute-start
  3.8 1.2 %collective-permute-done.refs_6_ = bf16[32,1024]{1,0:T(8,128)(2,1)S(1)} collective-permute-done((bf16[32,1024]{1,0:T(8,128)(2,1)S(1)}, bf16[32,1024]{1,0:T(8,128)(2,1)S(1)}, u32[]{:S(2)}, u32[]{:S(2)}) %collective-permute-start) | collective-permute-done | bytes 65568 | tf_op jit(solution)/shard_map/ppermute | solution.py:381
  5.1 0.0 copy-done.1
  5.1 0.0 copy-done
  5.1 0.3 join_0.1
  5.4 0.3 collective-permute-start.1
  5.7 3.3 %collective-permute-start.2 = (bf16[32,1024]{1,0:T(8,128)(2,1)S(1)}, bf16[32,1024]{1,0:T(8,128)(2,1)S(1)}, u32[]{:S(2)}, u32[]{:S(2)}) collective-permute-start(bf16[32,1024]{1,0:T(8,128)(2,1)S(1)} %get-tuple-element.42.refs_5_), channel_id=1, source_target_pairs={{0,8},{2,10},{4,12},{6,14},{8,0},{10,2},{12,4},{14,6},{16,24},{18,... | collective-permute-start | bytes 196616 | tf_op jit(solution)/shard_map/ppermute | solution.py:381
  8.9 2.9 %collective-permute-done.1.refs_6_ = bf16[32,1024]{1,0:T(8,128)(2,1)S(1)} collective-permute-done((bf16[32,1024]{1,0:T(8,128)(2,1)S(1)}, bf16[32,1024]{1,0:T(8,128)(2,1)S(1)}, u32[]{:S(2)}, u32[]{:S(2)}) %collective-permute-start.1) | collective-permute-done | bytes 65568 | tf_op jit(solution)/shard_map/ppermute | solution.py:381
  11.8 0.0 collective-permute-start.3
  11.8 0.0 copy-done.2
  11.8 0.0 copy-done.3
  11.8 1.6 %local_sent_0.1 = (f32[1024,128]{1,0:T(8,128)S(1)}, f32[1024,128]{1,0:T(8,128)S(1)}) custom-call(s32[1]{0:T(128)S(6)} %sub.2.part_id.ids, bf16[3,256,1024]{2,1,0:T(8,128)(2,1)} %bitcast.27, f32[3,3,1024]{2,1,0:T(4,128)S(1)} %copy-done.1, f32[2048,128]{1,0:T(8,128)S(1)} %get-tuple-element.65.gate_ref, f32[8,2,128,128]{3,2,1,0:T(8,128)S(1)} %get-tuple-element.48.ends_ref, ...), custom_call_target="tpu_custom_call" | custom-call | tf_op jit(solution)/shard_map/local_sent_0/pallas_call | solution.py:457
  13.4 0.3 collective-permute-done.2.refs_7_
  13.7 0.0 collective-permute-done.3.refs_8_
  13.7 0.5 join_1.1
  14.2 1.4 %collective-permute-start.4 = (bf16[32,1024]{1,0:T(8,128)(2,1)S(1)}, bf16[32,1024]{1,0:T(8,128)(2,1)S(1)}, u32[]{:S(2)}, u32[]{:S(2)}) collective-permute-start(bf16[32,1024]{1,0:T(8,128)(2,1)S(1)} %get-tuple-element.51.refs_5_), channel_id=1, source_target_pairs={{0,16},{2,50},{4,20},{6,54},{8,24},{10,58},{12,28},{14,62},{16,32}... | collective-permute-start | bytes 196616 | tf_op jit(solution)/shard_map/ppermute | solution.py:381
  15.6 2.7 %collective-permute-start.5 = (bf16[32,1024]{1,0:T(8,128)(2,1)S(1)}, bf16[32,1024]{1,0:T(8,128)(2,1)S(1)}, u32[]{:S(2)}, u32[]{:S(2)}) collective-permute-start(bf16[32,1024]{1,0:T(8,128)(2,1)S(1)} %get-tuple-element.51.refs_5_), channel_id=1, source_target_pairs={{0,32},{2,34},{4,36},{6,38},{8,40},{10,42},{12,44},{14,46},{16,48}... | collective-permute-start | bytes 196616 | tf_op jit(solution)/shard_map/ppermute | solution.py:381
  18.3 1.5 %collective-permute-done.4.refs_6_ = bf16[32,1024]{1,0:T(8,128)(2,1)S(1)} collective-permute-done((bf16[32,1024]{1,0:T(8,128)(2,1)S(1)}, bf16[32,1024]{1,0:T(8,128)(2,1)S(1)}, u32[]{:S(2)}, u32[]{:S(2)}) %collective-permute-start.4) | collective-permute-done | bytes 65568 | tf_op jit(solution)/shard_map/ppermute | solution.py:381
  19.7 0.0 collective-permute-start.6
  19.7 1.6 %local_sent_1.1 = (f32[1024,128]{1,0:T(8,128)S(1)}, f32[1024,128]{1,0:T(8,128)S(1)}) custom-call(s32[1]{0:T(128)S(6)} %sub.2.part_id.ids, bf16[3,256,1024]{2,1,0:T(8,128)(2,1)} %bitcast.28, f32[3,3,1024]{2,1,0:T(4,128)S(1)} %copy-done.1, f32[2048,128]{1,0:T(8,128)S(1)} %get-tuple-element.65.gate_ref, ...), custom_call_target="tpu_custom_call", output_to_operand_aliasing={{0}: (8, {}), {1}: (9, {})} | custom-call | tf_op jit(solution)/shard_map/local_sent_1/pallas_call | solution.py:457
  21.3 0.6 %collective-permute-done.5.refs_7_ = bf16[32,1024]{1,0:T(8,128)(2,1)S(1)} collective-permute-done((bf16[32,1024]{1,0:T(8,128)(2,1)S(1)}, bf16[32,1024]{1,0:T(8,128)(2,1)S(1)}, u32[]{:S(2)}, u32[]{:S(2)}) %collective-permute-start.5) | collective-permute-done | bytes 65568 | tf_op jit(solution)/shard_map/ppermute | solution.py:381
  21.9 0.0 collective-permute-done.6.refs_8_
  21.9 0.5 join_2.1
  22.4 1.7 %collective-permute-start.7 = (bf16[32,1024]{1,0:T(8,128)(2,1)S(1)}, bf16[32,1024]{1,0:T(8,128)(2,1)S(1)}, u32[]{:S(2)}, u32[]{:S(2)}) collective-permute-start(bf16[32,1024]{1,0:T(8,128)(2,1)S(1)} %get-tuple-element.62.refs_5_), channel_id=1, source_target_pairs={{0,64},{2,194},{4,68},{6,198},{8,72},{10,202},{12,76},{14,206},{16... | collective-permute-start | bytes 196616 | tf_op jit(solution)/shard_map/ppermute | solution.py:381
  24.0 2.9 %collective-permute-start.8 = (bf16[32,1024]{1,0:T(8,128)(2,1)S(1)}, bf16[32,1024]{1,0:T(8,128)(2,1)S(1)}, u32[]{:S(2)}, u32[]{:S(2)}) collective-permute-start(bf16[32,1024]{1,0:T(8,128)(2,1)S(1)} %get-tuple-element.62.refs_5_), channel_id=1, source_target_pairs={{0,128},{2,130},{4,132},{6,134},{8,136},{10,138},{12,140},{14,142}... | collective-permute-start | bytes 196616 | tf_op jit(solution)/shard_map/ppermute | solution.py:381
  26.9 1.0 %collective-permute-done.7.refs_6_ = bf16[32,1024]{1,0:T(8,128)(2,1)S(1)} collective-permute-done((bf16[32,1024]{1,0:T(8,128)(2,1)S(1)}, bf16[32,1024]{1,0:T(8,128)(2,1)S(1)}, u32[]{:S(2)}, u32[]{:S(2)}) %collective-permute-start.7) | collective-permute-done | bytes 65568 | tf_op jit(solution)/shard_map/ppermute | solution.py:381
  27.9 0.0 collective-permute-start.9
  27.9 2.4 %collective-permute-done.8.refs_7_ = bf16[32,1024]{1,0:T(8,128)(2,1)S(1)} collective-permute-done((bf16[32,1024]{1,0:T(8,128)(2,1)S(1)}, bf16[32,1024]{1,0:T(8,128)(2,1)S(1)}, u32[]{:S(2)}, u32[]{:S(2)}) %collective-permute-start.8) | collective-permute-done | bytes 65568 | tf_op jit(solution)/shard_map/ppermute | solution.py:381
  30.4 0.0 collective-permute-done.9.refs_8_
  30.4 0.4 join_3.1
  30.8 0.9 %finish_sent.1 = bf16[128,1024]{1,0:T(8,128)(2,1)S(1)} custom-call(s32[1]{0:T(128)S(6)} %sub.2.part_id.ids, f32[1024,128]{1,0:T(8,128)S(1)} %get-tuple-element.57.query_ref, f32[1024,128]{1,0:T(8,128)S(1)} %get-tuple-element.58.local_ref, f32[16,1024]{1,0:T(8,128)S(1)} %get-tuple-element.68.prefix_ref, f32[8,1024]{1,0:T(8,128)S(1)} %get-tuple-element.64.past_ref, ...), custom_call_target="tpu_custom_call" | custom-call | tf_op jit(solution)/shard_map/finish_sent/pallas_call | solution.py:573
  31.7 5.9 %collective-permute-start.10 = (bf16[128,1024]{1,0:T(8,128)(2,1)S(1)}, bf16[128,1024]{1,0:T(8,128)(2,1)S(1)}, u32[]{:S(2)}, u32[]{:S(2)}) collective-permute-start(bf16[128,1024]{1,0:T(8,128)(2,1)S(1)} %finish_sent.1), channel_id=1, source_target_pairs={{0,1},{1,0},{2,3},{3,2},{4,5},{5,4},{6,7},{7,6},{8,9},{9,8},{10,11... | collective-permute-start | bytes 786440 | tf_op jit(solution)/shard_map/ppermute | solution.py:582
  37.6 0.1 pad_add_fusion.ids
  37.7 2.6 %local_own.1 = (f32[1024,128]{1,0:T(8,128)S(1)}, f32[1024,128]{1,0:T(8,128)S(1)}) custom-call(s32[1]{0:T(128)} %bitcast.part_id, bf16[3,256,1024]{2,1,0:T(8,128)(2,1)} %bitcast.29, f32[3,3,1024]{2,1,0:T(4,128)S(1)} %copy-done.1, f32[2048,128]{1,0:T(8,128)S(1)} %get-tuple-element.65.gate_ref, f32[8,2,128,128]{3,2,1,0:T(8,128)S(1)} %get-tuple-element.48.ends_ref, ...), custom_call_target="tpu_custom_call" | custom-call | tf_op jit(solution)/shard_map/local_own/pallas_call | solution.py:457
  40.3 2.7 %finish_own.1.held_ref = bf16[128,2048]{1,0:T(8,128)(2,1)} custom-call(s32[2]{0:T(128)S(1)} %pad_add_fusion.ids, f32[1024,128]{1,0:T(8,128)S(1)} %get-tuple-element.66.query_ref, f32[1024,128]{1,0:T(8,128)S(1)} %get-tuple-element.67.local_ref, f32[16,1024]{1,0:T(8,128)S(1)} %get-tuple-element.68.prefix_ref, f32[8,1024]{1,0:T(8,128)S(1)} %get-tuple-element.64.past_ref, ...), custom_call_target="tpu_custom_call" | custom-call | tf_op jit(solution)/shard_map/finish_own/pallas_call | solution.py:536
  43.0 6.9 %collective-permute-done.10.far_ref = bf16[128,1024]{1,0:T(8,128)(2,1)S(1)} collective-permute-done((bf16[128,1024]{1,0:T(8,128)(2,1)S(1)}, bf16[128,1024]{1,0:T(8,128)(2,1)S(1)}, u32[]{:S(2)}, u32[]{:S(2)}) %collective-permute-start.10) | collective-permute-done | bytes 262176 | tf_op jit(solution)/shard_map/ppermute | solution.py:582
  49.9 0.7 %place.1 = bf16[128,2048]{1,0:T(8,128)(2,1)} custom-call(s32[1]{0:T(128)S(6)} %sub.2.part_id.ids, bf16[128,1024]{1,0:T(8,128)(2,1)S(1)} %collective-permute-done.10.far_ref, bf16[128,2048]{1,0:T(8,128)(2,1)} %finish_own.1.held_ref), custom_call_target="tpu_custom_call", output_to_operand_aliasing={{}: (2, {})} | custom-call | tf_op jit(solution)/shard_map/place/pallas_call | solution.py:586
  (2 shorter events, 0.0 us)
Async XLA Ops:
  0.0 5.1 %copy-start.1 = (f32[3,3,1024]{2,1,0:T(4,128)S(1)}, f32[3,3,1024]{2,1,0:T(4,128)}, u32[]{:S(2)}) copy-start(f32[3,3,1024]{2,1,0:T(4,128)} %taps_ref.9) | copy-start | bytes 110596
  0.0 5.1 %copy-start = (f32[1024,16]{0,1:T(8,128)S(1)}, f32[1024,16]{0,1:T(8,128)}, u32[]{:S(2)}) copy-start(f32[1024,16]{0,1:T(8,128)} %param.8) | copy-start | bytes 196612
  0.0 11.8 %copy-start.2 = (f32[1024,16]{0,1:T(8,128)S(1)}, f32[1024,16]{0,1:T(8,128)}, u32[]{:S(2)}) copy-start(f32[1024,16]{0,1:T(8,128)} %param.7) | copy-start | bytes 196612
  0.0 11.8 %copy-start.3 = (f32[1024]{0:T(1024)S(1)}, f32[1024]{0:T(1024)}, u32[]{:S(2)}) copy-start(f32[1024]{0:T(1024)} %param.9) | copy-start | bytes 12292
  3.7 1.3 %collective-permute-start = (bf16[32,1024]{1,0:T(8,128)(2,1)S(1)}, bf16[32,1024]{1,0:T(8,128)(2,1)S(1)}, u32[]{:S(2)}, u32[]{:S(2)}) collective-permute-start(bf16[32,1024]{1,0:T(8,128)(2,1)S(1)} %get-tuple-element.38.refs_5_.sum_ref), channel_id=1, source_target_pairs={{0,2},{2,0},{4,6},{6,4},{8,10},{10,8},{12,14},{14,12},{16,18},{18,... | collective-permute-start | bytes 196616 | tf_op jit(solution)/shard_map/ppermute | solution.py:381
  5.4 6.4 %collective-permute-start.1 = (bf16[32,1024]{1,0:T(8,128)(2,1)S(1)}, bf16[32,1024]{1,0:T(8,128)(2,1)S(1)}, u32[]{:S(2)}, u32[]{:S(2)}) collective-permute-start(bf16[32,1024]{1,0:T(8,128)(2,1)S(1)} %get-tuple-element.42.refs_5_), channel_id=1, source_target_pairs={{0,4},{2,14},{4,8},{6,2},{8,12},{10,6},{12,0},{14,10},{16,20},{18,... | collective-permute-start | bytes 196616 | tf_op jit(solution)/shard_map/ppermute | solution.py:381
  5.7 8.0 %collective-permute-start.2 = (bf16[32,1024]{1,0:T(8,128)(2,1)S(1)}, bf16[32,1024]{1,0:T(8,128)(2,1)S(1)}, u32[]{:S(2)}, u32[]{:S(2)}) collective-permute-start(bf16[32,1024]{1,0:T(8,128)(2,1)S(1)} %get-tuple-element.42.refs_5_), channel_id=1, source_target_pairs={{0,8},{2,10},{4,12},{6,14},{8,0},{10,2},{12,4},{14,6},{16,24},{18,... | collective-permute-start | bytes 196616 | tf_op jit(solution)/shard_map/ppermute | solution.py:381
  11.8 1.9 %collective-permute-start.3 = (bf16[32,1024]{1,0:T(8,128)(2,1)S(1)}, bf16[32,1024]{1,0:T(8,128)(2,1)S(1)}, u32[]{:S(2)}, u32[]{:S(2)}) collective-permute-start(bf16[32,1024]{1,0:T(8,128)(2,1)S(1)} %collective-permute-done.1.refs_6_), channel_id=1, source_target_pairs={{0,2},{2,0},{4,6},{6,4},{8,10},{10,8},{12,14},{14,12},{16,18},{18,... | collective-permute-start | bytes 196616 | tf_op jit(solution)/shard_map/ppermute | solution.py:387
  14.2 5.6 %collective-permute-start.4 = (bf16[32,1024]{1,0:T(8,128)(2,1)S(1)}, bf16[32,1024]{1,0:T(8,128)(2,1)S(1)}, u32[]{:S(2)}, u32[]{:S(2)}) collective-permute-start(bf16[32,1024]{1,0:T(8,128)(2,1)S(1)} %get-tuple-element.51.refs_5_), channel_id=1, source_target_pairs={{0,16},{2,50},{4,20},{6,54},{8,24},{10,58},{12,28},{14,62},{16,32}... | collective-permute-start | bytes 196616 | tf_op jit(solution)/shard_map/ppermute | solution.py:381
  15.6 6.3 %collective-permute-start.5 = (bf16[32,1024]{1,0:T(8,128)(2,1)S(1)}, bf16[32,1024]{1,0:T(8,128)(2,1)S(1)}, u32[]{:S(2)}, u32[]{:S(2)}) collective-permute-start(bf16[32,1024]{1,0:T(8,128)(2,1)S(1)} %get-tuple-element.51.refs_5_), channel_id=1, source_target_pairs={{0,32},{2,34},{4,36},{6,38},{8,40},{10,42},{12,44},{14,46},{16,48}... | collective-permute-start | bytes 196616 | tf_op jit(solution)/shard_map/ppermute | solution.py:381
  19.7 2.1 %collective-permute-start.6 = (bf16[32,1024]{1,0:T(8,128)(2,1)S(1)}, bf16[32,1024]{1,0:T(8,128)(2,1)S(1)}, u32[]{:S(2)}, u32[]{:S(2)}) collective-permute-start(bf16[32,1024]{1,0:T(8,128)(2,1)S(1)} %collective-permute-done.4.refs_6_), channel_id=1, source_target_pairs={{0,2},{2,0},{4,6},{6,4},{8,10},{10,8},{12,14},{14,12},{16,18},{18,... | collective-permute-start | bytes 196616 | tf_op jit(solution)/shard_map/ppermute | solution.py:387
  22.4 5.6 %collective-permute-start.7 = (bf16[32,1024]{1,0:T(8,128)(2,1)S(1)}, bf16[32,1024]{1,0:T(8,128)(2,1)S(1)}, u32[]{:S(2)}, u32[]{:S(2)}) collective-permute-start(bf16[32,1024]{1,0:T(8,128)(2,1)S(1)} %get-tuple-element.62.refs_5_), channel_id=1, source_target_pairs={{0,64},{2,194},{4,68},{6,198},{8,72},{10,202},{12,76},{14,206},{16... | collective-permute-start | bytes 196616 | tf_op jit(solution)/shard_map/ppermute | solution.py:381
  24.0 6.3 %collective-permute-start.8 = (bf16[32,1024]{1,0:T(8,128)(2,1)S(1)}, bf16[32,1024]{1,0:T(8,128)(2,1)S(1)}, u32[]{:S(2)}, u32[]{:S(2)}) collective-permute-start(bf16[32,1024]{1,0:T(8,128)(2,1)S(1)} %get-tuple-element.62.refs_5_), channel_id=1, source_target_pairs={{0,128},{2,130},{4,132},{6,134},{8,136},{10,138},{12,140},{14,142}... | collective-permute-start | bytes 196616 | tf_op jit(solution)/shard_map/ppermute | solution.py:381
  27.9 2.4 %collective-permute-start.9 = (bf16[32,1024]{1,0:T(8,128)(2,1)S(1)}, bf16[32,1024]{1,0:T(8,128)(2,1)S(1)}, u32[]{:S(2)}, u32[]{:S(2)}) collective-permute-start(bf16[32,1024]{1,0:T(8,128)(2,1)S(1)} %collective-permute-done.7.refs_6_), channel_id=1, source_target_pairs={{0,2},{2,0},{4,6},{6,4},{8,10},{10,8},{12,14},{14,12},{16,18},{18,... | collective-permute-start | bytes 196616 | tf_op jit(solution)/shard_map/ppermute | solution.py:387
  31.7 18.2 %collective-permute-start.10 = (bf16[128,1024]{1,0:T(8,128)(2,1)S(1)}, bf16[128,1024]{1,0:T(8,128)(2,1)S(1)}, u32[]{:S(2)}, u32[]{:S(2)}) collective-permute-start(bf16[128,1024]{1,0:T(8,128)(2,1)S(1)} %finish_sent.1), channel_id=1, source_target_pairs={{0,1},{1,0},{2,3},{3,2},{4,5},{5,4},{6,7},{7,6},{8,9},{9,8},{10,11... | collective-permute-start | bytes 786440 | tf_op jit(solution)/shard_map/ppermute | solution.py:582

commit v5 on v4

--- a/solution.py
+++ b/solution.py
@@ -9,6 +9,7 @@
 
 LANES = 128
 SUB = 8
+UNROLL = 8
 STEP = 32
 PAIR = 16
 F32 = jnp.float32
@@ -191,9 +192,16 @@
         extra = [value[modes:] for value in full]
         firsts = [(e[0:2], e[2:4]) for e in extra]
         states = [state_ref[:, cols]] + [value[:modes] for value in full[1:]]
-        first_keep = jnp.exp(-rates * float(toks - 1))
+        keep = jnp.exp(-rates)
         second_keep = jnp.exp(-rates * float(toks - 2))
-        rest = jnp.exp(-span * float(stride - 1))
+        first_keep = second_keep * keep
+        block_keep = first_keep * keep
+        rest = jnp.exp(-span * float(stride - 1)) if stride > 1 else 1.0
+        run_keep = rest * block_keep
+        powers = [1.0, run_keep]
+        while len(powers) < count:
+            powers.append(powers[-1] * run_keep)
+        before = jnp.exp(-span * as_float(jnp.maximum(behind - 1, 0)))
         joins = []
         for k in range(count):
             linked = origins[k] >= 1
@@ -205,14 +213,10 @@
                 join = jnp.where(linked, join, 0.0)
             joins.append(join)
             states[k] = states[k] + rest * join
-        prefix = prefix_ref[:, cols] + jnp.where(
-            behind >= 1,
-            jnp.exp(-span * as_float(jnp.maximum(behind - 1, 0))) * joins[0],
-            0.0,
-        )
+        passed = jnp.where(behind >= 1, before * block_keep, 1.0)
+        prefix = prefix_ref[:, cols] + jnp.where(behind >= 1, before * joins[0], 0.0)
         for k in range(1, count):
-            gap = as_float((k - 1) * stride + behind)
-            prefix = prefix + jnp.where(place >= k, jnp.exp(-span * gap) * states[k], 0.0)
+            prefix = prefix + jnp.where(place >= k, passed * powers[k - 1] * states[k], 0.0)
         prefix_out[:, cols] = prefix
         past = jnp.where((place >= 1) & (behind == 0), extra[1][4:10], past_ref[0:6, cols])
         past_out[:, cols] = jnp.concatenate([past, jnp.zeros((SUB - 6, LANES), F32)], axis=0)
@@ -220,8 +224,10 @@
             state_out, sum_out = outs[2:]
             total = None
             for k in range(count):
-                gap = as_float((count - 1 - origins[k]) * stride)
-                term = jnp.exp(-span * gap) * states[k]
+                factor = jnp.ones_like(run_keep)
+                for gap in range(1, count):
+                    factor = jnp.where(origins[k] == count - 1 - gap, powers[gap], factor)
+                term = factor * states[k]
                 total = term if total is None else total + term
             state_out[:, cols] = total
             first = extra[0]
@@ -233,7 +239,7 @@
             sum_out[modes:, cols] = jnp.concatenate([first[0:4], end[4:]], axis=0).astype(BF16)
         return 0
 
-    lax.fori_loop(0, width // LANES, tile, 0)
+    lax.fori_loop(0, width // LANES, tile, 0, unroll=UNROLL)
 
 
 def local_kernel(
@@ -354,7 +360,7 @@
             out_ref[r : r + STEP, cols] = value.astype(BF16)
         return 0
 
-    lax.fori_loop(0, width // LANES, tile, 0)
+    lax.fori_loop(0, width // LANES, tile, 0, unroll=UNROLL)
 
 
 def place_kernel(ids, far_ref, held_ref, out_ref, sem):
@@ -489,8 +495,7 @@
         )(which, x_kept, short_filter, gate, ends, weights, rates, skip, *held)
 
     few = steps // 2
-    locals_sent = local(1 - side, gate, 0, few, (), "local_sent_0")
-
+    locals_sent = ()
     ids = index.astype(jnp.int32).reshape(1)
     in_vmem = pl.BlockSpec(memory_space=pltpu.VMEM)
     prefix = jnp.zeros((modes, width), F32)
@@ -500,12 +505,12 @@
     counts = scan_counts(ctx_count)
     for level, count in enumerate(counts):
         last = level == len(counts) - 1
-        if level == 2:
-            summary, locals_sent = lax.optimization_barrier((summary, locals_sent))
-            locals_sent = local(1 - side, gate, few, steps - few, locals_sent, "local_sent_1")
-        if level == 3:
-            summary, locals_sent = lax.optimization_barrier((summary, locals_sent))
         arrived = exchange(summary, ctx_count, index, stride, count)
+        if level >= 2:
+            gate, arrived[0] = lax.optimization_barrier((gate, arrived[0]))
+            first = 0 if level == 2 else few
+            locals_sent = local(1 - side, gate, first, few, locals_sent, f"local_sent_{level}")
+            locals_sent, arrived = lax.optimization_barrier((locals_sent, arrived))
         shapes = [
             jax.ShapeDtypeStruct((modes, width), F32),
             jax.ShapeDtypeStruct((SUB, width), F32),

time: 50.8 us -> 49.6 us (0.976)
  the two profiles are of different devices: /device:TPU:0 before, /device:TPU:96 now
where the time goes in v5:
time: 49.6 us; the launch traced here: 49.4 us
  waiting for transfers between devices  18 us (36%)
  starting transfers between devices  16.1 us (32%)
  Pallas kernels  15 us (30%)
    ppermute x7, waiting for transfers between devices, send(): return lax.ppermute(value, 'ctx', route(hop))  11 us
    ppermute x7, starting transfers between devices, send(): return lax.ppermute(value, 'ctx', route(hop))  10.6 us
    ppermute x1, waiting for transfers between devices, shards(): far = lax.ppermute(sent, 'chan', [(0, 1), (1, 0)])  6.96 us
    pallas_call x3, Pallas kernels, local(): pl.pallas_call(functools.partial(local_kernel, first), grid_spec=pltpu.Pr...  5.73 us
    ppermute x1, starting transfers between devices, shards(): far = lax.ppermute(sent, 'chan', [(0, 1), (1, 0)])  5.53 us
    pallas_call x1, Pallas kernels, shards(): pl.pallas_call(state_kernel, grid=(steps,), in_specs=[in_hbm] * 3, out_sp...  3.73 us
    pallas_call x1, Pallas kernels, finish(): pl.pallas_call(finish_kernel, grid_spec=pltpu.PrefetchScalarGridSpec(num_...  2.68 us
    pallas_call x4, Pallas kernels, shards(): pl.pallas_call(body, in_specs=[pl.BlockSpec(memory_space=pltpu.SMEM)] + [...  1.31 us
  transfers between devices with their start and end apart: 11, of which 8 were waited for; matrix products, arithmetic and copies ran while one was open for 0% of the time, Pallas kernels for 17%

profile of v5, /device:TPU:96, one launch (start us, length us, event | category | flops | bytes accessed | tf_op | source)
XLA Modules:
  0.0 49.4 jit_solution(9862544715556559905)
XLA Ops:
  0.0 0.0 copy-start
  0.0 0.0 copy-start.1
  0.0 0.0 copy-start.2
  0.0 0.0 copy-start.3
  0.0 3.7 %states.1 = (f32[2048,128]{1,0:T(8,128)S(1)}, f32[8,2,128,128]{3,2,1,0:T(8,128)S(1)}, f32[16,1024]{1,0:T(8,128)S(1)}, bf16[32,1024]{1,0:T(8,128)(2,1)S(1)}) custom-call(bf16[3,256,1024]{2,1,0:T(8,128)(2,1)} %bitcast.26, f32[3,3,1024]{2,1,0:T(4,128)} %taps_ref.9, f32[16,1024]{1,0:T(8,128)} %bitcast.6), custom_call_target="tpu_custom_call" | custom-call | tf_op jit(solution)/shard_map/states/pallas_call | solution.py:433
  3.8 0.1 collective-permute-start
  3.9 1.2 %collective-permute-done.refs_6_ = bf16[32,1024]{1,0:T(8,128)(2,1)S(1)} collective-permute-done((bf16[32,1024]{1,0:T(8,128)(2,1)S(1)}, bf16[32,1024]{1,0:T(8,128)(2,1)S(1)}, u32[]{:S(2)}, u32[]{:S(2)}) %collective-permute-start) | collective-permute-done | bytes 65568 | tf_op jit(solution)/shard_map/ppermute | solution.py:387
  5.1 0.0 copy-done
  5.1 0.0 copy-done.1
  5.1 0.2 join_0.1
  5.3 1.0 %collective-permute-start.1 = (bf16[32,1024]{1,0:T(8,128)(2,1)S(1)}, bf16[32,1024]{1,0:T(8,128)(2,1)S(1)}, u32[]{:S(2)}, u32[]{:S(2)}) collective-permute-start(bf16[32,1024]{1,0:T(8,128)(2,1)S(1)} %get-tuple-element.51.refs_5_), channel_id=1, source_target_pairs={{0,4},{2,14},{4,8},{6,2},{8,12},{10,6},{12,0},{14,10},{16,20},{18,... | collective-permute-start | bytes 196616 | tf_op jit(solution)/shard_map/ppermute | solution.py:387
  6.3 0.7 %collective-permute-start.2 = (bf16[32,1024]{1,0:T(8,128)(2,1)S(1)}, bf16[32,1024]{1,0:T(8,128)(2,1)S(1)}, u32[]{:S(2)}, u32[]{:S(2)}) collective-permute-start(bf16[32,1024]{1,0:T(8,128)(2,1)S(1)} %get-tuple-element.51.refs_5_), channel_id=1, source_target_pairs={{0,8},{2,10},{4,12},{6,14},{8,0},{10,2},{12,4},{14,6},{16,24},{18,... | collective-permute-start | bytes 196616 | tf_op jit(solution)/shard_map/ppermute | solution.py:387
  7.0 4.1 %collective-permute-done.1.refs_6_ = bf16[32,1024]{1,0:T(8,128)(2,1)S(1)} collective-permute-done((bf16[32,1024]{1,0:T(8,128)(2,1)S(1)}, bf16[32,1024]{1,0:T(8,128)(2,1)S(1)}, u32[]{:S(2)}, u32[]{:S(2)}) %collective-permute-start.1) | collective-permute-done | bytes 65568 | tf_op jit(solution)/shard_map/ppermute | solution.py:387
  11.1 0.0 collective-permute-start.3
  11.1 1.7 %collective-permute-done.2.refs_7_ = bf16[32,1024]{1,0:T(8,128)(2,1)S(1)} collective-permute-done((bf16[32,1024]{1,0:T(8,128)(2,1)S(1)}, bf16[32,1024]{1,0:T(8,128)(2,1)S(1)}, u32[]{:S(2)}, u32[]{:S(2)}) %collective-permute-start.2) | collective-permute-done | bytes 65568 | tf_op jit(solution)/shard_map/ppermute | solution.py:387
  12.7 0.0 collective-permute-done.3.refs_8_
  12.7 0.4 join_1.1
  13.2 1.6 %collective-permute-start.4 = (bf16[32,1024]{1,0:T(8,128)(2,1)S(1)}, bf16[32,1024]{1,0:T(8,128)(2,1)S(1)}, u32[]{:S(2)}, u32[]{:S(2)}) collective-permute-start(bf16[32,1024]{1,0:T(8,128)(2,1)S(1)} %get-tuple-element.52.refs_5_), channel_id=1, source_target_pairs={{0,16},{2,50},{4,20},{6,54},{8,24},{10,58},{12,28},{14,62},{16,32}... | collective-permute-start | bytes 196616 | tf_op jit(solution)/shard_map/ppermute | solution.py:387
  14.7 2.7 %collective-permute-start.5 = (bf16[32,1024]{1,0:T(8,128)(2,1)S(1)}, bf16[32,1024]{1,0:T(8,128)(2,1)S(1)}, u32[]{:S(2)}, u32[]{:S(2)}) collective-permute-start(bf16[32,1024]{1,0:T(8,128)(2,1)S(1)} %get-tuple-element.52.refs_5_), channel_id=1, source_target_pairs={{0,32},{2,34},{4,36},{6,38},{8,40},{10,42},{12,44},{14,46},{16,48}... | collective-permute-start | bytes 196616 | tf_op jit(solution)/shard_map/ppermute | solution.py:387
  17.5 1.3 %collective-permute-done.4.refs_6_ = bf16[32,1024]{1,0:T(8,128)(2,1)S(1)} collective-permute-done((bf16[32,1024]{1,0:T(8,128)(2,1)S(1)}, bf16[32,1024]{1,0:T(8,128)(2,1)S(1)}, u32[]{:S(2)}, u32[]{:S(2)}) %collective-permute-start.4) | collective-permute-done | bytes 65568 | tf_op jit(solution)/shard_map/ppermute | solution.py:387
  18.7 0.0 collective-permute-start.6
  18.7 0.0 copy-done.2
  18.7 0.0 copy-done.3
  18.7 1.6 %local_sent_2.1 = (f32[1024,128]{1,0:T(8,128)S(1)}, f32[1024,128]{1,0:T(8,128)S(1)}) custom-call(s32[1]{0:T(128)S(6)} %sub.2.part_id.ids, bf16[3,256,1024]{2,1,0:T(8,128)(2,1)} %bitcast.27, f32[3,3,1024]{2,1,0:T(4,128)S(1)} %copy-done.1, f32[2048,128]{1,0:T(8,128)S(1)} %get-tuple-element.81.gate_ref, f32[8,2,128,128]{3,2,1,0:T(8,128)S(1)} %get-tuple-element.57.ends_ref, ...), custom_call_target="tpu_custom_call" | custom-call | tf_op jit(solution)/shard_map/local_sent_2/pallas_call | solution.py:463
  20.3 0.8 %collective-permute-done.5.refs_7_ = bf16[32,1024]{1,0:T(8,128)(2,1)S(1)} collective-permute-done((bf16[32,1024]{1,0:T(8,128)(2,1)S(1)}, bf16[32,1024]{1,0:T(8,128)(2,1)S(1)}, u32[]{:S(2)}, u32[]{:S(2)}) %collective-permute-start.5) | collective-permute-done | bytes 65568 | tf_op jit(solution)/shard_map/ppermute | solution.py:387
  21.1 0.0 collective-permute-done.6.refs_8_
  21.1 0.4 join_2.1
  21.5 1.7 %collective-permute-start.7 = (bf16[32,1024]{1,0:T(8,128)(2,1)S(1)}, bf16[32,1024]{1,0:T(8,128)(2,1)S(1)}, u32[]{:S(2)}, u32[]{:S(2)}) collective-permute-start(bf16[32,1024]{1,0:T(8,128)(2,1)S(1)} %get-tuple-element.64.refs_5_), channel_id=1, source_target_pairs={{0,64},{2,194},{4,68},{6,198},{8,72},{10,202},{12,76},{14,206},{16... | collective-permute-start | bytes 196616 | tf_op jit(solution)/shard_map/ppermute | solution.py:387
  23.2 2.9 %collective-permute-start.8 = (bf16[32,1024]{1,0:T(8,128)(2,1)S(1)}, bf16[32,1024]{1,0:T(8,128)(2,1)S(1)}, u32[]{:S(2)}, u32[]{:S(2)}) collective-permute-start(bf16[32,1024]{1,0:T(8,128)(2,1)S(1)} %get-tuple-element.64.refs_5_), channel_id=1, source_target_pairs={{0,128},{2,130},{4,132},{6,134},{8,136},{10,138},{12,140},{14,142}... | collective-permute-start | bytes 196616 | tf_op jit(solution)/shard_map/ppermute | solution.py:387
  26.1 1.0 %collective-permute-done.7.refs_6_ = bf16[32,1024]{1,0:T(8,128)(2,1)S(1)} collective-permute-done((bf16[32,1024]{1,0:T(8,128)(2,1)S(1)}, bf16[32,1024]{1,0:T(8,128)(2,1)S(1)}, u32[]{:S(2)}, u32[]{:S(2)}) %collective-permute-start.7) | collective-permute-done | bytes 65568 | tf_op jit(solution)/shard_map/ppermute | solution.py:387
  27.1 0.0 collective-permute-start.9
  27.1 1.6 %local_sent_3.1 = (f32[1024,128]{1,0:T(8,128)S(1)}, f32[1024,128]{1,0:T(8,128)S(1)}) custom-call(s32[1]{0:T(128)S(6)} %sub.2.part_id.ids, bf16[3,256,1024]{2,1,0:T(8,128)(2,1)} %bitcast.28, f32[3,3,1024]{2,1,0:T(4,128)S(1)} %copy-done.1, f32[2048,128]{1,0:T(8,128)S(1)} %get-tuple-element.81.gate_ref, ...), custom_call_target="tpu_custom_call", output_to_operand_aliasing={{0}: (8, {}), {1}: (9, {})} | custom-call | tf_op jit(solution)/shard_map/local_sent_3/pallas_call | solution.py:463
  28.6 1.0 %collective-permute-done.8.refs_7_ = bf16[32,1024]{1,0:T(8,128)(2,1)S(1)} collective-permute-done((bf16[32,1024]{1,0:T(8,128)(2,1)S(1)}, bf16[32,1024]{1,0:T(8,128)(2,1)S(1)}, u32[]{:S(2)}, u32[]{:S(2)}) %collective-permute-start.8) | collective-permute-done | bytes 65568 | tf_op jit(solution)/shard_map/ppermute | solution.py:387
  29.6 0.0 collective-permute-done.9.refs_8_
  29.6 0.3 join_3.1
  30.0 0.9 %finish_sent.1 = bf16[128,1024]{1,0:T(8,128)(2,1)S(1)} custom-call(s32[1]{0:T(128)S(6)} %sub.2.part_id.ids, f32[1024,128]{1,0:T(8,128)S(1)} %get-tuple-element.71.query_ref, f32[1024,128]{1,0:T(8,128)S(1)} %get-tuple-element.72.local_ref, f32[16,1024]{1,0:T(8,128)S(1)} %get-tuple-element.84.prefix_ref, f32[8,1024]{1,0:T(8,128)S(1)} %get-tuple-element.80.past_ref, ...), custom_call_target="tpu_custom_call" | custom-call | tf_op jit(solution)/shard_map/finish_sent/pallas_call | solution.py:578
  30.8 5.5 %collective-permute-start.10 = (bf16[128,1024]{1,0:T(8,128)(2,1)S(1)}, bf16[128,1024]{1,0:T(8,128)(2,1)S(1)}, u32[]{:S(2)}, u32[]{:S(2)}) collective-permute-start(bf16[128,1024]{1,0:T(8,128)(2,1)S(1)} %finish_sent.1), channel_id=1, source_target_pairs={{0,1},{1,0},{2,3},{3,2},{4,5},{5,4},{6,7},{7,6},{8,9},{9,8},{10,11... | collective-permute-start | bytes 786440 | tf_op jit(solution)/shard_map/ppermute | solution.py:587
  36.4 0.1 pad_add_fusion.ids
  36.4 2.6 %local_own.1 = (f32[1024,128]{1,0:T(8,128)S(1)}, f32[1024,128]{1,0:T(8,128)S(1)}) custom-call(s32[1]{0:T(128)} %bitcast.part_id, bf16[3,256,1024]{2,1,0:T(8,128)(2,1)} %bitcast.29, f32[3,3,1024]{2,1,0:T(4,128)S(1)} %copy-done.1, f32[2048,128]{1,0:T(8,128)S(1)} %get-tuple-element.81.gate_ref, f32[8,2,128,128]{3,2,1,0:T(8,128)S(1)} %get-tuple-element.57.ends_ref, ...), custom_call_target="tpu_custom_call" | custom-call | tf_op jit(solution)/shard_map/local_own/pallas_call | solution.py:463
  39.1 2.7 %finish_own.1.held_ref = bf16[128,2048]{1,0:T(8,128)(2,1)} custom-call(s32[2]{0:T(128)S(1)} %pad_add_fusion.ids, f32[1024,128]{1,0:T(8,128)S(1)} %get-tuple-element.82.query_ref, f32[1024,128]{1,0:T(8,128)S(1)} %get-tuple-element.83.local_ref, f32[16,1024]{1,0:T(8,128)S(1)} %get-tuple-element.84.prefix_ref, f32[8,1024]{1,0:T(8,128)S(1)} %get-tuple-element.80.past_ref, ...), custom_call_target="tpu_custom_call" | custom-call | tf_op jit(solution)/shard_map/finish_own/pallas_call | solution.py:541
  41.7 7.0 %collective-permute-done.10.far_ref = bf16[128,1024]{1,0:T(8,128)(2,1)S(1)} collective-permute-done((bf16[128,1024]{1,0:T(8,128)(2,1)S(1)}, bf16[128,1024]{1,0:T(8,128)(2,1)S(1)}, u32[]{:S(2)}, u32[]{:S(2)}) %collective-permute-start.10) | collective-permute-done | bytes 262176 | tf_op jit(solution)/shard_map/ppermute | solution.py:587
  48.7 0.7 %place.1 = bf16[128,2048]{1,0:T(8,128)(2,1)} custom-call(s32[1]{0:T(128)S(6)} %sub.2.part_id.ids, bf16[128,1024]{1,0:T(8,128)(2,1)S(1)} %collective-permute-done.10.far_ref, bf16[128,2048]{1,0:T(8,128)(2,1)} %finish_own.1.held_ref), custom_call_target="tpu_custom_call", output_to_operand_aliasing={{}: (2, {})} | custom-call | tf_op jit(solution)/shard_map/place/pallas_call | solution.py:591
  (2 shorter events, 0.0 us)
Async XLA Ops:
  0.0 5.1 %copy-start = (f32[1024,16]{0,1:T(8,128)S(1)}, f32[1024,16]{0,1:T(8,128)}, u32[]{:S(2)}) copy-start(f32[1024,16]{0,1:T(8,128)} %param.8) | copy-start | bytes 196612
  0.0 5.1 %copy-start.1 = (f32[3,3,1024]{2,1,0:T(4,128)S(1)}, f32[3,3,1024]{2,1,0:T(4,128)}, u32[]{:S(2)}) copy-start(f32[3,3,1024]{2,1,0:T(4,128)} %taps_ref.9) | copy-start | bytes 110596
  0.0 18.7 %copy-start.2 = (f32[1024,16]{0,1:T(8,128)S(1)}, f32[1024,16]{0,1:T(8,128)}, u32[]{:S(2)}) copy-start(f32[1024,16]{0,1:T(8,128)} %param.7) | copy-start | bytes 196612
  0.0 18.7 %copy-start.3 = (f32[1024]{0:T(1024)S(1)}, f32[1024]{0:T(1024)}, u32[]{:S(2)}) copy-start(f32[1024]{0:T(1024)} %param.9) | copy-start | bytes 12292
  3.8 1.3 %collective-permute-start = (bf16[32,1024]{1,0:T(8,128)(2,1)S(1)}, bf16[32,1024]{1,0:T(8,128)(2,1)S(1)}, u32[]{:S(2)}, u32[]{:S(2)}) collective-permute-start(bf16[32,1024]{1,0:T(8,128)(2,1)S(1)} %get-tuple-element.47.refs_5_.sum_ref), channel_id=1, source_target_pairs={{0,2},{2,0},{4,6},{6,4},{8,10},{10,8},{12,14},{14,12},{16,18},{18,... | collective-permute-start | bytes 196616 | tf_op jit(solution)/shard_map/ppermute | solution.py:387
  5.3 5.8 %collective-permute-start.1 = (bf16[32,1024]{1,0:T(8,128)(2,1)S(1)}, bf16[32,1024]{1,0:T(8,128)(2,1)S(1)}, u32[]{:S(2)}, u32[]{:S(2)}) collective-permute-start(bf16[32,1024]{1,0:T(8,128)(2,1)S(1)} %get-tuple-element.51.refs_5_), channel_id=1, source_target_pairs={{0,4},{2,14},{4,8},{6,2},{8,12},{10,6},{12,0},{14,10},{16,20},{18,... | collective-permute-start | bytes 196616 | tf_op jit(solution)/shard_map/ppermute | solution.py:387
  6.3 6.4 %collective-permute-start.2 = (bf16[32,1024]{1,0:T(8,128)(2,1)S(1)}, bf16[32,1024]{1,0:T(8,128)(2,1)S(1)}, u32[]{:S(2)}, u32[]{:S(2)}) collective-permute-start(bf16[32,1024]{1,0:T(8,128)(2,1)S(1)} %get-tuple-element.51.refs_5_), channel_id=1, source_target_pairs={{0,8},{2,10},{4,12},{6,14},{8,0},{10,2},{12,4},{14,6},{16,24},{18,... | collective-permute-start | bytes 196616 | tf_op jit(solution)/shard_map/ppermute | solution.py:387
  11.1 1.7 %collective-permute-start.3 = (bf16[32,1024]{1,0:T(8,128)(2,1)S(1)}, bf16[32,1024]{1,0:T(8,128)(2,1)S(1)}, u32[]{:S(2)}, u32[]{:S(2)}) collective-permute-start(bf16[32,1024]{1,0:T(8,128)(2,1)S(1)} %collective-permute-done.1.refs_6_), channel_id=1, source_target_pairs={{0,2},{2,0},{4,6},{6,4},{8,10},{10,8},{12,14},{14,12},{16,18},{18,... | collective-permute-start | bytes 196616 | tf_op jit(solution)/shard_map/ppermute | solution.py:393
  13.2 5.6 %collective-permute-start.4 = (bf16[32,1024]{1,0:T(8,128)(2,1)S(1)}, bf16[32,1024]{1,0:T(8,128)(2,1)S(1)}, u32[]{:S(2)}, u32[]{:S(2)}) collective-permute-start(bf16[32,1024]{1,0:T(8,128)(2,1)S(1)} %get-tuple-element.52.refs_5_), channel_id=1, source_target_pairs={{0,16},{2,50},{4,20},{6,54},{8,24},{10,58},{12,28},{14,62},{16,32}... | collective-permute-start | bytes 196616 | tf_op jit(solution)/shard_map/ppermute | solution.py:387
  14.7 6.4 %collective-permute-start.5 = (bf16[32,1024]{1,0:T(8,128)(2,1)S(1)}, bf16[32,1024]{1,0:T(8,128)(2,1)S(1)}, u32[]{:S(2)}, u32[]{:S(2)}) collective-permute-start(bf16[32,1024]{1,0:T(8,128)(2,1)S(1)} %get-tuple-element.52.refs_5_), channel_id=1, source_target_pairs={{0,32},{2,34},{4,36},{6,38},{8,40},{10,42},{12,44},{14,46},{16,48}... | collective-permute-start | bytes 196616 | tf_op jit(solution)/shard_map/ppermute | solution.py:387
  18.7 2.4 %collective-permute-start.6 = (bf16[32,1024]{1,0:T(8,128)(2,1)S(1)}, bf16[32,1024]{1,0:T(8,128)(2,1)S(1)}, u32[]{:S(2)}, u32[]{:S(2)}) collective-permute-start(bf16[32,1024]{1,0:T(8,128)(2,1)S(1)} %collective-permute-done.4.refs_6_), channel_id=1, source_target_pairs={{0,2},{2,0},{4,6},{6,4},{8,10},{10,8},{12,14},{14,12},{16,18},{18,... | collective-permute-start | bytes 196616 | tf_op jit(solution)/shard_map/ppermute | solution.py:393
  21.5 5.6 %collective-permute-start.7 = (bf16[32,1024]{1,0:T(8,128)(2,1)S(1)}, bf16[32,1024]{1,0:T(8,128)(2,1)S(1)}, u32[]{:S(2)}, u32[]{:S(2)}) collective-permute-start(bf16[32,1024]{1,0:T(8,128)(2,1)S(1)} %get-tuple-element.64.refs_5_), channel_id=1, source_target_pairs={{0,64},{2,194},{4,68},{6,198},{8,72},{10,202},{12,76},{14,206},{16... | collective-permute-start | bytes 196616 | tf_op jit(solution)/shard_map/ppermute | solution.py:387
  23.2 6.5 %collective-permute-start.8 = (bf16[32,1024]{1,0:T(8,128)(2,1)S(1)}, bf16[32,1024]{1,0:T(8,128)(2,1)S(1)}, u32[]{:S(2)}, u32[]{:S(2)}) collective-permute-start(bf16[32,1024]{1,0:T(8,128)(2,1)S(1)} %get-tuple-element.64.refs_5_), channel_id=1, source_target_pairs={{0,128},{2,130},{4,132},{6,134},{8,136},{10,138},{12,140},{14,142}... | collective-permute-start | bytes 196616 | tf_op jit(solution)/shard_map/ppermute | solution.py:387
  27.1 2.6 %collective-permute-start.9 = (bf16[32,1024]{1,0:T(8,128)(2,1)S(1)}, bf16[32,1024]{1,0:T(8,128)(2,1)S(1)}, u32[]{:S(2)}, u32[]{:S(2)}) collective-permute-start(bf16[32,1024]{1,0:T(8,128)(2,1)S(1)} %collective-permute-done.7.refs_6_), channel_id=1, source_target_pairs={{0,2},{2,0},{4,6},{6,4},{8,10},{10,8},{12,14},{14,12},{16,18},{18,... | collective-permute-start | bytes 196616 | tf_op jit(solution)/shard_map/ppermute | solution.py:393
  30.8 17.9 %collective-permute-start.10 = (bf16[128,1024]{1,0:T(8,128)(2,1)S(1)}, bf16[128,1024]{1,0:T(8,128)(2,1)S(1)}, u32[]{:S(2)}, u32[]{:S(2)}) collective-permute-start(bf16[128,1024]{1,0:T(8,128)(2,1)S(1)} %finish_sent.1), channel_id=1, source_target_pairs={{0,1},{1,0},{2,3},{3,2},{4,5},{5,4},{6,7},{7,6},{8,9},{9,8},{10,11... | collective-permute-start | bytes 786440 | tf_op jit(solution)/shard_map/ppermute | solution.py:587

commit v6 on v5

--- a/solution.py
+++ b/solution.py
@@ -417,6 +417,9 @@
     steps = width // tile
     tiles = tile // LANES
     all_tiles = width // LANES
+    wide_tile = 512 if width % 512 == 0 else tile
+    wide_steps = width // wide_tile
+    wide_tiles = wide_tile // LANES
 
     x = jnp.transpose(streams, (1, 0, 2))
     rates = decay_rate.T
@@ -432,9 +435,14 @@
     ends_spec = pl.BlockSpec((tiles, 2, modes * SUB, LANES), lambda i, *_: (i, 0, 0, 0))
     gate, ends, state, summary = pl.pallas_call(
         state_kernel,
-        grid=(steps,),
+        grid=(wide_steps,),
         in_specs=[in_hbm] * 3,
-        out_specs=[tall(toks), ends_spec, strip(modes), strip(modes + PAIR)],
+        out_specs=[
+            pl.BlockSpec((wide_tiles * toks, LANES), lambda i: (i, 0)),
+            pl.BlockSpec((wide_tiles, 2, modes * SUB, LANES), lambda i: (i, 0, 0, 0)),
+            pl.BlockSpec((modes, wide_tile), lambda i: (0, i)),
+            pl.BlockSpec((modes + PAIR, wide_tile), lambda i: (0, i)),
+        ],
         out_shape=[
             jax.ShapeDtypeStruct((all_tiles * toks, LANES), F32),
             jax.ShapeDtypeStruct((all_tiles, 2, modes * SUB, LANES), F32),
@@ -442,14 +450,14 @@
             jax.ShapeDtypeStruct((modes + PAIR, width), BF16),
         ],
         scratch_shapes=[
-            pltpu.VMEM((steps, 2, toks, tile), BF16),
-            pltpu.VMEM((steps, 2, PAIR, tile), BF16),
+            pltpu.VMEM((wide_steps, 2, toks, wide_tile), BF16),
+            pltpu.VMEM((wide_steps, 2, PAIR, wide_tile), BF16),
             pltpu.VMEM((2, toks + SUB, LANES), F32),
-            pltpu.VMEM((modes, tile), F32),
-            pltpu.VMEM((modes, tile), F32),
+            pltpu.VMEM((modes, wide_tile), F32),
+            pltpu.VMEM((modes, wide_tile), F32),
             pltpu.VMEM((rim + 1, 3, width), F32),
             pltpu.VMEM((modes, width), F32),
-            pltpu.SemaphoreType.DMA((3, steps)),
+            pltpu.SemaphoreType.DMA((3, wide_steps)),
             pltpu.SemaphoreType.DMA((2,)),
         ],
         compiler_params=params,

time: 49.6 us -> 49.3 us (level)
  no operation moved by 1% of the time
where the time goes in v6:
time: 49.3 us; the launch traced here: 49.2 us
  waiting for transfers between devices  18 us (37%)
  starting transfers between devices  16.1 us (33%)
  Pallas kernels  14.8 us (30%)
    ppermute x7, waiting for transfers between devices, send(): return lax.ppermute(value, 'ctx', route(hop))  11 us
    ppermute x7, starting transfers between devices, send(): return lax.ppermute(value, 'ctx', route(hop))  10.6 us
    ppermute x1, waiting for transfers between devices, shards(): far = lax.ppermute(sent, 'chan', [(0, 1), (1, 0)])  6.96 us
    pallas_call x3, Pallas kernels, local(): pl.pallas_call(functools.partial(local_kernel, first), grid_spec=pltpu.Pr...  5.73 us
    ppermute x1, starting transfers between devices, shards(): far = lax.ppermute(sent, 'chan', [(0, 1), (1, 0)])  5.53 us
    pallas_call x1, Pallas kernels, shards(): pl.pallas_call(state_kernel, grid=(wide_steps,), in_specs=[in_hbm] * 3, o...  3.52 us
    pallas_call x1, Pallas kernels, finish(): pl.pallas_call(finish_kernel, grid_spec=pltpu.PrefetchScalarGridSpec(num_...  2.68 us
    pallas_call x4, Pallas kernels, shards(): pl.pallas_call(body, in_specs=[pl.BlockSpec(memory_space=pltpu.SMEM)] + [...  1.31 us
  transfers between devices with their start and end apart: 11, of which 8 were waited for; matrix products, arithmetic and copies ran while one was open for 0% of the time, Pallas kernels for 17%

profile of v6, /device:TPU:96, one launch (start us, length us, event | category | flops | bytes accessed | tf_op | source)
XLA Modules:
  0.0 49.2 jit_solution(15869108071091801852)
XLA Ops:
  0.0 0.0 copy-start
  0.0 0.0 copy-start.1
  0.0 0.0 copy-start.2
  0.0 0.0 copy-start.3
  0.0 3.5 %states.1 = (f32[2048,128]{1,0:T(8,128)S(1)}, f32[8,2,128,128]{3,2,1,0:T(8,128)S(1)}, f32[16,1024]{1,0:T(8,128)S(1)}, bf16[32,1024]{1,0:T(8,128)(2,1)S(1)}) custom-call(bf16[3,256,1024]{2,1,0:T(8,128)(2,1)} %bitcast.26, f32[3,3,1024]{2,1,0:T(4,128)} %taps_ref.9, f32[16,1024]{1,0:T(8,128)} %bitcast.6), custom_call_target="tpu_custom_call" | custom-call | tf_op jit(solution)/shard_map/states/pallas_call | solution.py:436
  3.5 0.1 collective-permute-start
  3.7 1.2 %collective-permute-done.refs_6_ = bf16[32,1024]{1,0:T(8,128)(2,1)S(1)} collective-permute-done((bf16[32,1024]{1,0:T(8,128)(2,1)S(1)}, bf16[32,1024]{1,0:T(8,128)(2,1)S(1)}, u32[]{:S(2)}, u32[]{:S(2)}) %collective-permute-start) | collective-permute-done | bytes 65568 | tf_op jit(solution)/shard_map/ppermute | solution.py:387
  4.9 0.0 copy-done
  4.9 0.0 copy-done.1
  4.9 0.2 join_0.1
  5.1 1.0 %collective-permute-start.1 = (bf16[32,1024]{1,0:T(8,128)(2,1)S(1)}, bf16[32,1024]{1,0:T(8,128)(2,1)S(1)}, u32[]{:S(2)}, u32[]{:S(2)}) collective-permute-start(bf16[32,1024]{1,0:T(8,128)(2,1)S(1)} %get-tuple-element.51.refs_5_), channel_id=1, source_target_pairs={{0,4},{2,14},{4,8},{6,2},{8,12},{10,6},{12,0},{14,10},{16,20},{18,... | collective-permute-start | bytes 196616 | tf_op jit(solution)/shard_map/ppermute | solution.py:387
  6.1 0.7 %collective-permute-start.2 = (bf16[32,1024]{1,0:T(8,128)(2,1)S(1)}, bf16[32,1024]{1,0:T(8,128)(2,1)S(1)}, u32[]{:S(2)}, u32[]{:S(2)}) collective-permute-start(bf16[32,1024]{1,0:T(8,128)(2,1)S(1)} %get-tuple-element.51.refs_5_), channel_id=1, source_target_pairs={{0,8},{2,10},{4,12},{6,14},{8,0},{10,2},{12,4},{14,6},{16,24},{18,... | collective-permute-start | bytes 196616 | tf_op jit(solution)/shard_map/ppermute | solution.py:387
  6.7 4.1 %collective-permute-done.1.refs_6_ = bf16[32,1024]{1,0:T(8,128)(2,1)S(1)} collective-permute-done((bf16[32,1024]{1,0:T(8,128)(2,1)S(1)}, bf16[32,1024]{1,0:T(8,128)(2,1)S(1)}, u32[]{:S(2)}, u32[]{:S(2)}) %collective-permute-start.1) | collective-permute-done | bytes 65568 | tf_op jit(solution)/shard_map/ppermute | solution.py:387
  10.9 0.0 collective-permute-start.3
  10.9 1.7 %collective-permute-done.2.refs_7_ = bf16[32,1024]{1,0:T(8,128)(2,1)S(1)} collective-permute-done((bf16[32,1024]{1,0:T(8,128)(2,1)S(1)}, bf16[32,1024]{1,0:T(8,128)(2,1)S(1)}, u32[]{:S(2)}, u32[]{:S(2)}) %collective-permute-start.2) | collective-permute-done | bytes 65568 | tf_op jit(solution)/shard_map/ppermute | solution.py:387
  12.5 0.0 collective-permute-done.3.refs_8_
  12.5 0.4 join_1.1
  12.9 1.6 %collective-permute-start.4 = (bf16[32,1024]{1,0:T(8,128)(2,1)S(1)}, bf16[32,1024]{1,0:T(8,128)(2,1)S(1)}, u32[]{:S(2)}, u32[]{:S(2)}) collective-permute-start(bf16[32,1024]{1,0:T(8,128)(2,1)S(1)} %get-tuple-element.52.refs_5_), channel_id=1, source_target_pairs={{0,16},{2,50},{4,20},{6,54},{8,24},{10,58},{12,28},{14,62},{16,32}... | collective-permute-start | bytes 196616 | tf_op jit(solution)/shard_map/ppermute | solution.py:387
  14.5 2.7 %collective-permute-start.5 = (bf16[32,1024]{1,0:T(8,128)(2,1)S(1)}, bf16[32,1024]{1,0:T(8,128)(2,1)S(1)}, u32[]{:S(2)}, u32[]{:S(2)}) collective-permute-start(bf16[32,1024]{1,0:T(8,128)(2,1)S(1)} %get-tuple-element.52.refs_5_), channel_id=1, source_target_pairs={{0,32},{2,34},{4,36},{6,38},{8,40},{10,42},{12,44},{14,46},{16,48}... | collective-permute-start | bytes 196616 | tf_op jit(solution)/shard_map/ppermute | solution.py:387
  17.2 1.3 %collective-permute-done.4.refs_6_ = bf16[32,1024]{1,0:T(8,128)(2,1)S(1)} collective-permute-done((bf16[32,1024]{1,0:T(8,128)(2,1)S(1)}, bf16[32,1024]{1,0:T(8,128)(2,1)S(1)}, u32[]{:S(2)}, u32[]{:S(2)}) %collective-permute-start.4) | collective-permute-done | bytes 65568 | tf_op jit(solution)/shard_map/ppermute | solution.py:387
  18.5 0.0 collective-permute-start.6
  18.5 0.0 copy-done.2
  18.5 0.0 copy-done.3
  18.5 1.6 %local_sent_2.1 = (f32[1024,128]{1,0:T(8,128)S(1)}, f32[1024,128]{1,0:T(8,128)S(1)}) custom-call(s32[1]{0:T(128)S(6)} %sub.2.part_id.ids, bf16[3,256,1024]{2,1,0:T(8,128)(2,1)} %bitcast.27, f32[3,3,1024]{2,1,0:T(4,128)S(1)} %copy-done.1, f32[2048,128]{1,0:T(8,128)S(1)} %get-tuple-element.81.gate_ref, f32[8,2,128,128]{3,2,1,0:T(8,128)S(1)} %get-tuple-element.57.ends_ref, ...), custom_call_target="tpu_custom_call" | custom-call | tf_op jit(solution)/shard_map/local_sent_2/pallas_call | solution.py:471
  20.1 0.8 %collective-permute-done.5.refs_7_ = bf16[32,1024]{1,0:T(8,128)(2,1)S(1)} collective-permute-done((bf16[32,1024]{1,0:T(8,128)(2,1)S(1)}, bf16[32,1024]{1,0:T(8,128)(2,1)S(1)}, u32[]{:S(2)}, u32[]{:S(2)}) %collective-permute-start.5) | collective-permute-done | bytes 65568 | tf_op jit(solution)/shard_map/ppermute | solution.py:387
  20.9 0.0 collective-permute-done.6.refs_8_
  20.9 0.4 join_2.1
  21.3 1.7 %collective-permute-start.7 = (bf16[32,1024]{1,0:T(8,128)(2,1)S(1)}, bf16[32,1024]{1,0:T(8,128)(2,1)S(1)}, u32[]{:S(2)}, u32[]{:S(2)}) collective-permute-start(bf16[32,1024]{1,0:T(8,128)(2,1)S(1)} %get-tuple-element.64.refs_5_), channel_id=1, source_target_pairs={{0,64},{2,194},{4,68},{6,198},{8,72},{10,202},{12,76},{14,206},{16... | collective-permute-start | bytes 196616 | tf_op jit(solution)/shard_map/ppermute | solution.py:387
  23.0 2.9 %collective-permute-start.8 = (bf16[32,1024]{1,0:T(8,128)(2,1)S(1)}, bf16[32,1024]{1,0:T(8,128)(2,1)S(1)}, u32[]{:S(2)}, u32[]{:S(2)}) collective-permute-start(bf16[32,1024]{1,0:T(8,128)(2,1)S(1)} %get-tuple-element.64.refs_5_), channel_id=1, source_target_pairs={{0,128},{2,130},{4,132},{6,134},{8,136},{10,138},{12,140},{14,142}... | collective-permute-start | bytes 196616 | tf_op jit(solution)/shard_map/ppermute | solution.py:387
  25.9 1.0 %collective-permute-done.7.refs_6_ = bf16[32,1024]{1,0:T(8,128)(2,1)S(1)} collective-permute-done((bf16[32,1024]{1,0:T(8,128)(2,1)S(1)}, bf16[32,1024]{1,0:T(8,128)(2,1)S(1)}, u32[]{:S(2)}, u32[]{:S(2)}) %collective-permute-start.7) | collective-permute-done | bytes 65568 | tf_op jit(solution)/shard_map/ppermute | solution.py:387
  26.9 0.0 collective-permute-start.9
  26.9 1.6 %local_sent_3.1 = (f32[1024,128]{1,0:T(8,128)S(1)}, f32[1024,128]{1,0:T(8,128)S(1)}) custom-call(s32[1]{0:T(128)S(6)} %sub.2.part_id.ids, bf16[3,256,1024]{2,1,0:T(8,128)(2,1)} %bitcast.28, f32[3,3,1024]{2,1,0:T(4,128)S(1)} %copy-done.1, f32[2048,128]{1,0:T(8,128)S(1)} %get-tuple-element.81.gate_ref, ...), custom_call_target="tpu_custom_call", output_to_operand_aliasing={{0}: (8, {}), {1}: (9, {})} | custom-call | tf_op jit(solution)/shard_map/local_sent_3/pallas_call | solution.py:471
  28.4 1.0 %collective-permute-done.8.refs_7_ = bf16[32,1024]{1,0:T(8,128)(2,1)S(1)} collective-permute-done((bf16[32,1024]{1,0:T(8,128)(2,1)S(1)}, bf16[32,1024]{1,0:T(8,128)(2,1)S(1)}, u32[]{:S(2)}, u32[]{:S(2)}) %collective-permute-start.8) | collective-permute-done | bytes 65568 | tf_op jit(solution)/shard_map/ppermute | solution.py:387
  29.4 0.0 collective-permute-done.9.refs_8_
  29.4 0.3 join_3.1
  29.7 0.9 %finish_sent.1 = bf16[128,1024]{1,0:T(8,128)(2,1)S(1)} custom-call(s32[1]{0:T(128)S(6)} %sub.2.part_id.ids, f32[1024,128]{1,0:T(8,128)S(1)} %get-tuple-element.71.query_ref, f32[1024,128]{1,0:T(8,128)S(1)} %get-tuple-element.72.local_ref, f32[16,1024]{1,0:T(8,128)S(1)} %get-tuple-element.84.prefix_ref, f32[8,1024]{1,0:T(8,128)S(1)} %get-tuple-element.80.past_ref, ...), custom_call_target="tpu_custom_call" | custom-call | tf_op jit(solution)/shard_map/finish_sent/pallas_call | solution.py:586
  30.6 5.5 %collective-permute-start.10 = (bf16[128,1024]{1,0:T(8,128)(2,1)S(1)}, bf16[128,1024]{1,0:T(8,128)(2,1)S(1)}, u32[]{:S(2)}, u32[]{:S(2)}) collective-permute-start(bf16[128,1024]{1,0:T(8,128)(2,1)S(1)} %finish_sent.1), channel_id=1, source_target_pairs={{0,1},{1,0},{2,3},{3,2},{4,5},{5,4},{6,7},{7,6},{8,9},{9,8},{10,11... | collective-permute-start | bytes 786440 | tf_op jit(solution)/shard_map/ppermute | solution.py:595
  36.2 0.1 pad_add_fusion.ids
  36.2 2.6 %local_own.1 = (f32[1024,128]{1,0:T(8,128)S(1)}, f32[1024,128]{1,0:T(8,128)S(1)}) custom-call(s32[1]{0:T(128)} %bitcast.part_id, bf16[3,256,1024]{2,1,0:T(8,128)(2,1)} %bitcast.29, f32[3,3,1024]{2,1,0:T(4,128)S(1)} %copy-done.1, f32[2048,128]{1,0:T(8,128)S(1)} %get-tuple-element.81.gate_ref, f32[8,2,128,128]{3,2,1,0:T(8,128)S(1)} %get-tuple-element.57.ends_ref, ...), custom_call_target="tpu_custom_call" | custom-call | tf_op jit(solution)/shard_map/local_own/pallas_call | solution.py:471
  38.8 2.7 %finish_own.1.held_ref = bf16[128,2048]{1,0:T(8,128)(2,1)} custom-call(s32[2]{0:T(128)S(1)} %pad_add_fusion.ids, f32[1024,128]{1,0:T(8,128)S(1)} %get-tuple-element.82.query_ref, f32[1024,128]{1,0:T(8,128)S(1)} %get-tuple-element.83.local_ref, f32[16,1024]{1,0:T(8,128)S(1)} %get-tuple-element.84.prefix_ref, f32[8,1024]{1,0:T(8,128)S(1)} %get-tuple-element.80.past_ref, ...), custom_call_target="tpu_custom_call" | custom-call | tf_op jit(solution)/shard_map/finish_own/pallas_call | solution.py:549
  41.5 7.0 %collective-permute-done.10.far_ref = bf16[128,1024]{1,0:T(8,128)(2,1)S(1)} collective-permute-done((bf16[128,1024]{1,0:T(8,128)(2,1)S(1)}, bf16[128,1024]{1,0:T(8,128)(2,1)S(1)}, u32[]{:S(2)}, u32[]{:S(2)}) %collective-permute-start.10) | collective-permute-done | bytes 262176 | tf_op jit(solution)/shard_map/ppermute | solution.py:595
  48.5 0.7 %place.1 = bf16[128,2048]{1,0:T(8,128)(2,1)} custom-call(s32[1]{0:T(128)S(6)} %sub.2.part_id.ids, bf16[128,1024]{1,0:T(8,128)(2,1)S(1)} %collective-permute-done.10.far_ref, bf16[128,2048]{1,0:T(8,128)(2,1)} %finish_own.1.held_ref), custom_call_target="tpu_custom_call", output_to_operand_aliasing={{}: (2, {})} | custom-call | tf_op jit(solution)/shard_map/place/pallas_call | solution.py:599
  (2 shorter events, 0.0 us)
Async XLA Ops:
  0.0 4.9 %copy-start = (f32[1024,16]{0,1:T(8,128)S(1)}, f32[1024,16]{0,1:T(8,128)}, u32[]{:S(2)}) copy-start(f32[1024,16]{0,1:T(8,128)} %param.8) | copy-start | bytes 196612
  0.0 4.9 %copy-start.1 = (f32[3,3,1024]{2,1,0:T(4,128)S(1)}, f32[3,3,1024]{2,1,0:T(4,128)}, u32[]{:S(2)}) copy-start(f32[3,3,1024]{2,1,0:T(4,128)} %taps_ref.9) | copy-start | bytes 110596
  0.0 18.5 %copy-start.2 = (f32[1024,16]{0,1:T(8,128)S(1)}, f32[1024,16]{0,1:T(8,128)}, u32[]{:S(2)}) copy-start(f32[1024,16]{0,1:T(8,128)} %param.7) | copy-start | bytes 196612
  0.0 18.5 %copy-start.3 = (f32[1024]{0:T(1024)S(1)}, f32[1024]{0:T(1024)}, u32[]{:S(2)}) copy-start(f32[1024]{0:T(1024)} %param.9) | copy-start | bytes 12292
  3.5 1.3 %collective-permute-start = (bf16[32,1024]{1,0:T(8,128)(2,1)S(1)}, bf16[32,1024]{1,0:T(8,128)(2,1)S(1)}, u32[]{:S(2)}, u32[]{:S(2)}) collective-permute-start(bf16[32,1024]{1,0:T(8,128)(2,1)S(1)} %get-tuple-element.47.refs_5_.sum_ref), channel_id=1, source_target_pairs={{0,2},{2,0},{4,6},{6,4},{8,10},{10,8},{12,14},{14,12},{16,18},{18,... | collective-permute-start | bytes 196616 | tf_op jit(solution)/shard_map/ppermute | solution.py:387
  5.1 5.8 %collective-permute-start.1 = (bf16[32,1024]{1,0:T(8,128)(2,1)S(1)}, bf16[32,1024]{1,0:T(8,128)(2,1)S(1)}, u32[]{:S(2)}, u32[]{:S(2)}) collective-permute-start(bf16[32,1024]{1,0:T(8,128)(2,1)S(1)} %get-tuple-element.51.refs_5_), channel_id=1, source_target_pairs={{0,4},{2,14},{4,8},{6,2},{8,12},{10,6},{12,0},{14,10},{16,20},{18,... | collective-permute-start | bytes 196616 | tf_op jit(solution)/shard_map/ppermute | solution.py:387
  6.1 6.4 %collective-permute-start.2 = (bf16[32,1024]{1,0:T(8,128)(2,1)S(1)}, bf16[32,1024]{1,0:T(8,128)(2,1)S(1)}, u32[]{:S(2)}, u32[]{:S(2)}) collective-permute-start(bf16[32,1024]{1,0:T(8,128)(2,1)S(1)} %get-tuple-element.51.refs_5_), channel_id=1, source_target_pairs={{0,8},{2,10},{4,12},{6,14},{8,0},{10,2},{12,4},{14,6},{16,24},{18,... | collective-permute-start | bytes 196616 | tf_op jit(solution)/shard_map/ppermute | solution.py:387
  10.9 1.7 %collective-permute-start.3 = (bf16[32,1024]{1,0:T(8,128)(2,1)S(1)}, bf16[32,1024]{1,0:T(8,128)(2,1)S(1)}, u32[]{:S(2)}, u32[]{:S(2)}) collective-permute-start(bf16[32,1024]{1,0:T(8,128)(2,1)S(1)} %collective-permute-done.1.refs_6_), channel_id=1, source_target_pairs={{0,2},{2,0},{4,6},{6,4},{8,10},{10,8},{12,14},{14,12},{16,18},{18,... | collective-permute-start | bytes 196616 | tf_op jit(solution)/shard_map/ppermute | solution.py:393
  12.9 5.6 %collective-permute-start.4 = (bf16[32,1024]{1,0:T(8,128)(2,1)S(1)}, bf16[32,1024]{1,0:T(8,128)(2,1)S(1)}, u32[]{:S(2)}, u32[]{:S(2)}) collective-permute-start(bf16[32,1024]{1,0:T(8,128)(2,1)S(1)} %get-tuple-element.52.refs_5_), channel_id=1, source_target_pairs={{0,16},{2,50},{4,20},{6,54},{8,24},{10,58},{12,28},{14,62},{16,32}... | collective-permute-start | bytes 196616 | tf_op jit(solution)/shard_map/ppermute | solution.py:387
  14.5 6.4 %collective-permute-start.5 = (bf16[32,1024]{1,0:T(8,128)(2,1)S(1)}, bf16[32,1024]{1,0:T(8,128)(2,1)S(1)}, u32[]{:S(2)}, u32[]{:S(2)}) collective-permute-start(bf16[32,1024]{1,0:T(8,128)(2,1)S(1)} %get-tuple-element.52.refs_5_), channel_id=1, source_target_pairs={{0,32},{2,34},{4,36},{6,38},{8,40},{10,42},{12,44},{14,46},{16,48}... | collective-permute-start | bytes 196616 | tf_op jit(solution)/shard_map/ppermute | solution.py:387
  18.5 2.4 %collective-permute-start.6 = (bf16[32,1024]{1,0:T(8,128)(2,1)S(1)}, bf16[32,1024]{1,0:T(8,128)(2,1)S(1)}, u32[]{:S(2)}, u32[]{:S(2)}) collective-permute-start(bf16[32,1024]{1,0:T(8,128)(2,1)S(1)} %collective-permute-done.4.refs_6_), channel_id=1, source_target_pairs={{0,2},{2,0},{4,6},{6,4},{8,10},{10,8},{12,14},{14,12},{16,18},{18,... | collective-permute-start | bytes 196616 | tf_op jit(solution)/shard_map/ppermute | solution.py:393
  21.3 5.6 %collective-permute-start.7 = (bf16[32,1024]{1,0:T(8,128)(2,1)S(1)}, bf16[32,1024]{1,0:T(8,128)(2,1)S(1)}, u32[]{:S(2)}, u32[]{:S(2)}) collective-permute-start(bf16[32,1024]{1,0:T(8,128)(2,1)S(1)} %get-tuple-element.64.refs_5_), channel_id=1, source_target_pairs={{0,64},{2,194},{4,68},{6,198},{8,72},{10,202},{12,76},{14,206},{16... | collective-permute-start | bytes 196616 | tf_op jit(solution)/shard_map/ppermute | solution.py:387
  23.0 6.5 %collective-permute-start.8 = (bf16[32,1024]{1,0:T(8,128)(2,1)S(1)}, bf16[32,1024]{1,0:T(8,128)(2,1)S(1)}, u32[]{:S(2)}, u32[]{:S(2)}) collective-permute-start(bf16[32,1024]{1,0:T(8,128)(2,1)S(1)} %get-tuple-element.64.refs_5_), channel_id=1, source_target_pairs={{0,128},{2,130},{4,132},{6,134},{8,136},{10,138},{12,140},{14,142}... | collective-permute-start | bytes 196616 | tf_op jit(solution)/shard_map/ppermute | solution.py:387
  26.9 2.6 %collective-permute-start.9 = (bf16[32,1024]{1,0:T(8,128)(2,1)S(1)}, bf16[32,1024]{1,0:T(8,128)(2,1)S(1)}, u32[]{:S(2)}, u32[]{:S(2)}) collective-permute-start(bf16[32,1024]{1,0:T(8,128)(2,1)S(1)} %collective-permute-done.7.refs_6_), channel_id=1, source_target_pairs={{0,2},{2,0},{4,6},{6,4},{8,10},{10,8},{12,14},{14,12},{16,18},{18,... | collective-permute-start | bytes 196616 | tf_op jit(solution)/shard_map/ppermute | solution.py:393
  30.6 17.9 %collective-permute-start.10 = (bf16[128,1024]{1,0:T(8,128)(2,1)S(1)}, bf16[128,1024]{1,0:T(8,128)(2,1)S(1)}, u32[]{:S(2)}, u32[]{:S(2)}) collective-permute-start(bf16[128,1024]{1,0:T(8,128)(2,1)S(1)} %finish_sent.1), channel_id=1, source_target_pairs={{0,1},{1,0},{2,3},{3,2},{4,5},{5,4},{6,7},{7,6},{8,9},{9,8},{10,11... | collective-permute-start | bytes 786440 | tf_op jit(solution)/shard_map/ppermute | solution.py:595

commit v7 on v6

--- a/solution.py
+++ b/solution.py
@@ -243,71 +243,58 @@
 
 
 def local_kernel(
-    first_strip, part_id, x_hbm, taps_ref, gate_ref, ends_ref, res_ref, rate_ref, skip_ref, *refs
+    first, part_id, x_hbm, taps_ref, gate_ref, ends_ref, res_ref, rate_ref, skip_ref, *refs
 ):
-    query_ref, local_ref, raw, wide, begins, keep_ref, gain_ref, run_ref, sems = refs[-9:]
-    step_id = pl.program_id(0)
+    query_ref, local_ref, raw, wide, begins, sem = refs[-6:]
     part = part_id[0]
-    _, toks, width = raw.shape
+    toks, width = raw.shape
     half = toks // 2
     rim = taps_ref.shape[0] - 1
     modes = rate_ref.shape[0]
     run = half // SUB
-
-    def fetch(i):
-        return pltpu.make_async_copy(
-            x_hbm.at[0, :, pl.ds(pl.multiple_of((first_strip + i) * width, LANES), width)],
-            raw.at[i],
-            sems.at[i],
-        )
-
-    @pl.when(step_id == 0)
-    def _():
-        for i in range(raw.shape[0]):
-            fetch(i).start()
-
-    rates = rate_ref[...]
-    keep_ref[...] = jnp.exp(-rates)
-    run_ref[...] = jnp.exp(-rates * run)
-    gain_ref[...] = res_ref[...] * jnp.sqrt(2.0 * rates)
-    for t, c in enumerate(range(0, width, LANES)):
-        cols = slice(c, c + LANES)
-        run_keep = run_ref[:, cols]
+    start = pl.multiple_of(part * half, half)
+    fetch = pltpu.make_async_copy(x_hbm.at[0, :, first : first + width], raw, sem)
+    fetch.start()
+    for t in range(width // LANES):
+        at = first // LANES + t
+        cols = slice(at * LANES, (at + 1) * LANES)
+        rates = rate_ref[:, cols]
+        keep_all = jnp.exp(-rates)
+        run_keep = jnp.exp(-rates * run)
+        gains = res_ref[:, cols] * jnp.sqrt(2.0 * rates)
         state = jnp.zeros((modes, LANES), F32)
         for i in range(SUB):
-            state = run_keep * state + modes_at(ends_ref.at[t, 0], i, modes)
+            state = run_keep * state + modes_at(ends_ref.at[at, 0], i, modes)
         state = jnp.where(part == 0, 0.0, state)
         for i in range(SUB):
-            put_modes_at(begins, i, state)
+            put_modes_at(begins.at[t], i, state)
             if i + 1 < SUB:
-                state = run_keep * state + modes_at(ends_ref.at[t, part], i, modes)
-        keep = [spread(keep_ref, m, cols) for m in range(modes)]
-        gains = [spread(gain_ref, m, cols) for m in range(modes)]
+                state = run_keep * state + modes_at(ends_ref.at[at, part], i, modes)
+        keep = [jnp.broadcast_to(keep_all[m : m + 1], (SUB, LANES)) for m in range(modes)]
+        gain = [jnp.broadcast_to(gains[m : m + 1], (SUB, LANES)) for m in range(modes)]
         skip = spread(skip_ref, 0, cols)
-        states = [begins[m * SUB : (m + 1) * SUB, :] for m in range(modes)]
+        states = [begins[t, m * SUB : (m + 1) * SUB, :] for m in range(modes)]
         for j in range(run):
-            now = gate_ref[pl.ds(t * toks + part * half + j, SUB, stride=run), :]
+            now = gate_ref[pl.ds(at * toks + part * half + j, SUB, stride=run), :]
             states = [k * state + now for k, state in zip(keep, states)]
-            local_ref[pl.ds(t * half + j, SUB, stride=run), :] = tree_sum(
-                [skip * now] + [gain * state for gain, state in zip(gains, states)]
+            local_ref[pl.ds(at * half + j, SUB, stride=run), :] = tree_sum(
+                [skip * now] + [g * state for g, state in zip(gain, states)]
             )
-
-    fetch(step_id).wait()
-    start = pl.multiple_of(part * half, half)
-    for t, c in enumerate(range(0, width, LANES)):
-        cols = slice(c, c + LANES)
+    fetch.wait()
+    for t in range(width // LANES):
+        at = first // LANES + t
+        near = slice(t * LANES, (t + 1) * LANES)
         for r in range(0, half, STEP):
-            wide[SUB + r : SUB + r + STEP, :] = raw[
-                step_id, pl.ds(pl.multiple_of(start + r, STEP), STEP), cols
+            wide[t, SUB + r : SUB + r + STEP, :] = raw[
+                pl.ds(pl.multiple_of(start + r, STEP), STEP), near
             ].astype(F32)
-        before = raw[step_id, half - 16 : half, cols].astype(F32)[16 - rim :]
-        wide[SUB - rim : SUB, :] = before
-        taps = tap_rows(taps_ref, 0, cols)
-        load = lambda at: wide[pl.ds(SUB + at, SUB, stride=run), :]
-        line = [load(at) for at in range(-rim, 0)]
+        wide[t, SUB - rim : SUB, :] = raw[half - PAIR : half, near].astype(F32)[PAIR - rim :]
+        taps = tap_rows(taps_ref, 0, slice(at * LANES, (at + 1) * LANES))
+        load = lambda j: wide[t, pl.ds(SUB + j, SUB, stride=run), :]
+        line = [load(j) for j in range(-rim, 0)]
         for j in range(run):
             line = line[-rim:] + [load(j)]
-            query_ref[pl.ds(t * half + j, SUB, stride=run), :] = short_conv(line, taps)
+            query_ref[pl.ds(at * half + j, SUB, stride=run), :] = short_conv(line, taps)
 
 
 def finish_kernel(
@@ -467,36 +454,21 @@
     def shifted(first, *lead):
         return pl.BlockSpec(lead + (tile,), lambda i, *_: (0,) * len(lead) + (first + i,))
 
+    in_vmem = pl.BlockSpec(memory_space=pltpu.VMEM)
+
     def local(which, gate, first, count, held, name):
         return pl.pallas_call(
-            functools.partial(local_kernel, first),
-            grid_spec=pltpu.PrefetchScalarGridSpec(
-                num_scalar_prefetch=1,
-                grid=(count,),
-                in_specs=[
-                    in_hbm,
-                    shifted(first, rim + 1, 3),
-                    pl.BlockSpec((tiles * toks, LANES), lambda i, *_: (first + i, 0)),
-                    pl.BlockSpec(
-                        (tiles, 2, modes * SUB, LANES), lambda i, *_: (first + i, 0, 0, 0)
-                    ),
-                    shifted(first, modes),
-                    shifted(first, modes),
-                    shifted(first, 1),
-                ]
-                + [pl.BlockSpec(memory_space=pl.ANY)] * len(held),
-                out_specs=[pl.BlockSpec((tiles * half, LANES), lambda i, *_: (first + i, 0))] * 2,
-                scratch_shapes=[
-                    pltpu.VMEM((count, toks, tile), BF16),
-                    pltpu.VMEM((half + SUB, LANES), F32),
-                    pltpu.VMEM((modes * SUB, LANES), F32),
-                    pltpu.VMEM((modes, tile), F32),
-                    pltpu.VMEM((modes, tile), F32),
-                    pltpu.VMEM((modes, tile), F32),
-                    pltpu.SemaphoreType.DMA((count,)),
-                ],
-            ),
+            functools.partial(local_kernel, first * tile),
+            in_specs=[pl.BlockSpec(memory_space=pltpu.SMEM), in_hbm]
+            + [in_vmem] * (6 + len(held)),
+            out_specs=[in_vmem] * 2,
             out_shape=[jax.ShapeDtypeStruct((all_tiles * half, LANES), F32)] * 2,
+            scratch_shapes=[
+                pltpu.VMEM((toks, count * tile), BF16),
+                pltpu.VMEM((count * tiles, half + SUB, LANES), F32),
+                pltpu.VMEM((count * tiles, modes * SUB, LANES), F32),
+                pltpu.SemaphoreType.DMA(()),
+            ],
             input_output_aliases={8: 0, 9: 1} if held else {},
             compiler_params=params,
             name=name,
@@ -505,7 +477,6 @@
     few = steps // 2
     locals_sent = ()
     ids = index.astype(jnp.int32).reshape(1)
-    in_vmem = pl.BlockSpec(memory_space=pltpu.VMEM)
     prefix = jnp.zeros((modes, width), F32)
     past = jnp.zeros((SUB, width), F32)
     own = summary

time: 49.3 us -> 49.3 us (level)
  Pallas kernels: 14.8 us -> 13.3 us
  waiting for transfers between devices: 18 us -> 19.5 us
    pallas_call x3, Pallas kernels: 5.73 us -> 4.23 us  [local(): pl.pallas_call(functools.partial(local_kernel, first * tile), in_specs=[p...]
    ppermute x7, waiting for transfers between devices: 11 us -> 11.9 us  [send(): return lax.ppermute(value, 'ctx', route(hop))]
    ppermute x1, waiting for transfers between devices: 6.96 us -> 7.57 us  [shards(): far = lax.ppermute(sent, 'chan', [(0, 1), (1, 0)])]
  transfers between devices with their start and end apart: 11 -> 11, of which waited for: 8 -> 8; matrix products, arithmetic and copies ran while one was open for 0% -> 0% of each run, Pallas kernels for 17% -> 14%
where the time goes in v7:
time: 49.3 us; the launch traced here: 49.2 us
  waiting for transfers between devices  19.5 us (40%)
  starting transfers between devices  16.1 us (33%)
  Pallas kernels  13.3 us (27%)
    ppermute x7, waiting for transfers between devices, send(): return lax.ppermute(value, 'ctx', route(hop))  11.9 us
    ppermute x7, starting transfers between devices, send(): return lax.ppermute(value, 'ctx', route(hop))  10.6 us
    ppermute x1, waiting for transfers between devices, shards(): far = lax.ppermute(sent, 'chan', [(0, 1), (1, 0)])  7.57 us
    ppermute x1, starting transfers between devices, shards(): far = lax.ppermute(sent, 'chan', [(0, 1), (1, 0)])  5.53 us
    pallas_call x3, Pallas kernels, local(): pl.pallas_call(functools.partial(local_kernel, first * tile), in_specs=[p...  4.23 us
    pallas_call x1, Pallas kernels, shards(): pl.pallas_call(state_kernel, grid=(wide_steps,), in_specs=[in_hbm] * 3, o...  3.52 us
    pallas_call x1, Pallas kernels, finish(): pl.pallas_call(finish_kernel, grid_spec=pltpu.PrefetchScalarGridSpec(num_...  2.68 us
    pallas_call x4, Pallas kernels, shards(): pl.pallas_call(body, in_specs=[pl.BlockSpec(memory_space=pltpu.SMEM)] + [...  1.31 us
  transfers between devices with their start and end apart: 11, of which 8 were waited for; matrix products, arithmetic and copies ran while one was open for 0% of the time, Pallas kernels for 14%

profile of v7, /device:TPU:96, one launch (start us, length us, event | category | flops | bytes accessed | tf_op | source)
XLA Modules:
  0.0 49.2 jit_solution(6703429304662912178)
XLA Ops:
  0.0 0.0 copy-start
  0.0 0.0 copy-start.1
  0.0 0.0 copy-start.2
  0.0 0.0 copy-start.3
  0.0 3.5 %states.1 = (f32[2048,128]{1,0:T(8,128)S(1)}, f32[8,2,128,128]{3,2,1,0:T(8,128)S(1)}, f32[16,1024]{1,0:T(8,128)S(1)}, bf16[32,1024]{1,0:T(8,128)(2,1)S(1)}) custom-call(bf16[3,256,1024]{2,1,0:T(8,128)(2,1)} %bitcast.26, f32[3,3,1024]{2,1,0:T(4,128)} %taps_ref.9, f32[16,1024]{1,0:T(8,128)} %bitcast.6), custom_call_target="tpu_custom_call" | custom-call | tf_op jit(solution)/shard_map/states/pallas_call | solution.py:423
  3.5 0.1 collective-permute-start
  3.7 1.2 %collective-permute-done.refs_6_ = bf16[32,1024]{1,0:T(8,128)(2,1)S(1)} collective-permute-done((bf16[32,1024]{1,0:T(8,128)(2,1)S(1)}, bf16[32,1024]{1,0:T(8,128)(2,1)S(1)}, u32[]{:S(2)}, u32[]{:S(2)}) %collective-permute-start) | collective-permute-done | bytes 65568 | tf_op jit(solution)/shard_map/ppermute | solution.py:374
  4.9 0.0 copy-done
  4.9 0.0 copy-done.1
  4.9 0.2 join_0.1
  5.1 1.0 %collective-permute-start.1 = (bf16[32,1024]{1,0:T(8,128)(2,1)S(1)}, bf16[32,1024]{1,0:T(8,128)(2,1)S(1)}, u32[]{:S(2)}, u32[]{:S(2)}) collective-permute-start(bf16[32,1024]{1,0:T(8,128)(2,1)S(1)} %get-tuple-element.51.refs_5_), channel_id=1, source_target_pairs={{0,4},{2,14},{4,8},{6,2},{8,12},{10,6},{12,0},{14,10},{16,20},{18,... | collective-permute-start | bytes 196616 | tf_op jit(solution)/shard_map/ppermute | solution.py:374
  6.1 0.7 %collective-permute-start.2 = (bf16[32,1024]{1,0:T(8,128)(2,1)S(1)}, bf16[32,1024]{1,0:T(8,128)(2,1)S(1)}, u32[]{:S(2)}, u32[]{:S(2)}) collective-permute-start(bf16[32,1024]{1,0:T(8,128)(2,1)S(1)} %get-tuple-element.51.refs_5_), channel_id=1, source_target_pairs={{0,8},{2,10},{4,12},{6,14},{8,0},{10,2},{12,4},{14,6},{16,24},{18,... | collective-permute-start | bytes 196616 | tf_op jit(solution)/shard_map/ppermute | solution.py:374
  6.7 4.1 %collective-permute-done.1.refs_6_ = bf16[32,1024]{1,0:T(8,128)(2,1)S(1)} collective-permute-done((bf16[32,1024]{1,0:T(8,128)(2,1)S(1)}, bf16[32,1024]{1,0:T(8,128)(2,1)S(1)}, u32[]{:S(2)}, u32[]{:S(2)}) %collective-permute-start.1) | collective-permute-done | bytes 65568 | tf_op jit(solution)/shard_map/ppermute | solution.py:374
  10.9 0.0 collective-permute-start.3
  10.9 1.7 %collective-permute-done.2.refs_7_ = bf16[32,1024]{1,0:T(8,128)(2,1)S(1)} collective-permute-done((bf16[32,1024]{1,0:T(8,128)(2,1)S(1)}, bf16[32,1024]{1,0:T(8,128)(2,1)S(1)}, u32[]{:S(2)}, u32[]{:S(2)}) %collective-permute-start.2) | collective-permute-done | bytes 65568 | tf_op jit(solution)/shard_map/ppermute | solution.py:374
  12.5 0.0 collective-permute-done.3.refs_8_
  12.5 0.4 join_1.1
  12.9 1.6 %collective-permute-start.4 = (bf16[32,1024]{1,0:T(8,128)(2,1)S(1)}, bf16[32,1024]{1,0:T(8,128)(2,1)S(1)}, u32[]{:S(2)}, u32[]{:S(2)}) collective-permute-start(bf16[32,1024]{1,0:T(8,128)(2,1)S(1)} %get-tuple-element.52.refs_5_), channel_id=1, source_target_pairs={{0,16},{2,50},{4,20},{6,54},{8,24},{10,58},{12,28},{14,62},{16,32}... | collective-permute-start | bytes 196616 | tf_op jit(solution)/shard_map/ppermute | solution.py:374
  14.5 2.7 %collective-permute-start.5 = (bf16[32,1024]{1,0:T(8,128)(2,1)S(1)}, bf16[32,1024]{1,0:T(8,128)(2,1)S(1)}, u32[]{:S(2)}, u32[]{:S(2)}) collective-permute-start(bf16[32,1024]{1,0:T(8,128)(2,1)S(1)} %get-tuple-element.52.refs_5_), channel_id=1, source_target_pairs={{0,32},{2,34},{4,36},{6,38},{8,40},{10,42},{12,44},{14,46},{16,48}... | collective-permute-start | bytes 196616 | tf_op jit(solution)/shard_map/ppermute | solution.py:374
  17.2 1.3 %collective-permute-done.4.refs_6_ = bf16[32,1024]{1,0:T(8,128)(2,1)S(1)} collective-permute-done((bf16[32,1024]{1,0:T(8,128)(2,1)S(1)}, bf16[32,1024]{1,0:T(8,128)(2,1)S(1)}, u32[]{:S(2)}, u32[]{:S(2)}) %collective-permute-start.4) | collective-permute-done | bytes 65568 | tf_op jit(solution)/shard_map/ppermute | solution.py:374
  18.5 0.0 collective-permute-start.6
  18.5 0.0 copy-done.2
  18.5 0.0 copy-done.3
  18.5 1.1 %local_sent_2.1 = (f32[1024,128]{1,0:T(8,128)S(1)}, f32[1024,128]{1,0:T(8,128)S(1)}) custom-call(s32[1]{0:T(128)S(6)} %sub.2.part_id.ids, bf16[3,256,1024]{2,1,0:T(8,128)(2,1)} %bitcast.27, f32[3,3,1024]{2,1,0:T(4,128)S(1)} %copy-done.1, f32[2048,128]{1,0:T(8,128)S(1)} %get-tuple-element.81.gate_ref, f32[8,2,128,128]{3,2,1,0:T(8,128)S(1)} %get-tuple-element.57.ends_ref, ...), custom_call_target="tpu_custom_call" | custom-call | tf_op jit(solution)/shard_map/local_sent_2/pallas_call | solution.py:460
  19.6 1.2 %collective-permute-done.5.refs_7_ = bf16[32,1024]{1,0:T(8,128)(2,1)S(1)} collective-permute-done((bf16[32,1024]{1,0:T(8,128)(2,1)S(1)}, bf16[32,1024]{1,0:T(8,128)(2,1)S(1)}, u32[]{:S(2)}, u32[]{:S(2)}) %collective-permute-start.5) | collective-permute-done | bytes 65568 | tf_op jit(solution)/shard_map/ppermute | solution.py:374
  20.9 0.0 collective-permute-done.6.refs_8_
  20.9 0.4 join_2.1
  21.3 1.7 %collective-permute-start.7 = (bf16[32,1024]{1,0:T(8,128)(2,1)S(1)}, bf16[32,1024]{1,0:T(8,128)(2,1)S(1)}, u32[]{:S(2)}, u32[]{:S(2)}) collective-permute-start(bf16[32,1024]{1,0:T(8,128)(2,1)S(1)} %get-tuple-element.64.refs_5_), channel_id=1, source_target_pairs={{0,64},{2,194},{4,68},{6,198},{8,72},{10,202},{12,76},{14,206},{16... | collective-permute-start | bytes 196616 | tf_op jit(solution)/shard_map/ppermute | solution.py:374
  23.0 2.9 %collective-permute-start.8 = (bf16[32,1024]{1,0:T(8,128)(2,1)S(1)}, bf16[32,1024]{1,0:T(8,128)(2,1)S(1)}, u32[]{:S(2)}, u32[]{:S(2)}) collective-permute-start(bf16[32,1024]{1,0:T(8,128)(2,1)S(1)} %get-tuple-element.64.refs_5_), channel_id=1, source_target_pairs={{0,128},{2,130},{4,132},{6,134},{8,136},{10,138},{12,140},{14,142}... | collective-permute-start | bytes 196616 | tf_op jit(solution)/shard_map/ppermute | solution.py:374
  25.9 1.0 %collective-permute-done.7.refs_6_ = bf16[32,1024]{1,0:T(8,128)(2,1)S(1)} collective-permute-done((bf16[32,1024]{1,0:T(8,128)(2,1)S(1)}, bf16[32,1024]{1,0:T(8,128)(2,1)S(1)}, u32[]{:S(2)}, u32[]{:S(2)}) %collective-permute-start.7) | collective-permute-done | bytes 65568 | tf_op jit(solution)/shard_map/ppermute | solution.py:374
  26.9 0.0 collective-permute-start.9
  26.9 1.1 %local_sent_3.1 = (f32[1024,128]{1,0:T(8,128)S(1)}, f32[1024,128]{1,0:T(8,128)S(1)}) custom-call(s32[1]{0:T(128)S(6)} %sub.2.part_id.ids, bf16[3,256,1024]{2,1,0:T(8,128)(2,1)} %bitcast.28, f32[3,3,1024]{2,1,0:T(4,128)S(1)} %copy-done.1, f32[2048,128]{1,0:T(8,128)S(1)} %get-tuple-element.81.gate_ref, ...), custom_call_target="tpu_custom_call", output_to_operand_aliasing={{0}: (8, {}), {1}: (9, {})} | custom-call | tf_op jit(solution)/shard_map/local_sent_3/pallas_call | solution.py:460
  28.0 1.4 %collective-permute-done.8.refs_7_ = bf16[32,1024]{1,0:T(8,128)(2,1)S(1)} collective-permute-done((bf16[32,1024]{1,0:T(8,128)(2,1)S(1)}, bf16[32,1024]{1,0:T(8,128)(2,1)S(1)}, u32[]{:S(2)}, u32[]{:S(2)}) %collective-permute-start.8) | collective-permute-done | bytes 65568 | tf_op jit(solution)/shard_map/ppermute | solution.py:374
  29.4 0.0 collective-permute-done.9.refs_8_
  29.4 0.3 join_3.1
  29.7 0.9 %finish_sent.1 = bf16[128,1024]{1,0:T(8,128)(2,1)S(1)} custom-call(s32[1]{0:T(128)S(6)} %sub.2.part_id.ids, f32[1024,128]{1,0:T(8,128)S(1)} %get-tuple-element.71.query_ref, f32[1024,128]{1,0:T(8,128)S(1)} %get-tuple-element.72.local_ref, f32[16,1024]{1,0:T(8,128)S(1)} %get-tuple-element.84.prefix_ref, f32[8,1024]{1,0:T(8,128)S(1)} %get-tuple-element.80.past_ref, ...), custom_call_target="tpu_custom_call" | custom-call | tf_op jit(solution)/shard_map/finish_sent/pallas_call | solution.py:557
  30.6 5.5 %collective-permute-start.10 = (bf16[128,1024]{1,0:T(8,128)(2,1)S(1)}, bf16[128,1024]{1,0:T(8,128)(2,1)S(1)}, u32[]{:S(2)}, u32[]{:S(2)}) collective-permute-start(bf16[128,1024]{1,0:T(8,128)(2,1)S(1)} %finish_sent.1), channel_id=1, source_target_pairs={{0,1},{1,0},{2,3},{3,2},{4,5},{5,4},{6,7},{7,6},{8,9},{9,8},{10,11... | collective-permute-start | bytes 786440 | tf_op jit(solution)/shard_map/ppermute | solution.py:566
  36.2 0.1 pad_add_fusion.ids
  36.2 2.0 %local_own.1 = (f32[1024,128]{1,0:T(8,128)S(1)}, f32[1024,128]{1,0:T(8,128)S(1)}) custom-call(s32[1]{0:T(128)} %bitcast.part_id, bf16[3,256,1024]{2,1,0:T(8,128)(2,1)} %bitcast.29, f32[3,3,1024]{2,1,0:T(4,128)S(1)} %copy-done.1, f32[2048,128]{1,0:T(8,128)S(1)} %get-tuple-element.81.gate_ref, f32[8,2,128,128]{3,2,1,0:T(8,128)S(1)} %get-tuple-element.57.ends_ref, ...), custom_call_target="tpu_custom_call" | custom-call | tf_op jit(solution)/shard_map/local_own/pallas_call | solution.py:460
  38.2 2.7 %finish_own.1.held_ref = bf16[128,2048]{1,0:T(8,128)(2,1)} custom-call(s32[2]{0:T(128)S(1)} %pad_add_fusion.ids, f32[1024,128]{1,0:T(8,128)S(1)} %get-tuple-element.82.query_ref, f32[1024,128]{1,0:T(8,128)S(1)} %get-tuple-element.83.local_ref, f32[16,1024]{1,0:T(8,128)S(1)} %get-tuple-element.84.prefix_ref, f32[8,1024]{1,0:T(8,128)S(1)} %get-tuple-element.80.past_ref, ...), custom_call_target="tpu_custom_call" | custom-call | tf_op jit(solution)/shard_map/finish_own/pallas_call | solution.py:520
  40.9 7.6 %collective-permute-done.10.far_ref = bf16[128,1024]{1,0:T(8,128)(2,1)S(1)} collective-permute-done((bf16[128,1024]{1,0:T(8,128)(2,1)S(1)}, bf16[128,1024]{1,0:T(8,128)(2,1)S(1)}, u32[]{:S(2)}, u32[]{:S(2)}) %collective-permute-start.10) | collective-permute-done | bytes 262176 | tf_op jit(solution)/shard_map/ppermute | solution.py:566
  48.5 0.7 %place.1 = bf16[128,2048]{1,0:T(8,128)(2,1)} custom-call(s32[1]{0:T(128)S(6)} %sub.2.part_id.ids, bf16[128,1024]{1,0:T(8,128)(2,1)S(1)} %collective-permute-done.10.far_ref, bf16[128,2048]{1,0:T(8,128)(2,1)} %finish_own.1.held_ref), custom_call_target="tpu_custom_call", output_to_operand_aliasing={{}: (2, {})} | custom-call | tf_op jit(solution)/shard_map/place/pallas_call | solution.py:570
  (2 shorter events, 0.0 us)
Async XLA Ops:
  0.0 4.9 %copy-start = (f32[1024,16]{0,1:T(8,128)S(1)}, f32[1024,16]{0,1:T(8,128)}, u32[]{:S(2)}) copy-start(f32[1024,16]{0,1:T(8,128)} %param.8) | copy-start | bytes 196612
  0.0 4.9 %copy-start.1 = (f32[3,3,1024]{2,1,0:T(4,128)S(1)}, f32[3,3,1024]{2,1,0:T(4,128)}, u32[]{:S(2)}) copy-start(f32[3,3,1024]{2,1,0:T(4,128)} %taps_ref.9) | copy-start | bytes 110596
  0.0 18.5 %copy-start.2 = (f32[1024,16]{0,1:T(8,128)S(1)}, f32[1024,16]{0,1:T(8,128)}, u32[]{:S(2)}) copy-start(f32[1024,16]{0,1:T(8,128)} %param.7) | copy-start | bytes 196612
  0.0 18.5 %copy-start.3 = (f32[1024]{0:T(1024)S(1)}, f32[1024]{0:T(1024)}, u32[]{:S(2)}) copy-start(f32[1024]{0:T(1024)} %param.9) | copy-start | bytes 12292
  3.5 1.3 %collective-permute-start = (bf16[32,1024]{1,0:T(8,128)(2,1)S(1)}, bf16[32,1024]{1,0:T(8,128)(2,1)S(1)}, u32[]{:S(2)}, u32[]{:S(2)}) collective-permute-start(bf16[32,1024]{1,0:T(8,128)(2,1)S(1)} %get-tuple-element.47.refs_5_.sum_ref), channel_id=1, source_target_pairs={{0,2},{2,0},{4,6},{6,4},{8,10},{10,8},{12,14},{14,12},{16,18},{18,... | collective-permute-start | bytes 196616 | tf_op jit(solution)/shard_map/ppermute | solution.py:374
  5.1 5.8 %collective-permute-start.1 = (bf16[32,1024]{1,0:T(8,128)(2,1)S(1)}, bf16[32,1024]{1,0:T(8,128)(2,1)S(1)}, u32[]{:S(2)}, u32[]{:S(2)}) collective-permute-start(bf16[32,1024]{1,0:T(8,128)(2,1)S(1)} %get-tuple-element.51.refs_5_), channel_id=1, source_target_pairs={{0,4},{2,14},{4,8},{6,2},{8,12},{10,6},{12,0},{14,10},{16,20},{18,... | collective-permute-start | bytes 196616 | tf_op jit(solution)/shard_map/ppermute | solution.py:374
  6.1 6.4 %collective-permute-start.2 = (bf16[32,1024]{1,0:T(8,128)(2,1)S(1)}, bf16[32,1024]{1,0:T(8,128)(2,1)S(1)}, u32[]{:S(2)}, u32[]{:S(2)}) collective-permute-start(bf16[32,1024]{1,0:T(8,128)(2,1)S(1)} %get-tuple-element.51.refs_5_), channel_id=1, source_target_pairs={{0,8},{2,10},{4,12},{6,14},{8,0},{10,2},{12,4},{14,6},{16,24},{18,... | collective-permute-start | bytes 196616 | tf_op jit(solution)/shard_map/ppermute | solution.py:374
  10.9 1.7 %collective-permute-start.3 = (bf16[32,1024]{1,0:T(8,128)(2,1)S(1)}, bf16[32,1024]{1,0:T(8,128)(2,1)S(1)}, u32[]{:S(2)}, u32[]{:S(2)}) collective-permute-start(bf16[32,1024]{1,0:T(8,128)(2,1)S(1)} %collective-permute-done.1.refs_6_), channel_id=1, source_target_pairs={{0,2},{2,0},{4,6},{6,4},{8,10},{10,8},{12,14},{14,12},{16,18},{18,... | collective-permute-start | bytes 196616 | tf_op jit(solution)/shard_map/ppermute | solution.py:380
  12.9 5.6 %collective-permute-start.4 = (bf16[32,1024]{1,0:T(8,128)(2,1)S(1)}, bf16[32,1024]{1,0:T(8,128)(2,1)S(1)}, u32[]{:S(2)}, u32[]{:S(2)}) collective-permute-start(bf16[32,1024]{1,0:T(8,128)(2,1)S(1)} %get-tuple-element.52.refs_5_), channel_id=1, source_target_pairs={{0,16},{2,50},{4,20},{6,54},{8,24},{10,58},{12,28},{14,62},{16,32}... | collective-permute-start | bytes 196616 | tf_op jit(solution)/shard_map/ppermute | solution.py:374
  14.5 6.4 %collective-permute-start.5 = (bf16[32,1024]{1,0:T(8,128)(2,1)S(1)}, bf16[32,1024]{1,0:T(8,128)(2,1)S(1)}, u32[]{:S(2)}, u32[]{:S(2)}) collective-permute-start(bf16[32,1024]{1,0:T(8,128)(2,1)S(1)} %get-tuple-element.52.refs_5_), channel_id=1, source_target_pairs={{0,32},{2,34},{4,36},{6,38},{8,40},{10,42},{12,44},{14,46},{16,48}... | collective-permute-start | bytes 196616 | tf_op jit(solution)/shard_map/ppermute | solution.py:374
  18.5 2.4 %collective-permute-start.6 = (bf16[32,1024]{1,0:T(8,128)(2,1)S(1)}, bf16[32,1024]{1,0:T(8,128)(2,1)S(1)}, u32[]{:S(2)}, u32[]{:S(2)}) collective-permute-start(bf16[32,1024]{1,0:T(8,128)(2,1)S(1)} %collective-permute-done.4.refs_6_), channel_id=1, source_target_pairs={{0,2},{2,0},{4,6},{6,4},{8,10},{10,8},{12,14},{14,12},{16,18},{18,... | collective-permute-start | bytes 196616 | tf_op jit(solution)/shard_map/ppermute | solution.py:380
  21.3 5.6 %collective-permute-start.7 = (bf16[32,1024]{1,0:T(8,128)(2,1)S(1)}, bf16[32,1024]{1,0:T(8,128)(2,1)S(1)}, u32[]{:S(2)}, u32[]{:S(2)}) collective-permute-start(bf16[32,1024]{1,0:T(8,128)(2,1)S(1)} %get-tuple-element.64.refs_5_), channel_id=1, source_target_pairs={{0,64},{2,194},{4,68},{6,198},{8,72},{10,202},{12,76},{14,206},{16... | collective-permute-start | bytes 196616 | tf_op jit(solution)/shard_map/ppermute | solution.py:374
  23.0 6.5 %collective-permute-start.8 = (bf16[32,1024]{1,0:T(8,128)(2,1)S(1)}, bf16[32,1024]{1,0:T(8,128)(2,1)S(1)}, u32[]{:S(2)}, u32[]{:S(2)}) collective-permute-start(bf16[32,1024]{1,0:T(8,128)(2,1)S(1)} %get-tuple-element.64.refs_5_), channel_id=1, source_target_pairs={{0,128},{2,130},{4,132},{6,134},{8,136},{10,138},{12,140},{14,142}... | collective-permute-start | bytes 196616 | tf_op jit(solution)/shard_map/ppermute | solution.py:374
  26.9 2.6 %collective-permute-start.9 = (bf16[32,1024]{1,0:T(8,128)(2,1)S(1)}, bf16[32,1024]{1,0:T(8,128)(2,1)S(1)}, u32[]{:S(2)}, u32[]{:S(2)}) collective-permute-start(bf16[32,1024]{1,0:T(8,128)(2,1)S(1)} %collective-permute-done.7.refs_6_), channel_id=1, source_target_pairs={{0,2},{2,0},{4,6},{6,4},{8,10},{10,8},{12,14},{14,12},{16,18},{18,... | collective-permute-start | bytes 196616 | tf_op jit(solution)/shard_map/ppermute | solution.py:380
  30.6 17.9 %collective-permute-start.10 = (bf16[128,1024]{1,0:T(8,128)(2,1)S(1)}, bf16[128,1024]{1,0:T(8,128)(2,1)S(1)}, u32[]{:S(2)}, u32[]{:S(2)}) collective-permute-start(bf16[128,1024]{1,0:T(8,128)(2,1)S(1)} %finish_sent.1), channel_id=1, source_target_pairs={{0,1},{1,0},{2,3},{3,2},{4,5},{5,4},{6,7},{7,6},{8,9},{9,8},{10,11... | collective-permute-start | bytes 786440 | tf_op jit(solution)/shard_map/ppermute | solution.py:566

commit v8 on v7

--- a/solution.py
+++ b/solution.py
@@ -485,9 +485,9 @@
     for level, count in enumerate(counts):
         last = level == len(counts) - 1
         arrived = exchange(summary, ctx_count, index, stride, count)
-        if level >= 2:
+        if 1 <= level <= 2:
             gate, arrived[0] = lax.optimization_barrier((gate, arrived[0]))
-            first = 0 if level == 2 else few
+            first = 0 if level == 1 else few
             locals_sent = local(1 - side, gate, first, few, locals_sent, f"local_sent_{level}")
             locals_sent, arrived = lax.optimization_barrier((locals_sent, arrived))
         shapes = [

time: 49.3 us -> 49.5 us (level); the launches traced: 49.2 us -> 48.8 us
  waiting for transfers between devices: 19.5 us -> 19 us
where the time goes in v8:
time: 49.5 us; the launch traced here: 48.8 us
  waiting for transfers between devices  19 us (38%)
  starting transfers between devices  16.3 us (33%)
  Pallas kernels  13.3 us (27%)
    ppermute x7, waiting for transfers between devices, send(): return lax.ppermute(value, 'ctx', route(hop))  11.8 us
    ppermute x7, starting transfers between devices, send(): return lax.ppermute(value, 'ctx', route(hop))  10.6 us
    ppermute x1, waiting for transfers between devices, shards(): far = lax.ppermute(sent, 'chan', [(0, 1), (1, 0)])  7.23 us
    ppermute x1, starting transfers between devices, shards(): far = lax.ppermute(sent, 'chan', [(0, 1), (1, 0)])  5.67 us
    pallas_call x3, Pallas kernels, local(): pl.pallas_call(functools.partial(local_kernel, first * tile), in_specs=[p...  4.23 us
    pallas_call x1, Pallas kernels, shards(): pl.pallas_call(state_kernel, grid=(wide_steps,), in_specs=[in_hbm] * 3, o...  3.52 us
    pallas_call x1, Pallas kernels, finish(): pl.pallas_call(finish_kernel, grid_spec=pltpu.PrefetchScalarGridSpec(num_...  2.68 us
    pallas_call x4, Pallas kernels, shards(): pl.pallas_call(body, in_specs=[pl.BlockSpec(memory_space=pltpu.SMEM)] + [...  1.31 us
  transfers between devices with their start and end apart: 11, of which 8 were waited for; matrix products, arithmetic and copies ran while one was open for 0% of the time, Pallas kernels for 14%

profile of v8, /device:TPU:96, one launch (start us, length us, event | category | flops | bytes accessed | tf_op | source)
XLA Modules:
  0.0 48.8 jit_solution(1308120007568600747)
XLA Ops:
  0.0 0.0 copy-start
  0.0 0.0 copy-start.1
  0.0 0.0 copy-start.2
  0.0 0.0 copy-start.3
  0.0 3.5 %states.1 = (f32[2048,128]{1,0:T(8,128)S(1)}, f32[8,2,128,128]{3,2,1,0:T(8,128)S(1)}, f32[16,1024]{1,0:T(8,128)S(1)}, bf16[32,1024]{1,0:T(8,128)(2,1)S(1)}) custom-call(bf16[3,256,1024]{2,1,0:T(8,128)(2,1)} %bitcast.26, f32[3,3,1024]{2,1,0:T(4,128)} %taps_ref.9, f32[16,1024]{1,0:T(8,128)} %bitcast.6), custom_call_target="tpu_custom_call" | custom-call | tf_op jit(solution)/shard_map/states/pallas_call | solution.py:423
  3.5 0.1 collective-permute-start
  3.7 1.2 %collective-permute-done.refs_6_ = bf16[32,1024]{1,0:T(8,128)(2,1)S(1)} collective-permute-done((bf16[32,1024]{1,0:T(8,128)(2,1)S(1)}, bf16[32,1024]{1,0:T(8,128)(2,1)S(1)}, u32[]{:S(2)}, u32[]{:S(2)}) %collective-permute-start) | collective-permute-done | bytes 65568 | tf_op jit(solution)/shard_map/ppermute | solution.py:374
  4.9 0.0 copy-done
  4.9 0.0 copy-done.1
  4.9 0.2 join_0.1
  5.1 1.0 %collective-permute-start.1 = (bf16[32,1024]{1,0:T(8,128)(2,1)S(1)}, bf16[32,1024]{1,0:T(8,128)(2,1)S(1)}, u32[]{:S(2)}, u32[]{:S(2)}) collective-permute-start(bf16[32,1024]{1,0:T(8,128)(2,1)S(1)} %get-tuple-element.48.refs_5_), channel_id=1, source_target_pairs={{0,4},{2,14},{4,8},{6,2},{8,12},{10,6},{12,0},{14,10},{16,20},{18,... | collective-permute-start | bytes 196616 | tf_op jit(solution)/shard_map/ppermute | solution.py:374
  6.1 0.7 %collective-permute-start.2 = (bf16[32,1024]{1,0:T(8,128)(2,1)S(1)}, bf16[32,1024]{1,0:T(8,128)(2,1)S(1)}, u32[]{:S(2)}, u32[]{:S(2)}) collective-permute-start(bf16[32,1024]{1,0:T(8,128)(2,1)S(1)} %get-tuple-element.48.refs_5_), channel_id=1, source_target_pairs={{0,8},{2,10},{4,12},{6,14},{8,0},{10,2},{12,4},{14,6},{16,24},{18,... | collective-permute-start | bytes 196616 | tf_op jit(solution)/shard_map/ppermute | solution.py:374
  6.7 4.1 %collective-permute-done.1.refs_6_ = bf16[32,1024]{1,0:T(8,128)(2,1)S(1)} collective-permute-done((bf16[32,1024]{1,0:T(8,128)(2,1)S(1)}, bf16[32,1024]{1,0:T(8,128)(2,1)S(1)}, u32[]{:S(2)}, u32[]{:S(2)}) %collective-permute-start.1) | collective-permute-done | bytes 65568 | tf_op jit(solution)/shard_map/ppermute | solution.py:374
  10.9 0.0 collective-permute-start.3
  10.9 0.0 copy-done.2
  10.9 0.0 copy-done.3
  10.9 1.1 %local_sent_1.1 = (f32[1024,128]{1,0:T(8,128)S(1)}, f32[1024,128]{1,0:T(8,128)S(1)}) custom-call(s32[1]{0:T(128)S(6)} %sub.2.part_id.ids, bf16[3,256,1024]{2,1,0:T(8,128)(2,1)} %bitcast.27, f32[3,3,1024]{2,1,0:T(4,128)S(1)} %copy-done.1, f32[2048,128]{1,0:T(8,128)S(1)} %get-tuple-element.81.gate_ref, f32[8,2,128,128]{3,2,1,0:T(8,128)S(1)} %get-tuple-element.53.ends_ref, ...), custom_call_target="tpu_custom_call" | custom-call | tf_op jit(solution)/shard_map/local_sent_1/pallas_call | solution.py:460
  12.0 0.5 %collective-permute-done.2.refs_7_ = bf16[32,1024]{1,0:T(8,128)(2,1)S(1)} collective-permute-done((bf16[32,1024]{1,0:T(8,128)(2,1)S(1)}, bf16[32,1024]{1,0:T(8,128)(2,1)S(1)}, u32[]{:S(2)}, u32[]{:S(2)}) %collective-permute-start.2) | collective-permute-done | bytes 65568 | tf_op jit(solution)/shard_map/ppermute | solution.py:374
  12.5 0.0 collective-permute-done.3.refs_8_
  12.5 0.4 join_1.1
  12.9 1.6 %collective-permute-start.4 = (bf16[32,1024]{1,0:T(8,128)(2,1)S(1)}, bf16[32,1024]{1,0:T(8,128)(2,1)S(1)}, u32[]{:S(2)}, u32[]{:S(2)}) collective-permute-start(bf16[32,1024]{1,0:T(8,128)(2,1)S(1)} %get-tuple-element.60.refs_5_), channel_id=1, source_target_pairs={{0,16},{2,50},{4,20},{6,54},{8,24},{10,58},{12,28},{14,62},{16,32}... | collective-permute-start | bytes 196616 | tf_op jit(solution)/shard_map/ppermute | solution.py:374
  14.5 2.7 %collective-permute-start.5 = (bf16[32,1024]{1,0:T(8,128)(2,1)S(1)}, bf16[32,1024]{1,0:T(8,128)(2,1)S(1)}, u32[]{:S(2)}, u32[]{:S(2)}) collective-permute-start(bf16[32,1024]{1,0:T(8,128)(2,1)S(1)} %get-tuple-element.60.refs_5_), channel_id=1, source_target_pairs={{0,32},{2,34},{4,36},{6,38},{8,40},{10,42},{12,44},{14,46},{16,48}... | collective-permute-start | bytes 196616 | tf_op jit(solution)/shard_map/ppermute | solution.py:374
  17.2 1.3 %collective-permute-done.4.refs_6_ = bf16[32,1024]{1,0:T(8,128)(2,1)S(1)} collective-permute-done((bf16[32,1024]{1,0:T(8,128)(2,1)S(1)}, bf16[32,1024]{1,0:T(8,128)(2,1)S(1)}, u32[]{:S(2)}, u32[]{:S(2)}) %collective-permute-start.4) | collective-permute-done | bytes 65568 | tf_op jit(solution)/shard_map/ppermute | solution.py:374
  18.5 0.0 collective-permute-start.6
  18.5 1.1 %local_sent_2.1 = (f32[1024,128]{1,0:T(8,128)S(1)}, f32[1024,128]{1,0:T(8,128)S(1)}) custom-call(s32[1]{0:T(128)S(6)} %sub.2.part_id.ids, bf16[3,256,1024]{2,1,0:T(8,128)(2,1)} %bitcast.28, f32[3,3,1024]{2,1,0:T(4,128)S(1)} %copy-done.1, f32[2048,128]{1,0:T(8,128)S(1)} %get-tuple-element.81.gate_ref, ...), custom_call_target="tpu_custom_call", output_to_operand_aliasing={{0}: (8, {}), {1}: (9, {})} | custom-call | tf_op jit(solution)/shard_map/local_sent_2/pallas_call | solution.py:460
  19.6 1.2 %collective-permute-done.5.refs_7_ = bf16[32,1024]{1,0:T(8,128)(2,1)S(1)} collective-permute-done((bf16[32,1024]{1,0:T(8,128)(2,1)S(1)}, bf16[32,1024]{1,0:T(8,128)(2,1)S(1)}, u32[]{:S(2)}, u32[]{:S(2)}) %collective-permute-start.5) | collective-permute-done | bytes 65568 | tf_op jit(solution)/shard_map/ppermute | solution.py:374
  20.9 0.0 collective-permute-done.6.refs_8_
  20.9 0.4 join_2.1
  21.3 1.7 %collective-permute-start.7 = (bf16[32,1024]{1,0:T(8,128)(2,1)S(1)}, bf16[32,1024]{1,0:T(8,128)(2,1)S(1)}, u32[]{:S(2)}, u32[]{:S(2)}) collective-permute-start(bf16[32,1024]{1,0:T(8,128)(2,1)S(1)} %get-tuple-element.78.refs_5_), channel_id=1, source_target_pairs={{0,64},{2,194},{4,68},{6,198},{8,72},{10,202},{12,76},{14,206},{16... | collective-permute-start | bytes 196616 | tf_op jit(solution)/shard_map/ppermute | solution.py:374
  23.0 2.9 %collective-permute-start.8 = (bf16[32,1024]{1,0:T(8,128)(2,1)S(1)}, bf16[32,1024]{1,0:T(8,128)(2,1)S(1)}, u32[]{:S(2)}, u32[]{:S(2)}) collective-permute-start(bf16[32,1024]{1,0:T(8,128)(2,1)S(1)} %get-tuple-element.78.refs_5_), channel_id=1, source_target_pairs={{0,128},{2,130},{4,132},{6,134},{8,136},{10,138},{12,140},{14,142}... | collective-permute-start | bytes 196616 | tf_op jit(solution)/shard_map/ppermute | solution.py:374
  25.9 1.0 %collective-permute-done.7.refs_6_ = bf16[32,1024]{1,0:T(8,128)(2,1)S(1)} collective-permute-done((bf16[32,1024]{1,0:T(8,128)(2,1)S(1)}, bf16[32,1024]{1,0:T(8,128)(2,1)S(1)}, u32[]{:S(2)}, u32[]{:S(2)}) %collective-permute-start.7) | collective-permute-done | bytes 65568 | tf_op jit(solution)/shard_map/ppermute | solution.py:374
  26.9 0.0 collective-permute-start.9
  26.9 2.4 %collective-permute-done.8.refs_7_ = bf16[32,1024]{1,0:T(8,128)(2,1)S(1)} collective-permute-done((bf16[32,1024]{1,0:T(8,128)(2,1)S(1)}, bf16[32,1024]{1,0:T(8,128)(2,1)S(1)}, u32[]{:S(2)}, u32[]{:S(2)}) %collective-permute-start.8) | collective-permute-done | bytes 65568 | tf_op jit(solution)/shard_map/ppermute | solution.py:374
  29.3 0.0 collective-permute-done.9.refs_8_
  29.3 0.3 join_3.1
  29.6 0.9 %finish_sent.1 = bf16[128,1024]{1,0:T(8,128)(2,1)S(1)} custom-call(s32[1]{0:T(128)S(6)} %sub.2.part_id.ids, f32[1024,128]{1,0:T(8,128)S(1)} %get-tuple-element.67.query_ref, f32[1024,128]{1,0:T(8,128)S(1)} %get-tuple-element.68.local_ref, f32[16,1024]{1,0:T(8,128)S(1)} %get-tuple-element.84.prefix_ref, f32[8,1024]{1,0:T(8,128)S(1)} %get-tuple-element.80.past_ref, ...), custom_call_target="tpu_custom_call" | custom-call | tf_op jit(solution)/shard_map/finish_sent/pallas_call | solution.py:557
  30.5 5.7 %collective-permute-start.10 = (bf16[128,1024]{1,0:T(8,128)(2,1)S(1)}, bf16[128,1024]{1,0:T(8,128)(2,1)S(1)}, u32[]{:S(2)}, u32[]{:S(2)}) collective-permute-start(bf16[128,1024]{1,0:T(8,128)(2,1)S(1)} %finish_sent.1), channel_id=1, source_target_pairs={{0,1},{1,0},{2,3},{3,2},{4,5},{5,4},{6,7},{7,6},{8,9},{9,8},{10,11... | collective-permute-start | bytes 786440 | tf_op jit(solution)/shard_map/ppermute | solution.py:566
  36.2 0.1 pad_add_fusion.ids
  36.2 2.0 %local_own.1 = (f32[1024,128]{1,0:T(8,128)S(1)}, f32[1024,128]{1,0:T(8,128)S(1)}) custom-call(s32[1]{0:T(128)} %bitcast.part_id, bf16[3,256,1024]{2,1,0:T(8,128)(2,1)} %bitcast.29, f32[3,3,1024]{2,1,0:T(4,128)S(1)} %copy-done.1, f32[2048,128]{1,0:T(8,128)S(1)} %get-tuple-element.81.gate_ref, f32[8,2,128,128]{3,2,1,0:T(8,128)S(1)} %get-tuple-element.53.ends_ref, ...), custom_call_target="tpu_custom_call" | custom-call | tf_op jit(solution)/shard_map/local_own/pallas_call | solution.py:460
  38.2 2.7 %finish_own.1.held_ref = bf16[128,2048]{1,0:T(8,128)(2,1)} custom-call(s32[2]{0:T(128)S(1)} %pad_add_fusion.ids, f32[1024,128]{1,0:T(8,128)S(1)} %get-tuple-element.82.query_ref, f32[1024,128]{1,0:T(8,128)S(1)} %get-tuple-element.83.local_ref, f32[16,1024]{1,0:T(8,128)S(1)} %get-tuple-element.84.prefix_ref, f32[8,1024]{1,0:T(8,128)S(1)} %get-tuple-element.80.past_ref, ...), custom_call_target="tpu_custom_call" | custom-call | tf_op jit(solution)/shard_map/finish_own/pallas_call | solution.py:520
  40.9 7.2 %collective-permute-done.10.far_ref = bf16[128,1024]{1,0:T(8,128)(2,1)S(1)} collective-permute-done((bf16[128,1024]{1,0:T(8,128)(2,1)S(1)}, bf16[128,1024]{1,0:T(8,128)(2,1)S(1)}, u32[]{:S(2)}, u32[]{:S(2)}) %collective-permute-start.10) | collective-permute-done | bytes 262176 | tf_op jit(solution)/shard_map/ppermute | solution.py:566
  48.1 0.7 %place.1 = bf16[128,2048]{1,0:T(8,128)(2,1)} custom-call(s32[1]{0:T(128)S(6)} %sub.2.part_id.ids, bf16[128,1024]{1,0:T(8,128)(2,1)S(1)} %collective-permute-done.10.far_ref, bf16[128,2048]{1,0:T(8,128)(2,1)} %finish_own.1.held_ref), custom_call_target="tpu_custom_call", output_to_operand_aliasing={{}: (2, {})} | custom-call | tf_op jit(solution)/shard_map/place/pallas_call | solution.py:570
  (2 shorter events, 0.0 us)
Async XLA Ops:
  0.0 4.9 %copy-start = (f32[1024,16]{0,1:T(8,128)S(1)}, f32[1024,16]{0,1:T(8,128)}, u32[]{:S(2)}) copy-start(f32[1024,16]{0,1:T(8,128)} %param.8) | copy-start | bytes 196612
  0.0 4.9 %copy-start.1 = (f32[3,3,1024]{2,1,0:T(4,128)S(1)}, f32[3,3,1024]{2,1,0:T(4,128)}, u32[]{:S(2)}) copy-start(f32[3,3,1024]{2,1,0:T(4,128)} %taps_ref.9) | copy-start | bytes 110596
  0.0 10.9 %copy-start.2 = (f32[1024,16]{0,1:T(8,128)S(1)}, f32[1024,16]{0,1:T(8,128)}, u32[]{:S(2)}) copy-start(f32[1024,16]{0,1:T(8,128)} %param.7) | copy-start | bytes 196612
  0.0 10.9 %copy-start.3 = (f32[1024]{0:T(1024)S(1)}, f32[1024]{0:T(1024)}, u32[]{:S(2)}) copy-start(f32[1024]{0:T(1024)} %param.9) | copy-start | bytes 12292
  3.5 1.3 %collective-permute-start = (bf16[32,1024]{1,0:T(8,128)(2,1)S(1)}, bf16[32,1024]{1,0:T(8,128)(2,1)S(1)}, u32[]{:S(2)}, u32[]{:S(2)}) collective-permute-start(bf16[32,1024]{1,0:T(8,128)(2,1)S(1)} %get-tuple-element.47.refs_5_.sum_ref), channel_id=1, source_target_pairs={{0,2},{2,0},{4,6},{6,4},{8,10},{10,8},{12,14},{14,12},{16,18},{18,... | collective-permute-start | bytes 196616 | tf_op jit(solution)/shard_map/ppermute | solution.py:374
  5.1 5.8 %collective-permute-start.1 = (bf16[32,1024]{1,0:T(8,128)(2,1)S(1)}, bf16[32,1024]{1,0:T(8,128)(2,1)S(1)}, u32[]{:S(2)}, u32[]{:S(2)}) collective-permute-start(bf16[32,1024]{1,0:T(8,128)(2,1)S(1)} %get-tuple-element.48.refs_5_), channel_id=1, source_target_pairs={{0,4},{2,14},{4,8},{6,2},{8,12},{10,6},{12,0},{14,10},{16,20},{18,... | collective-permute-start | bytes 196616 | tf_op jit(solution)/shard_map/ppermute | solution.py:374
  6.1 6.4 %collective-permute-start.2 = (bf16[32,1024]{1,0:T(8,128)(2,1)S(1)}, bf16[32,1024]{1,0:T(8,128)(2,1)S(1)}, u32[]{:S(2)}, u32[]{:S(2)}) collective-permute-start(bf16[32,1024]{1,0:T(8,128)(2,1)S(1)} %get-tuple-element.48.refs_5_), channel_id=1, source_target_pairs={{0,8},{2,10},{4,12},{6,14},{8,0},{10,2},{12,4},{14,6},{16,24},{18,... | collective-permute-start | bytes 196616 | tf_op jit(solution)/shard_map/ppermute | solution.py:374
  10.9 1.7 %collective-permute-start.3 = (bf16[32,1024]{1,0:T(8,128)(2,1)S(1)}, bf16[32,1024]{1,0:T(8,128)(2,1)S(1)}, u32[]{:S(2)}, u32[]{:S(2)}) collective-permute-start(bf16[32,1024]{1,0:T(8,128)(2,1)S(1)} %collective-permute-done.1.refs_6_), channel_id=1, source_target_pairs={{0,2},{2,0},{4,6},{6,4},{8,10},{10,8},{12,14},{14,12},{16,18},{18,... | collective-permute-start | bytes 196616 | tf_op jit(solution)/shard_map/ppermute | solution.py:380
  12.9 5.6 %collective-permute-start.4 = (bf16[32,1024]{1,0:T(8,128)(2,1)S(1)}, bf16[32,1024]{1,0:T(8,128)(2,1)S(1)}, u32[]{:S(2)}, u32[]{:S(2)}) collective-permute-start(bf16[32,1024]{1,0:T(8,128)(2,1)S(1)} %get-tuple-element.60.refs_5_), channel_id=1, source_target_pairs={{0,16},{2,50},{4,20},{6,54},{8,24},{10,58},{12,28},{14,62},{16,32}... | collective-permute-start | bytes 196616 | tf_op jit(solution)/shard_map/ppermute | solution.py:374
  14.5 6.4 %collective-permute-start.5 = (bf16[32,1024]{1,0:T(8,128)(2,1)S(1)}, bf16[32,1024]{1,0:T(8,128)(2,1)S(1)}, u32[]{:S(2)}, u32[]{:S(2)}) collective-permute-start(bf16[32,1024]{1,0:T(8,128)(2,1)S(1)} %get-tuple-element.60.refs_5_), channel_id=1, source_target_pairs={{0,32},{2,34},{4,36},{6,38},{8,40},{10,42},{12,44},{14,46},{16,48}... | collective-permute-start | bytes 196616 | tf_op jit(solution)/shard_map/ppermute | solution.py:374
  18.5 2.4 %collective-permute-start.6 = (bf16[32,1024]{1,0:T(8,128)(2,1)S(1)}, bf16[32,1024]{1,0:T(8,128)(2,1)S(1)}, u32[]{:S(2)}, u32[]{:S(2)}) collective-permute-start(bf16[32,1024]{1,0:T(8,128)(2,1)S(1)} %collective-permute-done.4.refs_6_), channel_id=1, source_target_pairs={{0,2},{2,0},{4,6},{6,4},{8,10},{10,8},{12,14},{14,12},{16,18},{18,... | collective-permute-start | bytes 196616 | tf_op jit(solution)/shard_map/ppermute | solution.py:380
  21.3 5.6 %collective-permute-start.7 = (bf16[32,1024]{1,0:T(8,128)(2,1)S(1)}, bf16[32,1024]{1,0:T(8,128)(2,1)S(1)}, u32[]{:S(2)}, u32[]{:S(2)}) collective-permute-start(bf16[32,1024]{1,0:T(8,128)(2,1)S(1)} %get-tuple-element.78.refs_5_), channel_id=1, source_target_pairs={{0,64},{2,194},{4,68},{6,198},{8,72},{10,202},{12,76},{14,206},{16... | collective-permute-start | bytes 196616 | tf_op jit(solution)/shard_map/ppermute | solution.py:374
  23.0 6.3 %collective-permute-start.8 = (bf16[32,1024]{1,0:T(8,128)(2,1)S(1)}, bf16[32,1024]{1,0:T(8,128)(2,1)S(1)}, u32[]{:S(2)}, u32[]{:S(2)}) collective-permute-start(bf16[32,1024]{1,0:T(8,128)(2,1)S(1)} %get-tuple-element.78.refs_5_), channel_id=1, source_target_pairs={{0,128},{2,130},{4,132},{6,134},{8,136},{10,138},{12,140},{14,142}... | collective-permute-start | bytes 196616 | tf_op jit(solution)/shard_map/ppermute | solution.py:374
  26.9 2.4 %collective-permute-start.9 = (bf16[32,1024]{1,0:T(8,128)(2,1)S(1)}, bf16[32,1024]{1,0:T(8,128)(2,1)S(1)}, u32[]{:S(2)}, u32[]{:S(2)}) collective-permute-start(bf16[32,1024]{1,0:T(8,128)(2,1)S(1)} %collective-permute-done.7.refs_6_), channel_id=1, source_target_pairs={{0,2},{2,0},{4,6},{6,4},{8,10},{10,8},{12,14},{14,12},{16,18},{18,... | collective-permute-start | bytes 196616 | tf_op jit(solution)/shard_map/ppermute | solution.py:380
  30.5 17.7 %collective-permute-start.10 = (bf16[128,1024]{1,0:T(8,128)(2,1)S(1)}, bf16[128,1024]{1,0:T(8,128)(2,1)S(1)}, u32[]{:S(2)}, u32[]{:S(2)}) collective-permute-start(bf16[128,1024]{1,0:T(8,128)(2,1)S(1)} %finish_sent.1), channel_id=1, source_target_pairs={{0,1},{1,0},{2,3},{3,2},{4,5},{5,4},{6,7},{7,6},{8,9},{9,8},{10,11... | collective-permute-start | bytes 786440 | tf_op jit(solution)/shard_map/ppermute | solution.py:566

commit v9 on v7

--- a/solution.py
+++ b/solution.py
@@ -299,7 +299,7 @@
 
 def finish_kernel(
     ids, query_ref, local_ref, prefix_ref, past_ref, sum_ref, taps_ref, res_ref, rate_ref, skip_ref,
-    out_ref, begins, carry,
+    out_ref, all_begins, all_carry,
 ):
     part = ids[0]
     modes, width = prefix_ref.shape
@@ -307,8 +307,9 @@
     run = half // SUB
     row = lax.broadcasted_iota(jnp.int32, (STEP, LANES), 0)
 
-    def tile(t, _):
-        cols = pl.ds(pl.multiple_of(t * LANES, LANES), LANES)
+    for t in range(width // LANES):
+        begins, carry = all_begins.at[t], all_carry.at[t]
+        cols = slice(t * LANES, (t + 1) * LANES)
         rates = rate_ref[:, cols]
         gains = res_ref[:, cols] * jnp.sqrt(2.0 * rates)
         keep_all = jnp.exp(-rates)
@@ -336,7 +337,7 @@
         skip = skip_ref[:, cols]
         over = jnp.sum(gains * grow, axis=0, keepdims=True)
         for r in range(0, half, STEP):
-            rows = pl.ds(pl.multiple_of(t * half + r, STEP), STEP)
+            rows = slice(t * half + r, t * half + r + STEP)
             value = query_ref[rows, :] * (local_ref[rows, :] + carry[r : r + STEP, :])
             if r == 0:
                 begin = carry[0:SUB, :]
@@ -345,9 +346,6 @@
                 value = jnp.where((row == 0) & (part == 0), head, value)
                 value = jnp.where((row == 1) & (part == 0), second, value)
             out_ref[r : r + STEP, cols] = value.astype(BF16)
-        return 0
-
-    lax.fori_loop(0, width // LANES, tile, 0, unroll=UNROLL)
 
 
 def place_kernel(ids, far_ref, held_ref, out_ref, sem):
@@ -535,8 +533,8 @@
                 ],
                 out_specs=pl.BlockSpec((half, tile), lambda i, ids: (0, ids[1] * steps + i)),
                 scratch_shapes=[
-                    pltpu.VMEM((modes * SUB, LANES), F32),
-                    pltpu.VMEM((half, LANES), F32),
+                    pltpu.VMEM((tiles, modes * SUB, LANES), F32),
+                    pltpu.VMEM((tiles, half, LANES), F32),
                 ],
             ),
             out_shape=jax.ShapeDtypeStruct((half, columns), BF16),
@@ -559,7 +557,10 @@
         in_specs=[pl.BlockSpec(memory_space=pltpu.SMEM)] + [in_vmem] * 9,
         out_specs=in_vmem,
         out_shape=jax.ShapeDtypeStruct((half, width), BF16),
-        scratch_shapes=[pltpu.VMEM((modes * SUB, LANES), F32), pltpu.VMEM((half, LANES), F32)],
+        scratch_shapes=[
+            pltpu.VMEM((all_tiles, modes * SUB, LANES), F32),
+            pltpu.VMEM((all_tiles, half, LANES), F32),
+        ],
         compiler_params=params,
         name="finish_sent",
     )(1 - side, *locals_sent, prefix, past, own, short_filter, weights, rates, skip)

time: 49.3 us -> 49.4 us (level)
  no operation moved by 1% of the time
where the time goes in v9:
time: 49.4 us; the launch traced here: 49.2 us
  waiting for transfers between devices  19.6 us (40%)
  starting transfers between devices  16.1 us (33%)
  Pallas kernels  13.2 us (27%)
    ppermute x7, waiting for transfers between devices, send(): return lax.ppermute(value, 'ctx', route(hop))  11.9 us
    ppermute x7, starting transfers between devices, send(): return lax.ppermute(value, 'ctx', route(hop))  10.6 us
    ppermute x1, waiting for transfers between devices, shards(): far = lax.ppermute(sent, 'chan', [(0, 1), (1, 0)])  7.68 us
    ppermute x1, starting transfers between devices, shards(): far = lax.ppermute(sent, 'chan', [(0, 1), (1, 0)])  5.53 us
    pallas_call x3, Pallas kernels, local(): pl.pallas_call(functools.partial(local_kernel, first * tile), in_specs=[p...  4.23 us
    pallas_call x1, Pallas kernels, shards(): pl.pallas_call(state_kernel, grid=(wide_steps,), in_specs=[in_hbm] * 3, o...  3.52 us
    pallas_call x1, Pallas kernels, finish(): pl.pallas_call(finish_kernel, grid_spec=pltpu.PrefetchScalarGridSpec(num_...  2.57 us
    pallas_call x4, Pallas kernels, shards(): pl.pallas_call(body, in_specs=[pl.BlockSpec(memory_space=pltpu.SMEM)] + [...  1.31 us
  transfers between devices with their start and end apart: 11, of which 8 were waited for; matrix products, arithmetic and copies ran while one was open for 0% of the time, Pallas kernels for 14%

profile of v9, /device:TPU:96, one launch (start us, length us, event | category | flops | bytes accessed | tf_op | source)
XLA Modules:
  0.0 49.2 jit_solution(1762487172139585315)
XLA Ops:
  0.0 0.0 copy-start
  0.0 0.0 copy-start.1
  0.0 0.0 copy-start.2
  0.0 0.0 copy-start.3
  0.0 3.5 %states.1 = (f32[2048,128]{1,0:T(8,128)S(1)}, f32[8,2,128,128]{3,2,1,0:T(8,128)S(1)}, f32[16,1024]{1,0:T(8,128)S(1)}, bf16[32,1024]{1,0:T(8,128)(2,1)S(1)}) custom-call(bf16[3,256,1024]{2,1,0:T(8,128)(2,1)} %bitcast.26, f32[3,3,1024]{2,1,0:T(4,128)} %taps_ref.9, f32[16,1024]{1,0:T(8,128)} %bitcast.6), custom_call_target="tpu_custom_call" | custom-call | tf_op jit(solution)/shard_map/states/pallas_call | solution.py:421
  3.5 0.1 collective-permute-start
  3.7 1.2 %collective-permute-done.refs_6_ = bf16[32,1024]{1,0:T(8,128)(2,1)S(1)} collective-permute-done((bf16[32,1024]{1,0:T(8,128)(2,1)S(1)}, bf16[32,1024]{1,0:T(8,128)(2,1)S(1)}, u32[]{:S(2)}, u32[]{:S(2)}) %collective-permute-start) | collective-permute-done | bytes 65568 | tf_op jit(solution)/shard_map/ppermute | solution.py:372
  4.9 0.0 copy-done
  4.9 0.0 copy-done.1
  4.9 0.2 join_0.1
  5.1 1.0 %collective-permute-start.1 = (bf16[32,1024]{1,0:T(8,128)(2,1)S(1)}, bf16[32,1024]{1,0:T(8,128)(2,1)S(1)}, u32[]{:S(2)}, u32[]{:S(2)}) collective-permute-start(bf16[32,1024]{1,0:T(8,128)(2,1)S(1)} %get-tuple-element.51.refs_5_), channel_id=1, source_target_pairs={{0,4},{2,14},{4,8},{6,2},{8,12},{10,6},{12,0},{14,10},{16,20},{18,... | collective-permute-start | bytes 196616 | tf_op jit(solution)/shard_map/ppermute | solution.py:372
  6.1 0.7 %collective-permute-start.2 = (bf16[32,1024]{1,0:T(8,128)(2,1)S(1)}, bf16[32,1024]{1,0:T(8,128)(2,1)S(1)}, u32[]{:S(2)}, u32[]{:S(2)}) collective-permute-start(bf16[32,1024]{1,0:T(8,128)(2,1)S(1)} %get-tuple-element.51.refs_5_), channel_id=1, source_target_pairs={{0,8},{2,10},{4,12},{6,14},{8,0},{10,2},{12,4},{14,6},{16,24},{18,... | collective-permute-start | bytes 196616 | tf_op jit(solution)/shard_map/ppermute | solution.py:372
  6.7 4.1 %collective-permute-done.1.refs_6_ = bf16[32,1024]{1,0:T(8,128)(2,1)S(1)} collective-permute-done((bf16[32,1024]{1,0:T(8,128)(2,1)S(1)}, bf16[32,1024]{1,0:T(8,128)(2,1)S(1)}, u32[]{:S(2)}, u32[]{:S(2)}) %collective-permute-start.1) | collective-permute-done | bytes 65568 | tf_op jit(solution)/shard_map/ppermute | solution.py:372
  10.9 0.0 collective-permute-start.3
  10.9 1.7 %collective-permute-done.2.refs_7_ = bf16[32,1024]{1,0:T(8,128)(2,1)S(1)} collective-permute-done((bf16[32,1024]{1,0:T(8,128)(2,1)S(1)}, bf16[32,1024]{1,0:T(8,128)(2,1)S(1)}, u32[]{:S(2)}, u32[]{:S(2)}) %collective-permute-start.2) | collective-permute-done | bytes 65568 | tf_op jit(solution)/shard_map/ppermute | solution.py:372
  12.5 0.0 collective-permute-done.3.refs_8_
  12.5 0.4 join_1.1
  12.9 1.6 %collective-permute-start.4 = (bf16[32,1024]{1,0:T(8,128)(2,1)S(1)}, bf16[32,1024]{1,0:T(8,128)(2,1)S(1)}, u32[]{:S(2)}, u32[]{:S(2)}) collective-permute-start(bf16[32,1024]{1,0:T(8,128)(2,1)S(1)} %get-tuple-element.52.refs_5_), channel_id=1, source_target_pairs={{0,16},{2,50},{4,20},{6,54},{8,24},{10,58},{12,28},{14,62},{16,32}... | collective-permute-start | bytes 196616 | tf_op jit(solution)/shard_map/ppermute | solution.py:372
  14.5 2.7 %collective-permute-start.5 = (bf16[32,1024]{1,0:T(8,128)(2,1)S(1)}, bf16[32,1024]{1,0:T(8,128)(2,1)S(1)}, u32[]{:S(2)}, u32[]{:S(2)}) collective-permute-start(bf16[32,1024]{1,0:T(8,128)(2,1)S(1)} %get-tuple-element.52.refs_5_), channel_id=1, source_target_pairs={{0,32},{2,34},{4,36},{6,38},{8,40},{10,42},{12,44},{14,46},{16,48}... | collective-permute-start | bytes 196616 | tf_op jit(solution)/shard_map/ppermute | solution.py:372
  17.2 1.3 %collective-permute-done.4.refs_6_ = bf16[32,1024]{1,0:T(8,128)(2,1)S(1)} collective-permute-done((bf16[32,1024]{1,0:T(8,128)(2,1)S(1)}, bf16[32,1024]{1,0:T(8,128)(2,1)S(1)}, u32[]{:S(2)}, u32[]{:S(2)}) %collective-permute-start.4) | collective-permute-done | bytes 65568 | tf_op jit(solution)/shard_map/ppermute | solution.py:372
  18.5 0.0 collective-permute-start.6
  18.5 0.0 copy-done.2
  18.5 0.0 copy-done.3
  18.5 1.1 %local_sent_2.1 = (f32[1024,128]{1,0:T(8,128)S(1)}, f32[1024,128]{1,0:T(8,128)S(1)}) custom-call(s32[1]{0:T(128)S(6)} %sub.2.part_id.ids, bf16[3,256,1024]{2,1,0:T(8,128)(2,1)} %bitcast.27, f32[3,3,1024]{2,1,0:T(4,128)S(1)} %copy-done.1, f32[2048,128]{1,0:T(8,128)S(1)} %get-tuple-element.81.gate_ref, f32[8,2,128,128]{3,2,1,0:T(8,128)S(1)} %get-tuple-element.57.ends_ref, ...), custom_call_target="tpu_custom_call" | custom-call | tf_op jit(solution)/shard_map/local_sent_2/pallas_call | solution.py:458
  19.6 1.2 %collective-permute-done.5.refs_7_ = bf16[32,1024]{1,0:T(8,128)(2,1)S(1)} collective-permute-done((bf16[32,1024]{1,0:T(8,128)(2,1)S(1)}, bf16[32,1024]{1,0:T(8,128)(2,1)S(1)}, u32[]{:S(2)}, u32[]{:S(2)}) %collective-permute-start.5) | collective-permute-done | bytes 65568 | tf_op jit(solution)/shard_map/ppermute | solution.py:372
  20.9 0.0 collective-permute-done.6.refs_8_
  20.9 0.4 join_2.1
  21.3 1.7 %collective-permute-start.7 = (bf16[32,1024]{1,0:T(8,128)(2,1)S(1)}, bf16[32,1024]{1,0:T(8,128)(2,1)S(1)}, u32[]{:S(2)}, u32[]{:S(2)}) collective-permute-start(bf16[32,1024]{1,0:T(8,128)(2,1)S(1)} %get-tuple-element.64.refs_5_), channel_id=1, source_target_pairs={{0,64},{2,194},{4,68},{6,198},{8,72},{10,202},{12,76},{14,206},{16... | collective-permute-start | bytes 196616 | tf_op jit(solution)/shard_map/ppermute | solution.py:372
  23.0 2.9 %collective-permute-start.8 = (bf16[32,1024]{1,0:T(8,128)(2,1)S(1)}, bf16[32,1024]{1,0:T(8,128)(2,1)S(1)}, u32[]{:S(2)}, u32[]{:S(2)}) collective-permute-start(bf16[32,1024]{1,0:T(8,128)(2,1)S(1)} %get-tuple-element.64.refs_5_), channel_id=1, source_target_pairs={{0,128},{2,130},{4,132},{6,134},{8,136},{10,138},{12,140},{14,142}... | collective-permute-start | bytes 196616 | tf_op jit(solution)/shard_map/ppermute | solution.py:372
  25.9 1.0 %collective-permute-done.7.refs_6_ = bf16[32,1024]{1,0:T(8,128)(2,1)S(1)} collective-permute-done((bf16[32,1024]{1,0:T(8,128)(2,1)S(1)}, bf16[32,1024]{1,0:T(8,128)(2,1)S(1)}, u32[]{:S(2)}, u32[]{:S(2)}) %collective-permute-start.7) | collective-permute-done | bytes 65568 | tf_op jit(solution)/shard_map/ppermute | solution.py:372
  26.9 0.0 collective-permute-start.9
  26.9 1.1 %local_sent_3.1 = (f32[1024,128]{1,0:T(8,128)S(1)}, f32[1024,128]{1,0:T(8,128)S(1)}) custom-call(s32[1]{0:T(128)S(6)} %sub.2.part_id.ids, bf16[3,256,1024]{2,1,0:T(8,128)(2,1)} %bitcast.28, f32[3,3,1024]{2,1,0:T(4,128)S(1)} %copy-done.1, f32[2048,128]{1,0:T(8,128)S(1)} %get-tuple-element.81.gate_ref, ...), custom_call_target="tpu_custom_call", output_to_operand_aliasing={{0}: (8, {}), {1}: (9, {})} | custom-call | tf_op jit(solution)/shard_map/local_sent_3/pallas_call | solution.py:458
  28.0 1.4 %collective-permute-done.8.refs_7_ = bf16[32,1024]{1,0:T(8,128)(2,1)S(1)} collective-permute-done((bf16[32,1024]{1,0:T(8,128)(2,1)S(1)}, bf16[32,1024]{1,0:T(8,128)(2,1)S(1)}, u32[]{:S(2)}, u32[]{:S(2)}) %collective-permute-start.8) | collective-permute-done | bytes 65568 | tf_op jit(solution)/shard_map/ppermute | solution.py:372
  29.4 0.0 collective-permute-done.9.refs_8_
  29.4 0.3 join_3.1
  29.7 0.9 %finish_sent.1 = bf16[128,1024]{1,0:T(8,128)(2,1)S(1)} custom-call(s32[1]{0:T(128)S(6)} %sub.2.part_id.ids, f32[1024,128]{1,0:T(8,128)S(1)} %get-tuple-element.71.query_ref, f32[1024,128]{1,0:T(8,128)S(1)} %get-tuple-element.72.local_ref, f32[16,1024]{1,0:T(8,128)S(1)} %get-tuple-element.84.prefix_ref, f32[8,1024]{1,0:T(8,128)S(1)} %get-tuple-element.80.past_ref, ...), custom_call_target="tpu_custom_call" | custom-call | tf_op jit(solution)/shard_map/finish_sent/pallas_call | solution.py:555
  30.6 5.5 %collective-permute-start.10 = (bf16[128,1024]{1,0:T(8,128)(2,1)S(1)}, bf16[128,1024]{1,0:T(8,128)(2,1)S(1)}, u32[]{:S(2)}, u32[]{:S(2)}) collective-permute-start(bf16[128,1024]{1,0:T(8,128)(2,1)S(1)} %finish_sent.1), channel_id=1, source_target_pairs={{0,1},{1,0},{2,3},{3,2},{4,5},{5,4},{6,7},{7,6},{8,9},{9,8},{10,11... | collective-permute-start | bytes 786440 | tf_op jit(solution)/shard_map/ppermute | solution.py:567
  36.2 0.1 pad_add_fusion.ids
  36.2 2.0 %local_own.1 = (f32[1024,128]{1,0:T(8,128)S(1)}, f32[1024,128]{1,0:T(8,128)S(1)}) custom-call(s32[1]{0:T(128)} %bitcast.part_id, bf16[3,256,1024]{2,1,0:T(8,128)(2,1)} %bitcast.29, f32[3,3,1024]{2,1,0:T(4,128)S(1)} %copy-done.1, f32[2048,128]{1,0:T(8,128)S(1)} %get-tuple-element.81.gate_ref, f32[8,2,128,128]{3,2,1,0:T(8,128)S(1)} %get-tuple-element.57.ends_ref, ...), custom_call_target="tpu_custom_call" | custom-call | tf_op jit(solution)/shard_map/local_own/pallas_call | solution.py:458
  38.2 2.6 %finish_own.1.held_ref = bf16[128,2048]{1,0:T(8,128)(2,1)} custom-call(s32[2]{0:T(128)S(1)} %pad_add_fusion.ids, f32[1024,128]{1,0:T(8,128)S(1)} %get-tuple-element.82.query_ref, f32[1024,128]{1,0:T(8,128)S(1)} %get-tuple-element.83.local_ref, f32[16,1024]{1,0:T(8,128)S(1)} %get-tuple-element.84.prefix_ref, f32[8,1024]{1,0:T(8,128)S(1)} %get-tuple-element.80.past_ref, ...), custom_call_target="tpu_custom_call" | custom-call | tf_op jit(solution)/shard_map/finish_own/pallas_call | solution.py:518
  40.8 7.7 %collective-permute-done.10.far_ref = bf16[128,1024]{1,0:T(8,128)(2,1)S(1)} collective-permute-done((bf16[128,1024]{1,0:T(8,128)(2,1)S(1)}, bf16[128,1024]{1,0:T(8,128)(2,1)S(1)}, u32[]{:S(2)}, u32[]{:S(2)}) %collective-permute-start.10) | collective-permute-done | bytes 262176 | tf_op jit(solution)/shard_map/ppermute | solution.py:567
  48.5 0.7 %place.1 = bf16[128,2048]{1,0:T(8,128)(2,1)} custom-call(s32[1]{0:T(128)S(6)} %sub.2.part_id.ids, bf16[128,1024]{1,0:T(8,128)(2,1)S(1)} %collective-permute-done.10.far_ref, bf16[128,2048]{1,0:T(8,128)(2,1)} %finish_own.1.held_ref), custom_call_target="tpu_custom_call", output_to_operand_aliasing={{}: (2, {})} | custom-call | tf_op jit(solution)/shard_map/place/pallas_call | solution.py:571
  (2 shorter events, 0.0 us)
Async XLA Ops:
  0.0 4.9 %copy-start = (f32[1024,16]{0,1:T(8,128)S(1)}, f32[1024,16]{0,1:T(8,128)}, u32[]{:S(2)}) copy-start(f32[1024,16]{0,1:T(8,128)} %param.8) | copy-start | bytes 196612
  0.0 4.9 %copy-start.1 = (f32[3,3,1024]{2,1,0:T(4,128)S(1)}, f32[3,3,1024]{2,1,0:T(4,128)}, u32[]{:S(2)}) copy-start(f32[3,3,1024]{2,1,0:T(4,128)} %taps_ref.9) | copy-start | bytes 110596
  0.0 18.5 %copy-start.2 = (f32[1024,16]{0,1:T(8,128)S(1)}, f32[1024,16]{0,1:T(8,128)}, u32[]{:S(2)}) copy-start(f32[1024,16]{0,1:T(8,128)} %param.7) | copy-start | bytes 196612
  0.0 18.5 %copy-start.3 = (f32[1024]{0:T(1024)S(1)}, f32[1024]{0:T(1024)}, u32[]{:S(2)}) copy-start(f32[1024]{0:T(1024)} %param.9) | copy-start | bytes 12292
  3.5 1.3 %collective-permute-start = (bf16[32,1024]{1,0:T(8,128)(2,1)S(1)}, bf16[32,1024]{1,0:T(8,128)(2,1)S(1)}, u32[]{:S(2)}, u32[]{:S(2)}) collective-permute-start(bf16[32,1024]{1,0:T(8,128)(2,1)S(1)} %get-tuple-element.47.refs_5_.sum_ref), channel_id=1, source_target_pairs={{0,2},{2,0},{4,6},{6,4},{8,10},{10,8},{12,14},{14,12},{16,18},{18,... | collective-permute-start | bytes 196616 | tf_op jit(solution)/shard_map/ppermute | solution.py:372
  5.1 5.8 %collective-permute-start.1 = (bf16[32,1024]{1,0:T(8,128)(2,1)S(1)}, bf16[32,1024]{1,0:T(8,128)(2,1)S(1)}, u32[]{:S(2)}, u32[]{:S(2)}) collective-permute-start(bf16[32,1024]{1,0:T(8,128)(2,1)S(1)} %get-tuple-element.51.refs_5_), channel_id=1, source_target_pairs={{0,4},{2,14},{4,8},{6,2},{8,12},{10,6},{12,0},{14,10},{16,20},{18,... | collective-permute-start | bytes 196616 | tf_op jit(solution)/shard_map/ppermute | solution.py:372
  6.1 6.4 %collective-permute-start.2 = (bf16[32,1024]{1,0:T(8,128)(2,1)S(1)}, bf16[32,1024]{1,0:T(8,128)(2,1)S(1)}, u32[]{:S(2)}, u32[]{:S(2)}) collective-permute-start(bf16[32,1024]{1,0:T(8,128)(2,1)S(1)} %get-tuple-element.51.refs_5_), channel_id=1, source_target_pairs={{0,8},{2,10},{4,12},{6,14},{8,0},{10,2},{12,4},{14,6},{16,24},{18,... | collective-permute-start | bytes 196616 | tf_op jit(solution)/shard_map/ppermute | solution.py:372
  10.9 1.7 %collective-permute-start.3 = (bf16[32,1024]{1,0:T(8,128)(2,1)S(1)}, bf16[32,1024]{1,0:T(8,128)(2,1)S(1)}, u32[]{:S(2)}, u32[]{:S(2)}) collective-permute-start(bf16[32,1024]{1,0:T(8,128)(2,1)S(1)} %collective-permute-done.1.refs_6_), channel_id=1, source_target_pairs={{0,2},{2,0},{4,6},{6,4},{8,10},{10,8},{12,14},{14,12},{16,18},{18,... | collective-permute-start | bytes 196616 | tf_op jit(solution)/shard_map/ppermute | solution.py:378
  12.9 5.6 %collective-permute-start.4 = (bf16[32,1024]{1,0:T(8,128)(2,1)S(1)}, bf16[32,1024]{1,0:T(8,128)(2,1)S(1)}, u32[]{:S(2)}, u32[]{:S(2)}) collective-permute-start(bf16[32,1024]{1,0:T(8,128)(2,1)S(1)} %get-tuple-element.52.refs_5_), channel_id=1, source_target_pairs={{0,16},{2,50},{4,20},{6,54},{8,24},{10,58},{12,28},{14,62},{16,32}... | collective-permute-start | bytes 196616 | tf_op jit(solution)/shard_map/ppermute | solution.py:372
  14.5 6.4 %collective-permute-start.5 = (bf16[32,1024]{1,0:T(8,128)(2,1)S(1)}, bf16[32,1024]{1,0:T(8,128)(2,1)S(1)}, u32[]{:S(2)}, u32[]{:S(2)}) collective-permute-start(bf16[32,1024]{1,0:T(8,128)(2,1)S(1)} %get-tuple-element.52.refs_5_), channel_id=1, source_target_pairs={{0,32},{2,34},{4,36},{6,38},{8,40},{10,42},{12,44},{14,46},{16,48}... | collective-permute-start | bytes 196616 | tf_op jit(solution)/shard_map/ppermute | solution.py:372
  18.5 2.4 %collective-permute-start.6 = (bf16[32,1024]{1,0:T(8,128)(2,1)S(1)}, bf16[32,1024]{1,0:T(8,128)(2,1)S(1)}, u32[]{:S(2)}, u32[]{:S(2)}) collective-permute-start(bf16[32,1024]{1,0:T(8,128)(2,1)S(1)} %collective-permute-done.4.refs_6_), channel_id=1, source_target_pairs={{0,2},{2,0},{4,6},{6,4},{8,10},{10,8},{12,14},{14,12},{16,18},{18,... | collective-permute-start | bytes 196616 | tf_op jit(solution)/shard_map/ppermute | solution.py:378
  21.3 5.6 %collective-permute-start.7 = (bf16[32,1024]{1,0:T(8,128)(2,1)S(1)}, bf16[32,1024]{1,0:T(8,128)(2,1)S(1)}, u32[]{:S(2)}, u32[]{:S(2)}) collective-permute-start(bf16[32,1024]{1,0:T(8,128)(2,1)S(1)} %get-tuple-element.64.refs_5_), channel_id=1, source_target_pairs={{0,64},{2,194},{4,68},{6,198},{8,72},{10,202},{12,76},{14,206},{16... | collective-permute-start | bytes 196616 | tf_op jit(solution)/shard_map/ppermute | solution.py:372
  23.0 6.5 %collective-permute-start.8 = (bf16[32,1024]{1,0:T(8,128)(2,1)S(1)}, bf16[32,1024]{1,0:T(8,128)(2,1)S(1)}, u32[]{:S(2)}, u32[]{:S(2)}) collective-permute-start(bf16[32,1024]{1,0:T(8,128)(2,1)S(1)} %get-tuple-element.64.refs_5_), channel_id=1, source_target_pairs={{0,128},{2,130},{4,132},{6,134},{8,136},{10,138},{12,140},{14,142}... | collective-permute-start | bytes 196616 | tf_op jit(solution)/shard_map/ppermute | solution.py:372
  26.9 2.6 %collective-permute-start.9 = (bf16[32,1024]{1,0:T(8,128)(2,1)S(1)}, bf16[32,1024]{1,0:T(8,128)(2,1)S(1)}, u32[]{:S(2)}, u32[]{:S(2)}) collective-permute-start(bf16[32,1024]{1,0:T(8,128)(2,1)S(1)} %collective-permute-done.7.refs_6_), channel_id=1, source_target_pairs={{0,2},{2,0},{4,6},{6,4},{8,10},{10,8},{12,14},{14,12},{16,18},{18,... | collective-permute-start | bytes 196616 | tf_op jit(solution)/shard_map/ppermute | solution.py:378
  30.6 17.9 %collective-permute-start.10 = (bf16[128,1024]{1,0:T(8,128)(2,1)S(1)}, bf16[128,1024]{1,0:T(8,128)(2,1)S(1)}, u32[]{:S(2)}, u32[]{:S(2)}) collective-permute-start(bf16[128,1024]{1,0:T(8,128)(2,1)S(1)} %finish_sent.1), channel_id=1, source_target_pairs={{0,1},{1,0},{2,3},{3,2},{4,5},{5,4},{6,7},{7,6},{8,9},{9,8},{10,11... | collective-permute-start | bytes 786440 | tf_op jit(solution)/shard_map/ppermute | solution.py:567
